TPU v7x, 32 devices: a whole 2x2x4 slice. The times are simulated.
32 devices in a mesh: dp: 4 (over y, x), expert: 8 (over z, core).
Axes of the slice: x: 2, y: 2, z: 4, core: 2. Of those that a mesh axis runs over, the one named last changes fastest.
Arguments:
- tokens: bfloat16 [4096, 2048], P(('dp', 'expert')), may hold values from -6 to 6
- segments: int32 [4, 1024], P('dp'), may hold values from 0 to 7, never falling along the last dimension, each value on 1 to 512 neighbouring positions
- routes: int32 [4096, 8], P(('dp', 'expert')), may hold values from 0 to 15, all different within a row; in each aligned block of 128 rows (0 to 127, 128 to 255, ...) at most 128 rows name the same one
- cotangent: bfloat16 [4096, 2048], P(('dp', 'expert')), may hold values from -6 to 6
- norm_gain_attn: float32 [2048], replicated, may hold values from 0.1 to 1.9
- query_weight: bfloat16 [2048, 4096], P('expert'), may hold values from -0.125 to 0.125
- key_matrix: bfloat16 [2048, 512], P('expert'), may hold values from -0.125 to 0.125
- value_matrix: bfloat16 [2048, 512], P('expert'), may hold values from -0.125 to 0.125
- query_gain: float32 [128], replicated, may hold values from 0.1 to 1.9
- key_gain: float32 [128], replicated, may hold values from 0.1 to 1.9
- out_weight: bfloat16 [4096, 2048], P('expert'), may hold values from -0.375 to 0.375
- norm_gain_ffn: float32 [2048], replicated, may hold values from 0.1 to 1.9
- router_weight: bfloat16 [2048, 16], replicated, may hold values from -0.0625 to 0.0625
- gate_weight: bfloat16 [16, 2048, 768], P('expert'), may hold values from -0.125 to 0.125
- up_weight: bfloat16 [16, 2048, 768], P('expert'), may hold values from -0.125 to 0.125
- down_weight: bfloat16 [16, 768, 2048], P('expert'), may hold values from -0.625 to 0.625
Outputs:
- output: bfloat16 [4096, 2048], P(('dp', 'expert'))
- input_grad: float32 [4096, 2048], P(('dp', 'expert'))
- grad_norm_attn: float32 [2048], replicated
- grad_query: float32 [2048, 4096], P('expert')
- grad_key: float32 [2048, 512], P('expert')
- grad_value: float32 [2048, 512], P('expert')
- grad_query_gain: float32 [128], replicated
- grad_key_gain: float32 [128], replicated
- grad_out: float32 [4096, 2048], P('expert')
- grad_norm_ffn: float32 [2048], replicated
- grad_router: float32 [2048, 16], replicated
- grad_gate: float32 [16, 2048, 768], P('expert', None, 'dp')
- grad_up: float32 [16, 2048, 768], P('expert', None, 'dp')
- grad_down: float32 [16, 768, 2048], P('expert', None, 'dp')
Inputs may be any that keep to these rules, and one draw needn't show every extreme that they name: Within the rows of one device no expert is named by more than 128 routes, a bound that some block reaches of them. `segments`: within a sequence document numbers never fall; a document has at most 512 positions, and some has exactly that many.
All inputs are finite; a program needn't handle non-finite values.
Results may differ from a plain program's by a relative error of at most 0.024.
Values may be sent and summed in bfloat16 or wider, within the bound.
A program may use at most 320 MiB of HBM per device.

v0:
```python
import jax
import jax.numpy as jnp
from jax import lax
from jax.sharding import PartitionSpec as P

eps_norm = 1e-06
rope_base = 1000000.0


def norm_rows(values, gain):
    factor = lax.rsqrt(jnp.mean(values * values, axis=-1, keepdims=True) + eps_norm)
    return values * factor * gain


def rotary_at(positions, head_size):
    half = head_size // 2
    freqs = rope_base ** (-jnp.arange(half, dtype=jnp.float32) * 2.0 / head_size)
    angles = positions.astype(jnp.float32)[:, None] * freqs[None, :]
    return (jnp.cos(angles)[:, None, :], jnp.sin(angles)[:, None, :])


def prepare_heads(raw, gain, cosines, sines):
    normed = norm_rows(raw, gain)
    half = raw.shape[-1] // 2
    first = normed[..., :half]
    second = normed[..., half:]
    return jnp.concatenate(
        [first * cosines - second * sines, second * cosines + first * sines], axis=-1
    )


def contract_first(left, right):
    return lax.dot_general(
        left, right, (((0,), (0,)), ((), ())), preferred_element_type=jnp.float32
    )


def contract_last(left, right):
    return lax.dot_general(
        left, right, (((1,), (1,)), ((), ())), preferred_element_type=jnp.float32
    )


def swiglu(gate_pre, up_pre):
    return jax.nn.silu(gate_pre) * up_pre


def expert_front(slot_rows, gate_weight, up_weight):
    gate_pre = jnp.einsum(
        "sxcd,xdf->sxcf", slot_rows, gate_weight, preferred_element_type=jnp.float32
    )
    up_pre = jnp.einsum("sxcd,xdf->sxcf", slot_rows, up_weight, preferred_element_type=jnp.float32)
    act_value, act_back = jax.vjp(swiglu, gate_pre, up_pre)
    return (act_value.astype(jnp.bfloat16), act_back)


def on_device(
    tokens,
    segments,
    routes,
    cotangent,
    norm_gain_attn,
    query_weight,
    key_matrix,
    value_matrix,
    query_gain,
    key_gain,
    out_weight,
    norm_gain_ffn,
    router_weight,
    gate_weight,
    up_weight,
    down_weight,
):
    length, model_width = tokens.shape
    head_size = query_gain.shape[0]
    peer_count = lax.axis_size("expert")
    kv_heads = key_matrix.shape[1] // head_size
    kv_width = kv_heads * head_size
    query_heads = out_weight.shape[0] * peer_count // head_size
    groups = query_heads // kv_heads
    local_experts = gate_weight.shape[0]
    experts = local_experts * peer_count
    route_count = routes.shape[1]
    capacity = 2 * length * route_count // experts
    score_scale = head_size ** (-0.5)
    slot_shape = (peer_count, local_experts * capacity, model_width)
    grid_shape = (peer_count, local_experts, capacity, model_width)
    full_query, full_key, full_value, full_out = (
        lax.all_gather(query_weight, "expert", axis=0, tiled=True),
        lax.all_gather(key_matrix, "expert", axis=0, tiled=True),
        lax.all_gather(value_matrix, "expert", axis=0, tiled=True),
        lax.all_gather(out_weight, "expert", axis=0, tiled=True),
    )
    inputs = tokens.astype(jnp.float32)
    normed_attn, norm_attn_back = jax.vjp(norm_rows, inputs, norm_gain_attn)
    attention_hidden = normed_attn.astype(jnp.bfloat16)
    query_raw = jnp.dot(attention_hidden, full_query, preferred_element_type=jnp.float32).reshape(
        length, query_heads, head_size
    )
    unrotated_key = jnp.dot(attention_hidden, full_key, preferred_element_type=jnp.float32).reshape(
        length, kv_heads, head_size
    )
    value_local = jnp.dot(attention_hidden, full_value, preferred_element_type=jnp.float32).astype(
        jnp.bfloat16
    )
    segment_row = segments[0]
    full_length = segment_row.shape[0]
    offset = lax.axis_index("expert") * length
    query_positions = offset + jnp.arange(length, dtype=jnp.int32)
    query_segments = lax.dynamic_slice_in_dim(segment_row, offset, length)
    cosines, sines = rotary_at(query_positions, head_size)

    def head_prep(raw, gain):
        return prepare_heads(raw, gain, cosines, sines)

    query_rot, query_back = jax.vjp(head_prep, query_raw, query_gain)
    key_rot, key_back = jax.vjp(head_prep, unrotated_key, key_gain)
    query_low = query_rot.astype(jnp.bfloat16)
    key_local = key_rot.astype(jnp.bfloat16).reshape(length, kv_width)
    grouped_rows = query_low.reshape(length, kv_heads, groups, head_size)
    keys_all, values_all = (
        lax.all_gather(key_local, "expert", axis=0, tiled=True),
        lax.all_gather(value_local, "expert", axis=0, tiled=True),
    )
    key_block = min(512, full_length)
    block_count = full_length // key_block
    key_blocks = keys_all.reshape(block_count, key_block, kv_heads, head_size)
    value_blocks = values_all.reshape(block_count, key_block, kv_heads, head_size)
    segment_blocks = segment_row.reshape(block_count, key_block)
    position_blocks = jnp.arange(full_length, dtype=jnp.int32).reshape(block_count, key_block)
    block_inputs = (key_blocks, value_blocks, segment_blocks, position_blocks)

    def block_scores(key_blk, segment_blk, position_blk):
        scores = (
            jnp.einsum("tkgd,skd->kgts", grouped_rows, key_blk, preferred_element_type=jnp.float32)
            * score_scale
        )
        allowed = (query_positions[:, None] >= position_blk[None, :]) & (
            query_segments[:, None] == segment_blk[None, :]
        )
        return (scores, allowed)

    def running_total(carry, pieces):
        top, total = carry
        key_blk, value_blk, segment_blk, position_blk = pieces
        scores, allowed = block_scores(key_blk, segment_blk, position_blk)
        new_top = jnp.maximum(top, jnp.max(jnp.where(allowed, scores, -1e30), axis=-1))
        terms = jnp.where(allowed, jnp.exp(scores - new_top[..., None]), 0.0)
        total = total * jnp.exp(top - new_top) + jnp.sum(terms, axis=-1)
        return ((new_top, total), None)

    stat_shape = (kv_heads, groups, length)
    (top, total), unused = lax.scan(
        running_total,
        (jnp.full(stat_shape, -1e30, jnp.float32), jnp.zeros(stat_shape, jnp.float32)),
        block_inputs,
    )
    log_total = top + jnp.log(total)

    def weighted_values(carry, pieces):
        rounded_sum, exact_sum = carry
        key_blk, value_blk, segment_blk, position_blk = pieces
        scores, allowed = block_scores(key_blk, segment_blk, position_blk)
        probs = jnp.where(allowed, jnp.exp(scores - log_total[..., None]), 0.0)
        rounded_sum = rounded_sum + jnp.einsum(
            "kgts,skd->tkgd",
            probs.astype(jnp.bfloat16),
            value_blk,
            preferred_element_type=jnp.float32,
        )
        exact_sum = exact_sum + jnp.einsum("kgts,skd->tkgd", probs, value_blk.astype(jnp.float32))
        return ((rounded_sum, exact_sum), None)

    head_shape = (length, kv_heads, groups, head_size)
    (mixed_sum, exact_mixed), unused = lax.scan(
        weighted_values,
        (jnp.zeros(head_shape, jnp.float32), jnp.zeros(head_shape, jnp.float32)),
        block_inputs,
    )
    mixed = mixed_sum.reshape(length, query_heads * head_size).astype(jnp.bfloat16)
    attn = jnp.dot(mixed, full_out, preferred_element_type=jnp.float32)
    resid = inputs + attn
    normed_ffn, norm_ffn_back = jax.vjp(norm_rows, resid, norm_gain_ffn)
    hidden_ffn = normed_ffn.astype(jnp.bfloat16)
    logits = jnp.dot(hidden_ffn, router_weight, preferred_element_type=jnp.float32)
    chosen = (routes[:, :, None] == jnp.arange(experts, dtype=jnp.int32)[None, None, :]).astype(
        jnp.float32
    )
    picked = jnp.sum(chosen * logits[:, None, :], axis=-1)
    picked_exp = jnp.exp(picked - jnp.max(picked, axis=-1, keepdims=True))
    gate_values = picked_exp / jnp.sum(picked_exp, axis=-1, keepdims=True)
    flat_routes = routes.reshape(-1)
    marks = (flat_routes[:, None] == jnp.arange(experts, dtype=jnp.int32)[None, :]).astype(
        jnp.int32
    )
    ranks = jnp.sum((jnp.cumsum(marks, axis=0) - 1) * marks, axis=1)
    slots = flat_routes * capacity + ranks
    outbox = (
        jnp.zeros((experts * capacity, model_width), jnp.bfloat16)
        .at[slots]
        .set(jnp.repeat(hidden_ffn, route_count, axis=0))
    )
    slot_rows = lax.all_to_all(
        outbox.reshape(slot_shape), "expert", split_axis=0, concat_axis=0, tiled=True
    ).reshape(grid_shape)
    act_low, act_back = expert_front(slot_rows, gate_weight, up_weight)
    expert_out = jnp.einsum(
        "sxcf,xfd->sxcd", act_low, down_weight, preferred_element_type=jnp.float32
    ).astype(jnp.bfloat16)
    returned = lax.all_to_all(
        expert_out.reshape(slot_shape), "expert", split_axis=0, concat_axis=0, tiled=True
    )
    fetched = returned.reshape(experts * capacity, model_width)[slots].reshape(
        length, route_count, model_width
    )
    mixture = jnp.sum(gate_values[:, :, None] * fetched.astype(jnp.float32), axis=1)
    output = (resid + mixture).astype(jnp.bfloat16)
    grad_final = cotangent.astype(jnp.float32)
    grad_gates = jnp.einsum("td,tjd->tj", cotangent, fetched, preferred_element_type=jnp.float32)
    grad_routed = (
        (gate_values[:, :, None] * grad_final[:, None, :])
        .astype(jnp.bfloat16)
        .reshape(length * route_count, model_width)
    )
    grad_box = jnp.zeros((experts * capacity, model_width), jnp.bfloat16).at[slots].set(grad_routed)
    grad_rows = lax.all_to_all(
        grad_box.reshape(slot_shape), "expert", split_axis=0, concat_axis=0, tiled=True
    ).reshape(grid_shape)
    grad_act = jnp.einsum(
        "sxcd,xfd->sxcf", grad_rows, down_weight, preferred_element_type=jnp.float32
    )
    grad_down_local = jnp.einsum(
        "sxcf,sxcd->xfd", act_low, grad_rows, preferred_element_type=jnp.float32
    )
    grad_gate_pre, grad_up_pre = act_back(grad_act)
    grad_gate_low = grad_gate_pre.astype(jnp.bfloat16)
    grad_up_low = grad_up_pre.astype(jnp.bfloat16)
    grad_gate_local = jnp.einsum(
        "sxcd,sxcf->xdf", slot_rows, grad_gate_low, preferred_element_type=jnp.float32
    )
    grad_up_local = jnp.einsum(
        "sxcd,sxcf->xdf", slot_rows, grad_up_low, preferred_element_type=jnp.float32
    )
    grad_slot_rows = jnp.einsum(
        "sxcf,xdf->sxcd", grad_gate_low, gate_weight, preferred_element_type=jnp.float32
    )
    grad_slot_rows = (
        grad_slot_rows
        + jnp.einsum("sxcf,xdf->sxcd", grad_up_low, up_weight, preferred_element_type=jnp.float32)
    ).astype(jnp.bfloat16)
    grad_returned = lax.all_to_all(
        grad_slot_rows.reshape(slot_shape), "expert", split_axis=0, concat_axis=0, tiled=True
    )
    grad_copies = grad_returned.reshape(experts * capacity, model_width)[slots].reshape(
        length, route_count, model_width
    )
    grad_picked = gate_values * (
        grad_gates - jnp.sum(gate_values * grad_gates, axis=-1, keepdims=True)
    )
    grad_logits = jnp.sum(chosen * grad_picked[:, :, None], axis=1).astype(jnp.bfloat16)
    grad_router_local = contract_first(hidden_ffn, grad_logits)
    grad_hidden_ffn = jnp.sum(grad_copies.astype(jnp.float32), axis=1) + contract_last(
        grad_logits, router_weight
    )
    grad_resid_norm, grad_gain_ffn = norm_ffn_back(grad_hidden_ffn)
    grad_resid = grad_final + grad_resid_norm
    grad_attn = grad_resid.astype(jnp.bfloat16)
    grad_mixed = contract_last(grad_attn, full_out).astype(jnp.bfloat16)
    grad_mixed_heads = grad_mixed.reshape(length, kv_heads, groups, head_size)
    row_terms = jnp.einsum("tkgd,tkgd->kgt", grad_mixed_heads.astype(jnp.float32), exact_mixed)

    def backward_block(grad_query_sum, pieces):
        key_blk, value_blk, segment_blk, position_blk = pieces
        scores, allowed = block_scores(key_blk, segment_blk, position_blk)
        probs = jnp.where(allowed, jnp.exp(scores - log_total[..., None]), 0.0)
        grad_probs = jnp.einsum(
            "tkgd,skd->kgts", grad_mixed_heads, value_blk, preferred_element_type=jnp.float32
        )
        grad_scores = (probs * (grad_probs - row_terms[..., None])).astype(jnp.bfloat16)
        grad_query_sum = grad_query_sum + jnp.einsum(
            "kgts,skd->tkgd", grad_scores, key_blk, preferred_element_type=jnp.float32
        )
        grad_key_blk = (
            jnp.einsum(
                "kgts,tkgd->skd", grad_scores, grouped_rows, preferred_element_type=jnp.float32
            )
            * score_scale
        )
        grad_value_blk = jnp.einsum(
            "kgts,tkgd->skd",
            probs.astype(jnp.bfloat16),
            grad_mixed_heads,
            preferred_element_type=jnp.float32,
        )
        return (
            grad_query_sum,
            (
                grad_key_blk.reshape(key_block, kv_width),
                grad_value_blk.reshape(key_block, kv_width),
            ),
        )

    grad_query_sum, (grad_key_terms, grad_value_terms) = lax.scan(
        backward_block, jnp.zeros(head_shape, jnp.float32), block_inputs
    )
    grad_key_sum, grad_value_sum = (
        lax.psum_scatter(
            grad_key_terms.reshape(full_length, kv_width).astype(jnp.bfloat16),
            "expert",
            scatter_dimension=0,
            tiled=True,
        ).astype(jnp.float32),
        lax.psum_scatter(
            grad_value_terms.reshape(full_length, kv_width).astype(jnp.bfloat16),
            "expert",
            scatter_dimension=0,
            tiled=True,
        ).astype(jnp.float32),
    )
    grad_query_rot = grad_query_sum.reshape(length, query_heads, head_size) * score_scale
    grad_key_rot = grad_key_sum.reshape(length, kv_heads, head_size)
    grad_value_flat = grad_value_sum.astype(jnp.bfloat16)
    grad_query_raw, grad_query_gain = query_back(grad_query_rot)
    grad_key_raw, grad_key_gain = key_back(grad_key_rot)
    grad_query_low = grad_query_raw.reshape(length, query_heads * head_size).astype(jnp.bfloat16)
    grad_key_low = grad_key_raw.reshape(length, kv_width).astype(jnp.bfloat16)
    grad_hidden_attn = contract_last(grad_query_low, full_query) + contract_last(
        grad_key_low, full_key
    )
    grad_hidden_attn = grad_hidden_attn + contract_last(grad_value_flat, full_value)
    grad_inputs_norm, grad_gain_attn = norm_attn_back(grad_hidden_attn)
    input_grad = grad_resid + grad_inputs_norm
    shards = (
        lax.psum_scatter(
            contract_first(attention_hidden, grad_query_low).astype(jnp.bfloat16),
            "expert",
            scatter_dimension=0,
            tiled=True,
        ).astype(jnp.float32),
        lax.psum_scatter(
            contract_first(attention_hidden, grad_key_low).astype(jnp.bfloat16),
            "expert",
            scatter_dimension=0,
            tiled=True,
        ).astype(jnp.float32),
        lax.psum_scatter(
            contract_first(attention_hidden, grad_value_flat).astype(jnp.bfloat16),
            "expert",
            scatter_dimension=0,
            tiled=True,
        ).astype(jnp.float32),
        lax.psum_scatter(
            contract_first(mixed, grad_attn).astype(jnp.bfloat16),
            "expert",
            scatter_dimension=0,
            tiled=True,
        ).astype(jnp.float32),
    )
    summed = (
        lax.psum(shards[0].astype(jnp.bfloat16), "dp").astype(jnp.float32),
        lax.psum(shards[1].astype(jnp.bfloat16), "dp").astype(jnp.float32),
        lax.psum(shards[2].astype(jnp.bfloat16), "dp").astype(jnp.float32),
        lax.psum(shards[3].astype(jnp.bfloat16), "dp").astype(jnp.float32),
    )
    expert_sums = (
        lax.psum_scatter(
            grad_gate_local.astype(jnp.bfloat16), "dp", scatter_dimension=2, tiled=True
        ).astype(jnp.float32),
        lax.psum_scatter(
            grad_up_local.astype(jnp.bfloat16), "dp", scatter_dimension=2, tiled=True
        ).astype(jnp.float32),
        lax.psum_scatter(
            grad_down_local.astype(jnp.bfloat16), "dp", scatter_dimension=2, tiled=True
        ).astype(jnp.float32),
    )
    small = lax.psum(
        (grad_gain_attn, grad_query_gain, grad_key_gain, grad_gain_ffn, grad_router_local),
        ("dp", "expert"),
    )
    return (
        output,
        input_grad,
        small[0],
        summed[0],
        summed[1],
        summed[2],
        small[1],
        small[2],
        summed[3],
        small[3],
        small[4],
        expert_sums[0],
        expert_sums[1],
        expert_sums[2],
    )


def solution(mesh):
    placed = (
        P(("dp", "expert"), None),
        P("dp", None),
        P(("dp", "expert"), None),
        P(("dp", "expert"), None),
        P(),
        P("expert", None),
        P("expert", None),
        P("expert", None),
        P(),
        P(),
        P("expert", None),
        P(),
        P(),
        P("expert", None, None),
        P("expert", None, None),
        P("expert", None, None),
    )
    return jax.shard_map(
        on_device,
        mesh=mesh,
        in_specs=placed,
        out_specs=(
            P(("dp", "expert"), None),
            P(("dp", "expert"), None),
            P(),
            P("expert", None),
            P("expert", None),
            P("expert", None),
            P(),
            P(),
            P("expert", None),
            P(),
            P(),
            P("expert", None, "dp"),
            P("expert", None, "dp"),
            P("expert", None, "dp"),
        ),
        check_vma=False,
    )
```

profile of v0, /device:TPU:0, one launch (start us, length us, event | category | flops | bytes accessed | tf_op | source)
XLA Modules:
  0.0 2354.6 jit_solution(13473602474203498794)
XLA Ops:
  10.4 31.1 %all-gather.11.cloned.1.call-done = bf16[2048,512]{1,0:T(8,128)(2,1)} async-done(((bf16[256,512]{1,0:T(8,128)(2,1)}), bf16[2048,512]{1,0:T(8,128)(2,1)}) %all-gather.11.cloned.1.call-update) | async-done | bytes 2097168 | tf_op jit(solution)/shard_map/all_gather | solution.py:91
  45.8 25.9 %all-gather.7.cloned.1.call-done = bf16[2048,512]{1,0:T(8,128)(2,1)} async-done(((bf16[256,512]{1,0:T(8,128)(2,1)}), bf16[2048,512]{1,0:T(8,128)(2,1)}) %all-gather.7.cloned.1.call-update) | async-done | bytes 2097168 | tf_op jit(solution)/shard_map/all_gather | solution.py:92
  97.0 22.3 all-gather.9.cloned.1.call-done
  121.4 150.1 %all-gather.15.cloned.1.call-done = bf16[2048,4096]{1,0:T(8,128)(2,1)} async-done(((bf16[256,4096]{1,0:T(8,128)(2,1)}), bf16[2048,4096]{1,0:T(8,128)(2,1)}) %all-gather.15.cloned.1.call-update) | async-done | bytes 16777232 | tf_op jit(solution)/shard_map/all_gather | solution.py:90
  296.4 20.6 while.42
  320.1 102.2 %all-gather.17.cloned.1.call-done = bf16[4096,2048]{1,0:T(8,128)(2,1)} async-done(((bf16[512,2048]{1,0:T(8,128)(2,1)}), bf16[4096,2048]{1,0:T(8,128)(2,1)}) %all-gather.17.cloned.1.call-update) | async-done | bytes 16777232 | tf_op jit(solution)/shard_map/all_gather | solution.py:93
  442.7 188.3 %all_to_all.20 = bf16[8,256,2048]{2,1,0:T(8,128)(2,1)S(1)} all-to-all(bf16[8,256,2048]{2,1,0:T(8,128)(2,1)} %bitcast.374), channel_id=1, replica_groups=mesh['dp'=4,'expert'=8] {'expert'}, dimensions={0} | all-to-all | bytes 16777216 | tf_op jit(solution)/shard_map/all_to_all | solution.py:204
  682.3 183.4 %all-to-all-done.1 = bf16[8,256,2048]{2,1,0:T(8,128)(2,1)} async-done(((bf16[8,256,2048]{2,1,0:T(8,128)(2,1)}), bf16[8,256,2048]{2,1,0:T(8,128)(2,1)}, u32[]{:S(2)}, u32[]{:S(2)}) %all-to-all-start.1) | async-done | bytes 8388640 | tf_op jit(solution)/shard_map/all_to_all | solution.py:211
  895.8 190.3 %all_to_all.21 = bf16[8,256,2048]{2,1,0:T(8,128)(2,1)} all-to-all(bf16[8,256,2048]{2,1,0:T(8,128)(2,1)} %bitcast.373), channel_id=1, replica_groups=mesh['dp'=4,'expert'=8] {'expert'}, dimensions={0} | all-to-all | bytes 16777216 | tf_op jit(solution)/shard_map/all_to_all | solution.py:227
  1086.1 16.2 fusion.74
  1115.3 14.3 fusion.62
  1149.4 177.3 %all-to-all-done.3 = bf16[8,256,2048]{2,1,0:T(8,128)(2,1)} async-done(((bf16[8,256,2048]{2,1,0:T(8,128)(2,1)}), bf16[8,256,2048]{2,1,0:T(8,128)(2,1)}, u32[]{:S(2)}, u32[]{:S(2)}) %all-to-all-start.3) | async-done | bytes 8388640 | tf_op jit(solution)/shard_map/all_to_all | solution.py:252
  1326.7 13.4 gather_fusion.1
  1369.4 36.9 %while.43 = (s32[]{:T(128)}, f32[128,4,8,128]{0,3,2,1:T(8,128)}, bf16[2,512,512]{2,1,0:T(8,128)(2,1)}, bf16[2,512,512]{2,1,0:T(8,128)(2,1)}, bf16[2,512,4,128]{3...) while((s32[]{:T(128)}, f32[128,4,8,128]{0,3,2,1:T(8,128)}, ...), condition=%wide.region_24.25_spmd.clone, body=%wide.region_23.24_spmd.clone.sunk | while | flops 2707095552 | bytes 92141416 | solution.py:304
  1407.2 30.6 %reduce-scatter.10.cloned.1.call-done = bf16[128,512]{1,0:T(8,128)(2,1)} async-done(((bf16[1024,512]{1,0:T(8,128)(2,1)}), bf16[128,512]{1,0:T(8,128)(2,1)}) %reduce-scatter.10.cloned.1.call-update) | async-done | bytes 131088 | tf_op jit(solution)/shard_map/reduce_scatter | solution.py:308
  1443.9 26.8 %reduce-scatter.12.cloned.1.call-done = bf16[128,512]{1,0:T(8,128)(2,1)} async-done(((bf16[1024,512]{1,0:T(8,128)(2,1)}), bf16[128,512]{1,0:T(8,128)(2,1)}) %reduce-scatter.12.cloned.1.call-update) | async-done | bytes 131088 | tf_op jit(solution)/shard_map/reduce_scatter | solution.py:314
  1548.0 164.9 %reduce-scatter.20.cloned.1.call-done = bf16[512,2048]{1,0:T(8,128)(2,1)} async-done(((bf16[4096,2048]{1,0:T(8,128)(2,1)}), bf16[512,2048]{1,0:T(8,128)(2,1)}) %reduce-scatter.20.cloned.1.call-update) | async-done | bytes 2097168 | tf_op jit(solution)/shard_map/reduce_scatter | solution.py:353
  1712.9 168.8 %reduce-scatter.14.cloned.1.call-done = bf16[256,4096]{1,0:T(8,128)(2,1)} async-done(((bf16[2048,4096]{1,0:T(8,128)(2,1)}), bf16[256,4096]{1,0:T(8,128)(2,1)}) %reduce-scatter.14.cloned.1.call-update) | async-done | bytes 2097168 | tf_op jit(solution)/shard_map/reduce_scatter | solution.py:335
  1882.9 70.4 %reduce-scatter.26.cloned.1.call-done = bf16[2,768,512]{2,1,0:T(8,128)(2,1)} async-done(((bf16[2,768,2048]{2,1,0:T(8,128)(2,1)}), bf16[2,768,512]{2,1,0:T(8,128)(2,1)}) %reduce-scatter.26.cloned.1.call-update) | async-done | bytes 1572880 | tf_op jit(solution)/shard_map/reduce_scatter | solution.py:373
  1956.8 69.6 %reduce-scatter.22.cloned.1.call-done = bf16[2,2048,192]{1,2,0:T(8,128)(2,1)} async-done(((bf16[2,2048,768]{1,2,0:T(8,128)(2,1)}), bf16[2,2048,192]{1,2,0:T(8,128)(2,1)}) %reduce-scatter.22.cloned.1.call-update) | async-done | bytes 1572880 | tf_op jit(solution)/shard_map/reduce_scatter | solution.py:367
  2029.9 69.6 %reduce-scatter.24.cloned.1.call-done = bf16[2,2048,192]{1,2,0:T(8,128)(2,1)} async-done(((bf16[2,2048,768]{1,2,0:T(8,128)(2,1)}), bf16[2,2048,192]{1,2,0:T(8,128)(2,1)}) %reduce-scatter.24.cloned.1.call-update) | async-done | bytes 1572880 | tf_op jit(solution)/shard_map/reduce_scatter | solution.py:370
  2119.8 40.1 %all-reduce.4 = (f32[2048]{0:T(1024)}, f32[128]{0:T(128)}, f32[128]{0:T(128)}, f32[2048]{0:T(1024)}) all-reduce(f32[2048]{0:T(1024)S(1)} %get-tuple-element.495, f32[128]{0:T(128)S(1)} %get-tuple-element.491, f32[128]{0:T(128)S(1)} %copy-done.78, f32[2048]{0:T(1024)S(1)} %copy-done.65), channel_id=1, replica_groups=mesh['dp'=4,'expert'=8] {'dp','expert'}, use_global_device_ids=true, to_apply=%region_31.32 | all-reduce | flops 4352 | bytes 34816 | tf_op jit(solution)/shard_map/psum | solution.py:377
  2159.9 58.0 %all-reduce.11.cloned.1.call-done = (bf16[256,4096]{1,0:T(8,128)(2,1)}, bf16[256,512]{1,0:T(8,128)(2,1)}, bf16[256,512]{1,0:T(8,128)(2,1)}, bf16[512,2048]{1,0:T(8,128)(2,1)}) async-done(((bf16[256,4096]{1,0:T(8,128)(2,1)}, bf16[256,512]{1,0:T(8,128)(2,1)}, bf16[256,512]{1,0:T(8,128)(2,1)}, bf16[512,2048]{1,0:T(8,128)(2,1)}), (bf16[256,4096]{1,0:T(8,128)(2,1)}, bf16[256,512]{1,0:T(8,128)(2,1)}, ...) | async-done | bytes 4718608 | tf_op jit(solution)/shard_map/psum | solution.py:361
  2228.3 118.0 %all-reduce.9.cloned.1.call-done = f32[2048,16]{0,1:T(8,128)} async-done(((f32[2048,16]{0,1:T(8,128)}), f32[2048,16]{0,1:T(8,128)}) %all-reduce.9.cloned.1.call-update) | async-done | bytes 131088 | tf_op jit(solution)/shard_map/psum | solution.py:377
  (426 shorter events, 413.2 us)
Async XLA Ops:
  7.2 674.8 %copy-start = (bf16[2048,16]{0,1:T(8,128)(2,1)S(1)}, bf16[2048,16]{0,1:T(8,128)(2,1)}, u32[]{:S(2)}) copy-start(bf16[2048,16]{0,1:T(8,128)(2,1)} %param.34) | copy-start | bytes 196612
  7.2 34.3 %all-gather.11.cloned.1.call-start = ((), (), s32[]{:S(2)}) async-start(), calls=%async_computation.15 | async-start | bytes 2359296 | tf_op jit(solution)/shard_map/all_gather | solution.py:91
  8.0 63.8 %all-gather.7.cloned.1.call-start = ((), (), s32[]{:S(2)}) async-start(), calls=%async_computation.13 | async-start | bytes 2359296 | tf_op jit(solution)/shard_map/all_gather | solution.py:92
  8.7 86.8 %all-gather.13.cloned.1.call-start = ((), (), s32[]{:S(2)}) async-start(), calls=%async_computation.16 | async-start | bytes 1179648 | tf_op jit(solution)/shard_map/all_gather | solution.py:123
  10.4 271.5 %copy-start.37 = (f32[128,64]{1,0:T(8,128)}, f32[128,64]{1,0:T(8,128)S(1)}, u32[]{:S(2)}) copy-start(f32[128,64]{1,0:T(8,128)S(1)} %get-tuple-element.599) | copy-start | bytes 98308
  10.4 271.5 %copy-start.39 = (f32[128,64]{1,0:T(8,128)}, f32[128,64]{1,0:T(8,128)S(1)}, u32[]{:S(2)}) copy-start(f32[128,64]{1,0:T(8,128)S(1)} %get-tuple-element.600) | copy-start | bytes 98308
  45.7 73.6 %all-gather.9.cloned.1.call-start = ((), (), s32[]{:S(2)}) async-start(), calls=%async_computation.14 | async-start | bytes 1179648 | tf_op jit(solution)/shard_map/all_gather | solution.py:124
  74.5 197.0 %all-gather.15.cloned.1.call-start = ((), (), s32[]{:S(2)}) async-start(), calls=%async_computation.17 | async-start | bytes 18874368 | tf_op jit(solution)/shard_map/all_gather | solution.py:90
  75.1 347.2 %all-gather.17.cloned.1.call-start = ((), (), s32[]{:S(2)}) async-start(), calls=%async_computation.18 | async-start | bytes 18874368 | tf_op jit(solution)/shard_map/all_gather | solution.py:93
  676.5 189.2 %all-to-all-start.1 = ((bf16[8,256,2048]{2,1,0:T(8,128)(2,1)}), bf16[8,256,2048]{2,1,0:T(8,128)(2,1)}, u32[]{:S(2)}, u32[]{:S(2)}) async-start(bf16[8,256,2048]{2,1,0:T(8,128)(2,1)} %bitcast.372), calls=%async_computation.1 | async-start | bytes 16777216 | tf_op jit(solution)/shard_map/all_to_all | solution.py:211
  1137.8 188.9 %all-to-all-start.3 = ((bf16[8,256,2048]{2,1,0:T(8,128)(2,1)}), bf16[8,256,2048]{2,1,0:T(8,128)(2,1)}, u32[]{:S(2)}, u32[]{:S(2)}) async-start(bf16[8,256,2048]{2,1,0:T(8,128)(2,1)} %bitcast.371), calls=%async_computation.3 | async-start | bytes 16777216 | tf_op jit(solution)/shard_map/all_to_all | solution.py:252
  1142.8 294.9 %reduce-scatter.10.cloned.1.call-start = ((), (), s32[]{:S(2)}) async-start(), calls=%async_computation.19 | async-start | bytes 1179648 | tf_op jit(solution)/shard_map/reduce_scatter | solution.py:308
  1406.4 64.3 %reduce-scatter.12.cloned.1.call-start = ((), (), s32[]{:S(2)}) async-start(), calls=%async_computation.20 | async-start | bytes 1179648 | tf_op jit(solution)/shard_map/reduce_scatter | solution.py:314
  1407.1 140.9 %reduce-scatter.16.cloned.1.call-start = ((), (), s32[]{:S(2)}) async-start(), calls=%async_computation.22 | async-start | bytes 2359296 | tf_op jit(solution)/shard_map/reduce_scatter | solution.py:341
  1443.9 104.2 %reduce-scatter.18.cloned.1.call-start = ((), (), s32[]{:S(2)}) async-start(), calls=%async_computation.23 | async-start | bytes 2359296 | tf_op jit(solution)/shard_map/reduce_scatter | solution.py:347
  1473.8 239.2 %reduce-scatter.20.cloned.1.call-start = ((), (), s32[]{:S(2)}) async-start(), calls=%async_computation.24 | async-start | bytes 18874368 | tf_op jit(solution)/shard_map/reduce_scatter | solution.py:353
  1482.4 399.3 %reduce-scatter.14.cloned.1.call-start = ((), (), s32[]{:S(2)}) async-start(), calls=%async_computation.21 | async-start | bytes 18874368 | tf_op jit(solution)/shard_map/reduce_scatter | solution.py:335
  1509.8 443.5 %reduce-scatter.26.cloned.1.call-start = ((), (), s32[]{:S(2)}) async-start(), calls=%async_computation.28 | async-start | bytes 7864320 | tf_op jit(solution)/shard_map/reduce_scatter | solution.py:373
  1522.6 503.8 %reduce-scatter.22.cloned.1.call-start = ((), (), s32[]{:S(2)}) async-start(), calls=%async_computation.26 | async-start | bytes 7864320 | tf_op jit(solution)/shard_map/reduce_scatter | solution.py:367
  1535.2 564.3 %reduce-scatter.24.cloned.1.call-start = ((), (), s32[]{:S(2)}) async-start(), calls=%async_computation.27 | async-start | bytes 7864320 | tf_op jit(solution)/shard_map/reduce_scatter | solution.py:370
  1547.9 334.2 %copy-start.26 = (bf16[128,2048]{1,0:T(8,128)(2,1)S(1)}, bf16[128,2048]{1,0:T(8,128)(2,1)}, u32[]{:S(2)}) copy-start(bf16[128,2048]{1,0:T(8,128)(2,1)} %copy-done.25) | copy-start | bytes 1572868
  1547.9 334.2 %copy-start.64 = (bf16[128,16]{0,1:T(8,128)(2,1)S(1)}, bf16[128,16]{0,1:T(8,128)(2,1)}, u32[]{:S(2)}) copy-start(bf16[128,16]{0,1:T(8,128)(2,1)} %copy-done.63) | copy-start | bytes 12292
  1547.9 670.0 %all-reduce.11.cloned.1.call-start = ((), (), s32[]{:S(2)}) async-start(), calls=%async_computation.29 | async-start | bytes 9437184 | tf_op jit(solution)/shard_map/psum | solution.py:361
  1881.8 464.5 %all-reduce.9.cloned.1.call-start = ((), (), s32[]{:S(2)}) async-start(), calls=%async_computation.25 | async-start | bytes 262144 | tf_op jit(solution)/shard_map/psum | solution.py:377
  (91 other events, 2855.8 us)
Sparse Core Ops, SparseCore 0:
  9.7 31.7 all-gather.10
  43.1 28.5 all-gather.6
  73.9 21.5 all-gather.12
  97.5 21.7 all-gather.8
  120.8 150.7 all-gather.14
  273.0 149.3 all-gather.16
  1406.5 31.2 reduce-scatter.9
  1440.0 30.5 reduce-scatter.11
  1473.0 33.9 reduce-scatter.15
  1509.1 34.4 reduce-scatter.17
  1546.0 166.8 reduce-scatter.19
  1715.1 166.5 reduce-scatter.13
  1884.7 68.5 reduce-scatter.25
  1956.2 70.2 reduce-scatter.21
  2029.2 70.2 reduce-scatter.23
  2103.1 114.7 all-reduce.10
  2223.8 122.3 all-reduce.8
where the time goes:
time: 2360 us; the launch traced here: 2350 us
  waiting for transfers between devices  1480 us (63%)
  blocking collectives  419 us (18%)
  matrix products  237 us (10%)
  local copies, waits for them, and re-layouts  101 us (4%)
  other arithmetic  84 us (4%)
    all_to_all x1, blocking collectives, on_device(): lax.all_to_all(grad_box.reshape(slot_shape), 'expert', split_axis=0, conc...  190 us
    all_to_all x1, blocking collectives, on_device(): lax.all_to_all(outbox.reshape(slot_shape), 'expert', split_axis=0, concat...  188 us
    all_to_all x1, waiting for transfers between devices, on_device(): lax.all_to_all(expert_out.reshape(slot_shape), 'expert', split_axis=0, co...  183 us
    all_to_all x1, waiting for transfers between devices, on_device(): lax.all_to_all(grad_slot_rows.reshape(slot_shape), 'expert', split_axis=0...  177 us
    reduce_scatter x1, waiting for transfers between devices, on_device(): lax.psum_scatter(contract_first(attention_hidden, grad_query_low).astype(...  169 us
    reduce_scatter x1, waiting for transfers between devices, on_device(): lax.psum_scatter(contract_first(mixed, grad_attn).astype(jnp.bfloat16), '...  165 us
    all_gather x1, waiting for transfers between devices, on_device(): lax.all_gather(query_weight, 'expert', axis=0, tiled=True)  150 us
    psum x1, waiting for transfers between devices, on_device(): lax.psum((grad_gain_attn, grad_query_gain, grad_key_gain, grad_gain_ffn,...  118 us
  transfers between devices with their start and end apart: 19, of which 17 were waited for; matrix products, arithmetic and copies ran while one was open for 8% of the time, Pallas kernels for 0%

commit v1 on v0

v1 whole, which is shorter than its diff:
```python
import functools

import jax
import jax.numpy as jnp
from jax import lax
from jax.experimental import pallas as pl
from jax.experimental.pallas import tpu as pltpu
from jax.sharding import PartitionSpec as P

eps_norm = 1e-06
rope_base = 1000000.0
log2e = 1.4426950408889634
low = jnp.bfloat16
high = jnp.float32


def norm_rows(values, gain):
    factor = lax.rsqrt(jnp.mean(values * values, axis=-1, keepdims=True) + eps_norm)
    return values * factor * gain


def norm_back(values, gain, grad):
    factor = lax.rsqrt(jnp.mean(values * values, axis=-1, keepdims=True) + eps_norm)
    scaled = gain * grad
    inner = jnp.mean(values * scaled, axis=-1, keepdims=True)
    grad_values = factor * scaled - values * (factor * factor * factor * inner)
    return grad_values, grad * values * factor


def dot(left, right):
    return jnp.dot(left, right, preferred_element_type=high)


def dot_first(left, right):
    return lax.dot_general(left, right, (((0,), (0,)), ((), ())), preferred_element_type=high)


def dot_last(left, right):
    return lax.dot_general(left, right, (((1,), (1,)), ((), ())), preferred_element_type=high)


def rotary_tables(length, head_size):
    half = head_size // 2
    freqs = rope_base ** (-jnp.arange(half, dtype=high) * 2.0 / head_size)
    angles = jnp.arange(length, dtype=high)[:, None] * freqs[None, :]
    cosines, sines = jnp.cos(angles), jnp.sin(angles)
    return jnp.concatenate([cosines, cosines], 1), jnp.concatenate([-sines, sines], 1)


def rotate(values, cosines, sines):
    return values * cosines + pltpu.roll(values, values.shape[-1] // 2, 1) * sines


def unrotate(values, cosines, sines):
    return values * cosines - pltpu.roll(values, values.shape[-1] // 2, 1) * sines


def key_spans(length):
    block = min(256, length)
    longest = length // 2
    spans = []
    for begin in range(0, length, block):
        first = max(0, begin - longest + 1) // block * block
        spans.append((begin, block, first, begin + block - first))
    return spans


def tile_mask(seg_col, seg_row, begin, rows, first, keys):
    query_at = begin + lax.broadcasted_iota(jnp.int32, (rows, keys), 0)
    key_at = first + lax.broadcasted_iota(jnp.int32, (rows, keys), 1)
    return (query_at >= key_at) & (seg_col[begin : begin + rows, :1] == seg_row[:1, first : first + keys])


def attention_forward(
    query_ref, key_ref, value_ref, query_gain_ref, key_gain_ref, cos_ref, sin_ref, col_ref, row_ref,
    mixed_ref, query_low_ref, key_low_ref, value_low_ref, inverse_ref, value_wide,
):
    head_size = query_ref.shape[1]

    @pl.when(pl.program_id(0) == 0)
    def first_head():
        rotated = rotate(norm_rows(key_ref[...], key_gain_ref[...]), cos_ref[...], sin_ref[...])
        key_low_ref[...] = rotated.astype(low)
        value_low_ref[...] = value_ref[...].astype(low)
        value_wide[:, :head_size] = value_ref[...].astype(low)
        value_wide[:, head_size:] = jnp.ones_like(value_low_ref)

    rotated = rotate(norm_rows(query_ref[...], query_gain_ref[...]), cos_ref[...], sin_ref[...])
    query_low_ref[...] = (rotated * (head_size**-0.5 * log2e)).astype(low)
    for begin, rows, first, keys in key_spans(query_ref.shape[0]):
        scores = dot_last(query_low_ref[pl.ds(begin, rows)], key_low_ref[pl.ds(first, keys)])
        allowed = tile_mask(col_ref, row_ref, begin, rows, first, keys)
        terms = jnp.where(allowed, jnp.exp2(scores), 0.0).astype(low)
        sums = dot(terms, value_wide[pl.ds(first, keys)])
        inverse = 1.0 / sums[:, head_size:]
        mixed_ref[pl.ds(begin, rows)] = (sums[:, :head_size] * inverse).astype(low)
        inverse_ref[pl.ds(begin, rows)] = inverse


def attention_backward(
    query_ref, query_low_ref, key_low_ref, value_low_ref, inverse_ref, mixed_ref, grad_mixed_ref,
    query_gain_ref, cos_ref, sin_ref, col_ref, row_ref,
    grad_query_ref, grad_key_ref, grad_value_ref, grad_gain_ref,
):
    length, head_size = query_ref.shape

    @pl.when(pl.program_id(0) == 0)
    def first_head():
        grad_key_ref[...] = jnp.zeros_like(grad_key_ref)
        grad_value_ref[...] = jnp.zeros_like(grad_value_ref)
        grad_gain_ref[...] = jnp.zeros_like(grad_gain_ref)

    for begin, rows, first, keys in key_spans(length):
        block = pl.ds(begin, rows)
        query_low = query_low_ref[block]
        key_low = key_low_ref[pl.ds(first, keys)]
        scaled = grad_mixed_ref[block].astype(high) * inverse_ref[block]
        row_term = jnp.sum(scaled * mixed_ref[block].astype(high), axis=-1, keepdims=True)
        scaled = scaled.astype(low)
        scores = dot_last(query_low, key_low)
        allowed = tile_mask(col_ref, row_ref, begin, rows, first, keys)
        terms = jnp.where(allowed, jnp.exp2(scores), 0.0)
        grad_probs = dot_last(scaled, value_low_ref[pl.ds(first, keys)])
        grad_scores = (terms * (grad_probs - row_term)).astype(low)
        grad_value_ref[pl.ds(first, keys)] += dot_first(terms.astype(low), scaled)
        grad_key_ref[pl.ds(first, keys)] += dot_first(grad_scores, query_low) * (1.0 / log2e)
        grad_rotated = dot(grad_scores, key_low) * head_size**-0.5
        grad_normed = unrotate(grad_rotated, cos_ref[block], sin_ref[block])
        grad_raw, gain_rows = norm_back(query_ref[block], query_gain_ref[...], grad_normed)
        grad_query_ref[block] = grad_raw.astype(low)
        grad_gain_ref[...] += jnp.broadcast_to(
            jnp.sum(gain_rows, axis=0, keepdims=True), grad_gain_ref.shape
        )


def whole(shape):
    return pl.BlockSpec(shape, lambda head: (0,) * len(shape))


def run_attention_forward(raw, heads, head_size, query_gain, key_gain, cosines, sines, seg_col, seg_row):
    length = raw.shape[0]
    per_head = pl.BlockSpec((length, head_size), lambda head: (0, head))
    one = (length, head_size)
    wide = jax.ShapeDtypeStruct((length, heads * head_size), low)
    narrow = jax.ShapeDtypeStruct(one, low)
    return pl.pallas_call(
        attention_forward,
        grid=(heads,),
        in_specs=[
            per_head,
            pl.BlockSpec(one, lambda head: (0, heads)),
            pl.BlockSpec(one, lambda head: (0, heads + 1)),
            whole((1, head_size)),
            whole((1, head_size)),
            whole(one),
            whole(one),
            whole(one),
            whole((8, length)),
        ],
        out_specs=[per_head, per_head, whole(one), whole(one), per_head],
        out_shape=[wide, wide, narrow, narrow, jax.ShapeDtypeStruct((length, heads * head_size), high)],
        scratch_shapes=[pltpu.VMEM((length, 2 * head_size), low)],
        compiler_params=pltpu.CompilerParams(vmem_limit_bytes=50 << 20),
        cost_estimate=pl.CostEstimate(
            flops=3 * heads * length * length * head_size, bytes_accessed=8 * length * heads * head_size,
            transcendentals=heads * length * length // 2,
        ),
    )(raw, raw, raw, query_gain, key_gain, cosines, sines, seg_col, seg_row)


def run_attention_backward(
    raw, query_low, key_low, value_low, inverse, mixed, grad_mixed, heads, head_size, query_gain,
    cosines, sines, seg_col, seg_row,
):
    length = raw.shape[0]
    per_head = pl.BlockSpec((length, head_size), lambda head: (0, head))
    one = (length, head_size)
    return pl.pallas_call(
        attention_backward,
        grid=(heads,),
        in_specs=[
            per_head, per_head, whole(one), whole(one), per_head, per_head, per_head,
            whole((1, head_size)), whole(one), whole(one), whole(one), whole((8, length)),
        ],
        out_specs=[per_head, whole(one), whole(one), whole((8, head_size))],
        out_shape=[
            jax.ShapeDtypeStruct((length, heads * head_size), low),
            jax.ShapeDtypeStruct(one, high),
            jax.ShapeDtypeStruct(one, high),
            jax.ShapeDtypeStruct((8, head_size), high),
        ],
        compiler_params=pltpu.CompilerParams(vmem_limit_bytes=50 << 20),
        cost_estimate=pl.CostEstimate(
            flops=6 * heads * length * length * head_size, bytes_accessed=16 * length * heads * head_size,
            transcendentals=heads * length * length // 2,
        ),
    )(
        raw, query_low, key_low, value_low, inverse, mixed, grad_mixed, query_gain, cosines, sines,
        seg_col, seg_row,
    )


def gather_tokens(rows):
    return lax.all_gather(rows, "expert", axis=0, tiled=True)


def scatter_sum(partial):
    return lax.psum_scatter(partial, "expert", scatter_dimension=0, tiled=True)


def on_device(
    tokens,
    segments,
    routes,
    cotangent,
    norm_gain_attn,
    query_weight,
    key_matrix,
    value_matrix,
    query_gain,
    key_gain,
    out_weight,
    norm_gain_ffn,
    router_weight,
    gate_weight,
    up_weight,
    down_weight,
):
    length, model_width = tokens.shape
    head_size = query_gain.shape[0]
    peers = lax.axis_size("expert")
    groups = lax.axis_size("dp")
    me = lax.axis_index("expert")
    group = lax.axis_index("dp")
    shard_rows, query_width = query_weight.shape
    kv_width = key_matrix.shape[1]
    kv_heads = kv_width // head_size
    heads = query_width // head_size // peers
    sharers = peers // kv_heads
    local_width = heads * head_size
    local_experts = gate_weight.shape[0]
    experts = local_experts * peers
    full_length = length * peers
    piece = shard_rows // groups

    def own_rows(matrix):
        return lax.dynamic_slice_in_dim(matrix, group * piece, piece, 0)

    def columns(matrix, width, copies):
        split = own_rows(matrix).reshape(piece, -1, width).transpose(1, 0, 2)
        return jnp.repeat(split, copies, axis=0)

    outgoing = jnp.concatenate(
        [
            columns(query_weight, local_width, 1),
            columns(key_matrix, head_size, sharers),
            columns(value_matrix, head_size, sharers),
        ],
        axis=2,
    )
    arrived = lax.all_to_all(outgoing, "expert", split_axis=0, concat_axis=0, tiled=True)
    projection = lax.all_gather(arrived, "dp", axis=1, tiled=True).reshape(model_width, -1)

    inputs = tokens.astype(high)
    hidden_local = norm_rows(inputs, norm_gain_attn).astype(low)
    hidden = gather_tokens(hidden_local)
    raw = dot(hidden, projection)
    cosines, sines = rotary_tables(full_length, head_size)
    seg_col = jnp.broadcast_to(segments.reshape(full_length, 1), (full_length, head_size))
    seg_row = jnp.broadcast_to(segments.reshape(1, full_length), (8, full_length))
    query_gain_row = query_gain.reshape(1, head_size)
    key_gain_row = key_gain.reshape(1, head_size)
    mixed, query_low, key_low, value_low, inverse = run_attention_forward(
        raw, heads, head_size, query_gain_row, key_gain_row, cosines, sines, seg_col, seg_row
    )
    attn = scatter_sum(dot(mixed, out_weight).astype(low))
    resid = inputs + attn.astype(high)
    ffn_local = norm_rows(resid, norm_gain_ffn).astype(low)
    ffn_rows = gather_tokens(ffn_local)
    cotangents = gather_tokens(cotangent)
    all_routes = gather_tokens(routes)

    def gates_of(rows, route_rows):
        logits = dot(rows, router_weight)
        named = jnp.any(
            route_rows[:, :, None] == jnp.arange(experts, dtype=jnp.int32)[None, None, :], axis=1
        )
        top = jnp.max(jnp.where(named, logits, -jnp.inf), axis=-1, keepdims=True)
        terms = jnp.where(named, jnp.exp(jnp.where(named, logits - top, 0.0)), 0.0)
        return terms / jnp.sum(terms, axis=-1, keepdims=True)

    gates_all = gates_of(ffn_rows, all_routes)
    own_gates = lax.dynamic_slice_in_dim(gates_all, me * local_experts, local_experts, 1)
    mixture = 0.0
    grad_rows = 0.0
    gate_grads, grad_gate_w, grad_up_w, grad_down_w = [], [], [], []
    for expert in range(local_experts):
        gate_col = own_gates[:, expert : expert + 1]
        gate_pre = dot(ffn_rows, gate_weight[expert])
        up_pre = dot(ffn_rows, up_weight[expert])
        share = jax.nn.sigmoid(gate_pre)
        silu = gate_pre * share
        act = silu * up_pre
        gated_act = (act * gate_col).astype(low)
        mixture = mixture + dot(gated_act, down_weight[expert])
        plain = dot_last(cotangents, down_weight[expert])
        gate_grads.append(jnp.sum(act * plain, axis=-1, keepdims=True))
        grad_act = plain * gate_col
        grad_gate_pre = (grad_act * up_pre * (share * (1.0 + gate_pre * (1.0 - share)))).astype(low)
        grad_up_pre = (grad_act * silu).astype(low)
        grad_rows = (
            grad_rows
            + dot_last(grad_gate_pre, gate_weight[expert])
            + dot_last(grad_up_pre, up_weight[expert])
        )
        hidden_units = gated_act.shape[1]
        grad_gate_w.append(dot_first(grad_gate_pre, ffn_rows).astype(low).reshape(groups, -1, model_width))
        grad_up_w.append(dot_first(grad_up_pre, ffn_rows).astype(low).reshape(groups, -1, model_width))
        cut_width = model_width // groups
        grad_down_w.append(
            jnp.stack([
                dot_first(gated_act, cotangents[:, part * cut_width : (part + 1) * cut_width]).astype(low)
                for part in range(groups)
            ])
        )

    gate_grad = jnp.concatenate(gate_grads, axis=1)
    lane_pad = 128 - 2 * experts % 128
    placed = jnp.zeros((full_length, experts), high)
    placed = lax.dynamic_update_slice_in_dim(placed, gate_grad, me * local_experts, 1)
    upper = placed.astype(low)
    lower = (placed - upper.astype(high)).astype(low)
    sent = jnp.concatenate(
        [grad_rows.astype(low), upper, lower, jnp.zeros((full_length, lane_pad), low)], axis=1
    )
    summed_rows = scatter_sum(sent)
    output = (resid + scatter_sum(mixture.astype(low)).astype(high)).astype(low)
    grad_gates = summed_rows[:, model_width : model_width + experts].astype(high) + summed_rows[
        :, model_width + experts : model_width + 2 * experts
    ].astype(high)
    gates = gates_of(ffn_local, routes)
    grad_logits = (
        gates * (grad_gates - jnp.sum(gates * grad_gates, axis=-1, keepdims=True))
    ).astype(low)
    grad_router = dot_first(ffn_local, grad_logits)
    grad_hidden_ffn = summed_rows[:, :model_width].astype(high) + dot_last(grad_logits, router_weight)
    grad_resid_norm, gain_rows_ffn = norm_back(resid, norm_gain_ffn, grad_hidden_ffn)
    grad_resid = cotangent.astype(high) + grad_resid_norm
    grad_attn = gather_tokens(grad_resid.astype(low))
    grad_mixed = dot_last(grad_attn, out_weight).astype(low)
    grad_out = dot_first(mixed, grad_attn)
    grad_query_low, grad_key_part, grad_value_part, query_gain_part = run_attention_backward(
        raw, query_low, key_low, value_low, inverse, mixed, grad_mixed, heads, head_size,
        query_gain_row, cosines, sines, seg_col, seg_row,
    )
    both = jnp.concatenate([grad_key_part, grad_value_part], axis=1)
    step = 1
    while step < sharers:
        swap = [(peer, peer ^ step) for peer in range(peers)]
        both = both + lax.ppermute(both.astype(low), "expert", swap).astype(high)
        step *= 2
    grad_key_rot, grad_value = both[:, :head_size], both[:, head_size:].astype(low)
    place = me % sharers
    half = head_size // 2
    swapped = jnp.concatenate([grad_key_rot[:, half:], grad_key_rot[:, :half]], axis=1)
    key_raw = raw[:, local_width : local_width + head_size]
    grad_key, key_gain_rows = norm_back(key_raw, key_gain, grad_key_rot * cosines - swapped * sines)
    grad_shared = jnp.where(
        place == 0, grad_key.astype(low), jnp.where(place == 1, grad_value, jnp.zeros_like(grad_value))
    )
    own_columns = jnp.concatenate([grad_query_low, grad_shared], axis=1)
    shared_weight = jnp.where(
        place == 0,
        projection[:, local_width : local_width + head_size],
        projection[:, local_width + head_size :],
    )
    own_weight = jnp.concatenate([projection[:, :local_width], shared_weight], axis=1)
    grad_hidden_attn = scatter_sum(dot_last(own_columns, own_weight).astype(low)).astype(high)
    grad_inputs_norm, gain_rows_attn = norm_back(inputs, norm_gain_attn, grad_hidden_attn)
    input_grad = grad_resid + grad_inputs_norm

    grad_projection = dot_first(hidden, own_columns).astype(low)
    grad_projection = grad_projection.reshape(peers, shard_rows, -1)
    grad_projection = lax.psum_scatter(grad_projection, "dp", scatter_dimension=1, tiled=True)
    grad_projection = lax.all_to_all(
        grad_projection, "expert", split_axis=0, concat_axis=0, tiled=True
    )
    grad_projection = lax.all_gather(grad_projection, "dp", axis=1, tiled=True)
    grad_query_w = (
        grad_projection[:, :, :local_width].transpose(1, 0, 2).reshape(shard_rows, query_width)
    ).astype(high)
    shared = grad_projection[:, :, local_width:].reshape(kv_heads, sharers, shard_rows, head_size)
    grad_key_w = shared[:, 0].transpose(1, 0, 2).reshape(shard_rows, kv_width).astype(high)
    grad_value_w = shared[:, 1].transpose(1, 0, 2).reshape(shard_rows, kv_width).astype(high)
    grad_out_w = lax.psum_scatter(grad_out.astype(low), "dp", scatter_dimension=0, tiled=True)
    grad_out_w = lax.all_gather(grad_out_w, "dp", axis=0, tiled=True).astype(high)

    wide = jnp.concatenate(grad_gate_w + grad_up_w, axis=1)
    wide = lax.psum_scatter(wide, "dp", scatter_dimension=0, tiled=True)
    wide = wide.reshape(2, local_experts, hidden_units // groups, model_width).transpose(0, 1, 3, 2)
    wide = wide.astype(high)
    down = jnp.concatenate(grad_down_w, axis=1)
    down = lax.psum_scatter(down, "dp", scatter_dimension=0, tiled=True)
    down = down.reshape(local_experts, hidden_units, cut_width).astype(high)
    expert_sums = (wide[0], wide[1], down)
    key_gain_grad = jnp.where(place == 0, jnp.sum(key_gain_rows, axis=0), 0.0)
    small = jnp.concatenate(
        [
            jnp.sum(gain_rows_attn, axis=0),
            jnp.sum(gain_rows_ffn, axis=0),
            query_gain_part[0],
            key_gain_grad,
            grad_router.reshape(-1),
        ]
    )
    small = lax.psum(small, ("dp", "expert"))
    cut = 2 * model_width
    return (
        output,
        input_grad,
        small[:model_width],
        grad_query_w,
        grad_key_w,
        grad_value_w,
        small[cut : cut + head_size],
        small[cut + head_size : cut + 2 * head_size],
        grad_out_w,
        small[model_width:cut],
        small[cut + 2 * head_size :].reshape(model_width, experts),
        *expert_sums,
    )


def solution(mesh):
    rows = P(("dp", "expert"), None)
    split = P("expert", None)
    cube = P("expert", None, None)
    cut = P("expert", None, "dp")
    return jax.shard_map(
        on_device,
        mesh=mesh,
        in_specs=(
            rows, P("dp", None), rows, rows, P(), split, split, split, P(), P(), split, P(), P(),
            cube, cube, cube,
        ),
        out_specs=(
            rows, rows, P(), split, split, split, P(), P(), split, P(), P(), cut, cut, cut,
        ),
        check_vma=False,
    )
```

time: 2360 us -> 1100 us (0.47)
  waiting for transfers between devices: 1480 us -> 754 us
  blocking collectives: 419 us -> 41.4 us
  matrix products: 237 us -> 164 us
  local copies, waits for them, and re-layouts: 101 us -> 43.4 us
  other arithmetic: 84 us -> 44.2 us
  Pallas kernels: 0 us -> 24.2 us
    reduce_scatter x9 -> x6, waiting for transfers between devices: 601 us -> 188 us  [the longest x4 188 us: scatter_sum(): return lax.psum_scatter(partial, 'expert', scatter_dimension=0, tiled=True)]
    all_to_all x2 -> x1, waiting for transfers between devices: 361 us -> 0.01 us  [on_device(): lax.all_to_all(grad_projection, 'expert', split_axis=0, concat_axis=0, ti...]
    all_to_all x2 -> x1, blocking collectives: 379 us -> 27.1 us  [on_device(): lax.all_to_all(outgoing, 'expert', split_axis=0, concat_axis=0, tiled=True)]
    unnamed x17 -> x18, waiting for transfers between devices: 2.82 us -> 192 us
    all_gather x6 -> x7, waiting for transfers between devices: 345 us -> 251 us  [the longest x4 141 us: gather_tokens(): return lax.all_gather(rows, 'expert', axis=0, tiled=True)]
    dot_general x43 -> x34, matrix products: 237 us -> 164 us  [the longest x9 69.1 us: dot_last(): lax.dot_general(left, right, (((1,), (1,)), ((), ())), preferred_element_...]
    psum x2 -> x1, waiting for transfers between devices: 176 us -> 122 us  [on_device(): small = lax.psum(small, ('dp', 'expert'))]
    psum x1 -> x0, blocking collectives: 40.1 us -> none  [on_device(): lax.psum((grad_gain_attn, grad_query_gain, grad_key_gain, grad_gain_ffn,...]
  transfers between devices with their start and end apart: 19 -> 18, of which waited for: 17 -> 15; matrix products, arithmetic and copies ran while one was open for 8% -> 13% of each run, Pallas kernels for 0% -> 1%
where the time goes in v1:
time: 1100 us; the launch traced here: 1090 us
  waiting for transfers between devices  754 us (69%)
  matrix products  164 us (15%)
  other arithmetic  44.2 us (4%)
  local copies, waits for them, and re-layouts  43.4 us (4%)
  blocking collectives  41.4 us (4%)
  Pallas kernels  24.2 us (2%)
  between operations  15.4 us (1%)
    unnamed x18, waiting for transfers between devices  192 us
    reduce_scatter x4, waiting for transfers between devices, scatter_sum(): return lax.psum_scatter(partial, 'expert', scatter_dimension=0, tiled=True)  188 us
    all_gather x4, waiting for transfers between devices, gather_tokens(): return lax.all_gather(rows, 'expert', axis=0, tiled=True)  141 us
    psum x1, waiting for transfers between devices, on_device(): small = lax.psum(small, ('dp', 'expert'))  122 us
    dot_general x9, matrix products, dot_last(): lax.dot_general(left, right, (((1,), (1,)), ((), ())), preferred_element_...  69.1 us
    dot_general x10, matrix products, dot(): return jnp.dot(left, right, preferred_element_type=high)  53.9 us
    dot_general x15, matrix products, dot_first(): lax.dot_general(left, right, (((0,), (0,)), ((), ())), preferred_element_...  40.8 us
    all_gather x1, waiting for transfers between devices, on_device(): grad_projection = lax.all_gather(grad_projection, 'dp', axis=1, tiled=True)  38.7 us
  transfers between devices with their start and end apart: 18, of which 15 were waited for; matrix products, arithmetic and copies ran while one was open for 13% of the time, Pallas kernels for 1%

profile of v1, /device:TPU:0, one launch (start us, length us, event | category | flops | bytes accessed | tf_op | source)
XLA Modules:
  0.0 1091.8 jit_solution(15839926927203887695)
XLA Ops:
  10.0 27.1 %all_to_all.10 = bf16[8,64,768]{2,1,0:T(8,128)(2,1)S(1)} all-to-all(bf16[8,64,768]{2,1,0:T(8,128)(2,1)S(1)} %copy.121), channel_id=1, replica_groups=mesh['dp'=4,'expert'=8] {'expert'}, dimensions={0} | all-to-all | bytes 1572864 | tf_op jit(solution)/shard_map/all_to_all | solution.py:261
  43.9 37.6 %all-gather.10.cloned.1.call-done = bf16[8,256,768]{2,0,1:T(8,128)(2,1)} async-done(((bf16[8,64,768]{2,0,1:T(8,128)(2,1)}), bf16[8,256,768]{2,0,1:T(8,128)(2,1)}) %all-gather.10.cloned.1.call-update) | async-done | bytes 3145744 | tf_op jit(solution)/shard_map/all_gather | solution.py:262
  85.7 45.2 %all-gather.8.cloned.1.call-done = bf16[1024,2048]{1,0:T(8,128)(2,1)} async-done(((bf16[128,2048]{1,0:T(8,128)(2,1)}), bf16[1024,2048]{1,0:T(8,128)(2,1)}) %all-gather.8.cloned.1.call-update) | async-done | bytes 4194320 | tf_op jit(solution)/shard_map/all_gather | solution.py:204
  130.9 8.3 fusion.87.query_ref.key_ref.value_ref
  139.4 9.9 shard_map.263
  155.4 48.8 %reduce-scatter.13.cloned.1.call-done = bf16[128,2048]{1,0:T(8,128)(2,1)} async-done(((bf16[1024,2048]{1,0:T(8,128)(2,1)}), bf16[128,2048]{1,0:T(8,128)(2,1)}) %reduce-scatter.13.cloned.1.call-update) | async-done | bytes 524304 | tf_op jit(solution)/shard_map/reduce_scatter | solution.py:208
  208.6 14.3 %all_gather.27 = s32[1024,8]{0,1:T(8,128)S(1)} all-gather(s32[128,8]{0,1:T(8,128)S(1)} %copy-done.34), channel_id=1, replica_groups=mesh['dp'=4,'expert'=8] {'expert'}, dimensions={0}, use_global_device_ids=true | all-gather | bytes 36864 | tf_op jit(solution)/shard_map/all_gather | solution.py:204
  223.0 30.4 %all-gather.12.cloned.1.call-done = bf16[1024,2048]{1,0:T(8,128)(2,1)} async-done(((bf16[128,2048]{1,0:T(8,128)(2,1)}), bf16[1024,2048]{1,0:T(8,128)(2,1)}) %all-gather.12.cloned.1.call-update) | async-done | bytes 4194320 | tf_op jit(solution)/shard_map/all_gather | solution.py:204
  280.6 20.2 %all-gather.14.cloned.1.call-done = bf16[1024,2048]{1,0:T(8,128)(2,1)} async-done(((bf16[128,2048]{1,0:T(8,128)(2,1)}), bf16[1024,2048]{1,0:T(8,128)(2,1)}) %all-gather.14.cloned.1.call-update) | async-done | bytes 4194320 | tf_op jit(solution)/shard_map/all_gather | solution.py:204
  300.8 12.1 %multiply_reduce_fusion = (f32[1024]{0:T(1024)S(1)}, bf16[1024,768]{0,1:T(8,128)(2,1)}, bf16[1024,768]{0,1:T(8,128)(2,1)}, bf16[1024,768]{0,1:T(8,128)(2,1)}) fusion(f32[1024,768]{0,1:T(8,128)} %fusion.4, f32[1024,768]{0,1:T(8,128)} %fusion.8, f32[1024]{0:T(1024)S(1)} %bitcast.183, bf16[1024,2048]{1,0:T(8,128)(2,1)} %all-gather.14.cloned.1.call-done, ...), kind=kOutput, calls=%fused_computation.37 | convolution fusion | flops 3236166656 | bytes 18358272 | tf_op jit(solution)/shard_map/dot_general | solution.py:39
  312.9 8.7 multiply_reduce_fusion.1
  324.6 9.3 fusion.14
  347.4 12.4 %add_convert_fusion = bf16[1024,2048]{1,0:T(8,128)(2,1)} fusion(f32[1024,2048]{1,0:T(8,128)} %fusion.6, f32[1024,2048]{1,0:T(8,128)} %fusion.18, f32[1024,2048]{1,0:T(8,128)} %fusion.14, bf16[1024,768]{0,1:T(8,128)(2,1)S(1)} %copy-done.26, bf16[2,2048,768]{2,1,0:T(8,128)(2,1)} %param.30), kind=kOutput, calls=%fused_computation.1 | convolution fusion | flops 3229614080 | bytes 34078720 | tf_op jit(solution)/shard_map/dot_general | solution.py:39
  360.5 7.8 concatenate.40
  370.7 49.0 %reduce-scatter.17.cloned.1.call-done = bf16[128,2176]{1,0:T(8,128)(2,1)} async-done(((bf16[1024,2176]{1,0:T(8,128)(2,1)}), bf16[128,2176]{1,0:T(8,128)(2,1)}) %reduce-scatter.17.cloned.1.call-update) | async-done | bytes 557072 | tf_op jit(solution)/shard_map/reduce_scatter | solution.py:208
  426.4 45.4 %all-gather.16.cloned.1.call-done = bf16[1024,2048]{1,0:T(8,128)(2,1)} async-done(((bf16[128,2048]{1,0:T(8,128)(2,1)}), bf16[1024,2048]{1,0:T(8,128)(2,1)}) %all-gather.16.cloned.1.call-update) | async-done | bytes 4194320 | tf_op jit(solution)/shard_map/all_gather | solution.py:204
  483.7 14.4 %shard_map.264 = (bf16[1024,512]{1,0:T(8,128)(2,1)}, f32[1024,128]{1,0:T(8,128)S(1)}, f32[1024,128]{1,0:T(8,128)S(1)}, f32[8,128]{1,0:T(8,128)S(1)}) custom-call(f32[1024,768]{1,0:T(8,128)} %fusion.87.query_ref.key_ref.value_ref, bf16[1024,512]{1,0:T(8,128)(2,1)} %get-tuple-element.24.query_low_ref, bf16[1024,128]{1,0:T(8,128)(2,1)S(1)} %get-tuple-element.25.key_low_ref, ...), custom_call_target="tpu_custom_call" | custom-call | flops 3221225472 | bytes 8388608 | tf_op jit(solution)/shard_map/pallas_call | solution.py:178
  577.8 41.1 %reduce-scatter.19.cloned.1.call-done = bf16[128,2048]{1,0:T(8,128)(2,1)} async-done(((bf16[1024,2048]{1,0:T(8,128)(2,1)}), bf16[128,2048]{1,0:T(8,128)(2,1)}) %reduce-scatter.19.cloned.1.call-update) | async-done | bytes 524304 | tf_op jit(solution)/shard_map/reduce_scatter | solution.py:208
  622.4 71.8 %reduce-scatter.27.cloned.1.call-done = bf16[1,1536,512]{2,1,0:T(8,128)(2,1)} async-done(((bf16[4,1536,512]{2,1,0:T(8,128)(2,1)}), bf16[1,1536,512]{2,1,0:T(8,128)(2,1)}) %reduce-scatter.27.cloned.1.call-update) | async-done | bytes 1572880
  697.7 33.6 %all-gather.20.cloned.1.call-done = bf16[512,2048]{1,0:T(8,128)(2,1)} async-done(((bf16[128,2048]{1,0:T(8,128)(2,1)}), bf16[512,2048]{1,0:T(8,128)(2,1)}) %all-gather.20.cloned.1.call-update) | async-done | bytes 2097168 | tf_op jit(solution)/shard_map/all_gather | solution.py:396
  735.5 48.9 %reduce-scatter.15.cloned.1.call-done = bf16[128,2048]{1,0:T(8,128)(2,1)} async-done(((bf16[1024,2048]{1,0:T(8,128)(2,1)}), bf16[128,2048]{1,0:T(8,128)(2,1)}) %reduce-scatter.15.cloned.1.call-update) | async-done | bytes 524304 | tf_op jit(solution)/shard_map/reduce_scatter | solution.py:208
  787.5 119.1 %reduce-scatter.25.cloned.1.call-done = bf16[1,768,2048]{2,1,0:T(8,128)(2,1)} async-done(((bf16[4,768,2048]{2,1,0:T(8,128)(2,1)}), bf16[1,768,2048]{2,1,0:T(8,128)(2,1)}) %reduce-scatter.25.cloned.1.call-update) | async-done | bytes 3145744
  912.4 122.1 %all-reduce.4.cloned.1.call-done = f32[37120]{0:T(1024)} async-done(((f32[37120]{0:T(1024)}), f32[37120]{0:T(1024)}) %all-reduce.4.cloned.1.call-update) | async-done | bytes 148496 | tf_op jit(solution)/shard_map/psum | solution.py:416
  1039.3 38.7 %all-gather.18.cloned.1.call-done = bf16[8,256,640]{2,1,0:T(8,128)(2,1)} async-done(((bf16[8,64,640]{2,1,0:T(8,128)(2,1)}), bf16[8,256,640]{2,1,0:T(8,128)(2,1)}) %all-gather.18.cloned.1.call-update) | async-done | bytes 2621456 | tf_op jit(solution)/shard_map/all_gather | solution.py:388
  (293 shorter events, 200.3 us)
Async XLA Ops:
  7.2 143.7 %copy-start = (bf16[512,2048]{1,0:T(8,128)(2,1)S(1)}, bf16[512,2048]{1,0:T(8,128)(2,1)}, u32[]{:S(2)}) copy-start(bf16[512,2048]{1,0:T(8,128)(2,1)} %param.26) | copy-start | bytes 6291460
  7.2 74.3 %all-gather.10.cloned.1.call-start = ((), (), s32[]{:S(2)}) async-start(), calls=%async_computation.11 | async-start | bytes 3932160 | tf_op jit(solution)/shard_map/all_gather | solution.py:262
  38.5 92.4 %all-gather.8.cloned.1.call-start = ((), (), s32[]{:S(2)}) async-start(), calls=%async_computation.10 | async-start | bytes 4718592 | tf_op jit(solution)/shard_map/all_gather | solution.py:204
  40.8 163.4 %reduce-scatter.13.cloned.1.call-start = ((), (), s32[]{:S(2)}) async-start(), calls=%async_computation.12 | async-start | bytes 4718592 | tf_op jit(solution)/shard_map/reduce_scatter | solution.py:208
  155.3 98.1 %copy-start.28 = (bf16[2048,16]{0,1:T(8,128)(2,1)S(1)}, bf16[2048,16]{0,1:T(8,128)(2,1)}, u32[]{:S(2)}) copy-start(bf16[2048,16]{0,1:T(8,128)(2,1)} %param.28) | copy-start | bytes 196612
  155.3 98.1 %all-gather.12.cloned.1.call-start = ((), (), s32[]{:S(2)}) async-start(), calls=%async_computation.13 | async-start | bytes 4718592 | tf_op jit(solution)/shard_map/all_gather | solution.py:204
  207.9 92.9 %all-gather.14.cloned.1.call-start = ((), (), s32[]{:S(2)}) async-start(), calls=%async_computation.15 | async-start | bytes 4718592 | tf_op jit(solution)/shard_map/all_gather | solution.py:204
  208.5 211.2 %reduce-scatter.17.cloned.1.call-start = ((), (), s32[]{:S(2)}) async-start(), calls=%async_computation.16 | async-start | bytes 5013504 | tf_op jit(solution)/shard_map/reduce_scatter | solution.py:208
  368.3 103.5 %all-gather.16.cloned.1.call-start = ((), (), s32[]{:S(2)}) async-start(), calls=%async_computation.17 | async-start | bytes 4718592 | tf_op jit(solution)/shard_map/all_gather | solution.py:204
  426.4 108.8 %reduce-scatter.23.cloned.1.call-start = ((), (), s32[]{:S(2)}) async-start(), calls=%async_computation.22 | async-start | bytes 2621440 | tf_op jit(solution)/shard_map/reduce_scatter | solution.py:395
  478.1 94.4 %reduce-scatter.21.cloned.1.call-start = ((), (), s32[]{:S(2)}) async-start(), calls=%async_computation.20 | async-start | bytes 3276800 | tf_op jit(solution)/shard_map/reduce_scatter | solution.py:384
  499.3 2.0 collective-permute-start
  511.1 107.9 %reduce-scatter.19.cloned.1.call-start = ((), (), s32[]{:S(2)}) async-start(), calls=%async_computation.18 | async-start | bytes 4718592 | tf_op jit(solution)/shard_map/reduce_scatter | solution.py:208
  519.3 174.8 %reduce-scatter.27.cloned.1.call-start = ((), (), s32[]{:S(2)}) async-start(), calls=%async_computation.25 | async-start | bytes 7864320
  535.1 196.3 %all-gather.20.cloned.1.call-start = ((), (), s32[]{:S(2)}) async-start(), calls=%async_computation.23 | async-start | bytes 2621440 | tf_op jit(solution)/shard_map/all_gather | solution.py:396
  535.7 248.7 %reduce-scatter.15.cloned.1.call-start = ((), (), s32[]{:S(2)}) async-start(), calls=%async_computation.14 | async-start | bytes 4718592 | tf_op jit(solution)/shard_map/reduce_scatter | solution.py:208
  548.7 357.8 %reduce-scatter.25.cloned.1.call-start = ((), (), s32[]{:S(2)}) async-start(), calls=%async_computation.24 | async-start | bytes 15728640
  572.5 49.0 %all-to-all-start.1 = ((bf16[8,64,640]{2,1,0:T(8,128)(2,1)}), bf16[8,64,640]{2,1,0:T(8,128)(2,1)S(1)}, u32[]{:S(2)}, u32[]{:S(2)}) async-start(bf16[8,64,640]{2,1,0:T(8,128)(2,1)} %reduce-scatter.21.cloned.1.call-done), calls=%async_computation.6 | async-start | bytes 1310720 | tf_op jit(solution)/shard_map/all_to_all | solution.py:385
  576.2 458.3 %all-reduce.4.cloned.1.call-start = ((), (), s32[]{:S(2)}) async-start(), calls=%async_computation.19 | async-start | bytes 303104 | tf_op jit(solution)/shard_map/psum | solution.py:416
  621.2 456.9 %all-gather.18.cloned.1.call-start = ((), (), s32[]{:S(2)}) async-start(), calls=%async_computation.21 | async-start | bytes 3276800 | tf_op jit(solution)/shard_map/all_gather | solution.py:388
  697.7 86.7 %copy-start.13 = (bf16[128,2048]{1,0:T(8,128)(2,1)S(1)}, bf16[128,2048]{1,0:T(8,128)(2,1)}, u32[]{:S(2)}) copy-start(bf16[128,2048]{1,0:T(8,128)(2,1)} %reduce-scatter.13.cloned.1.call-done) | copy-start | bytes 1572868
  697.7 86.7 %copy-start.19 = (bf16[128,2048]{1,0:T(8,128)(2,1)S(1)}, bf16[128,2048]{1,0:T(8,128)(2,1)}, u32[]{:S(2)}) copy-start(bf16[128,2048]{1,0:T(8,128)(2,1)} %param.19) | copy-start | bytes 1572868
  697.7 86.7 %copy-start.23 = (f32[128,2048]{1,0:T(8,128)S(1)}, f32[128,2048]{1,0:T(8,128)}, u32[]{:S(2)}) copy-start(f32[128,2048]{1,0:T(8,128)} %copy-done.22) | copy-start | bytes 3145732
  697.7 86.7 %copy-start.42 = (f32[128]{0:T(128)S(1)}, f32[128]{0:T(128)}, u32[]{:S(2)}) copy-start(f32[128]{0:T(128)} %copy-done.41) | copy-start | bytes 1540
  (66 other events, 908.1 us)
Sparse Core Ops, SparseCore 0:
  38.6 42.8 all-gather.9
  83.7 47.1 all-gather.7
  155.4 48.7 reduce-scatter.12
  208.0 45.3 all-gather.11
  254.8 45.8 all-gather.13
  368.5 51.1 reduce-scatter.16
  426.5 45.3 all-gather.15
  478.2 33.9 reduce-scatter.22
  516.0 39.5 reduce-scatter.20
  558.4 60.4 reduce-scatter.18
  622.2 71.8 reduce-scatter.26
  696.0 35.2 all-gather.19
  734.3 49.9 reduce-scatter.14
  787.6 118.8 reduce-scatter.24
  913.4 121.0 all-reduce.3
  1036.4 41.6 all-gather.17

commit v2 on v1

--- a/solution.py
+++ b/solution.py
@@ -2,6 +2,7 @@
 
 import jax
 import jax.numpy as jnp
+import numpy as np
 from jax import lax
 from jax.experimental import pallas as pl
 from jax.experimental.pallas import tpu as pltpu
@@ -200,12 +201,1367 @@
     )
 
 
+MESH = pl.DeviceIdType.MESH
+VMEM = pl.BlockSpec(memory_space=pltpu.VMEM)
+ANY = pl.BlockSpec(memory_space=pl.ANY)
+
+
+def wait_all(copies):
+    for copy in copies:
+        copy.wait()
+
+
+class Chain:
+    def __init__(self):
+        self.n = lax.axis_size("expert") // 2
+        me = lax.axis_index("expert")
+        self.z, self.c = me // 2, me % 2
+        self.sibling, self.up, self.down = me + 1 - 2 * self.c, me + 2, me - 2
+        self.has_up, self.has_down = self.z < self.n - 1, self.z > 0
+
+    def greet(self):
+        barrier = pltpu.get_barrier_semaphore()
+
+        def signal(peer):
+            pl.semaphore_signal(barrier, inc=1, device_id={"expert": peer}, device_id_type=MESH)
+
+        signal(self.sibling)
+        pl.when(self.has_up)(lambda: signal(self.up))
+        pl.when(self.has_down)(lambda: signal(self.down))
+        peers = 1 + self.has_up.astype(jnp.int32) + self.has_down.astype(jnp.int32)
+        pl.semaphore_wait(barrier, peers)
+
+    def nearest(self, step):
+        turn = jnp.int32(0)
+        for z in range(self.n):
+            order = sorted(range(self.n), key=lambda other: (abs(other - z), other))
+            for at, chip in enumerate(order):
+                turn = jnp.where((self.z == z) & (step == at), chip, turn)
+        return turn
+
+
+class Gather:
+    def __init__(self, chain, own, whole, send, recv, local):
+        self.chain, self.own, self.whole = chain, own, whole
+        self.send, self.recv, self.local = send, recv, local
+        self.rows = own.shape[0]
+
+    @staticmethod
+    def semaphores(n):
+        return [
+            pltpu.SemaphoreType.DMA((3, n)),
+            pltpu.SemaphoreType.DMA((2 * n,)),
+            pltpu.SemaphoreType.DMA(()),
+        ]
+
+    def block(self, z, c):
+        return self.whole.at[pl.ds(pl.multiple_of((2 * z + c) * self.rows, self.rows), self.rows)]
+
+    def copy(self, source, z, way, peer):
+        c = self.chain.c
+        return pltpu.make_async_remote_copy(
+            src_ref=source,
+            dst_ref=self.block(z, c),
+            send_sem=self.send.at[way, z],
+            recv_sem=self.recv.at[2 * z + c],
+            device_id={"expert": peer},
+            device_id_type=MESH,
+        )
+
+    def wait_block(self, z, c):
+        block = self.block(z, c)
+        pltpu.make_async_remote_copy(
+            src_ref=block,
+            dst_ref=block,
+            send_sem=self.send.at[0, z],
+            recv_sem=self.recv.at[2 * z + c],
+            device_id={"expert": self.chain.sibling},
+            device_id_type=MESH,
+        ).wait_recv()
+
+    def keep(self):
+        return pltpu.make_async_copy(self.own, self.block(self.chain.z, self.chain.c), self.local)
+
+    def begin(self):
+        ch = self.chain
+        pl.when(ch.has_up)(lambda: self.copy(self.own, ch.z, 0, ch.up).start())
+        pl.when(ch.has_down)(lambda: self.copy(self.own, ch.z, 1, ch.down).start())
+        self.copy(self.own, ch.z, 2, ch.sibling).start()
+        self.keep().start()
+
+    def service(self, step):
+        ch = self.chain
+
+        def from_below():
+            z = ch.z - step
+            self.wait_block(z, ch.c)
+            pl.when(ch.has_up)(lambda: self.copy(self.block(z, ch.c), z, 0, ch.up).start())
+            self.copy(self.block(z, ch.c), z, 2, ch.sibling).start()
+
+        def from_above():
+            z = ch.z + step
+            self.wait_block(z, ch.c)
+            pl.when(ch.has_down)(lambda: self.copy(self.block(z, ch.c), z, 1, ch.down).start())
+            self.copy(self.block(z, ch.c), z, 2, ch.sibling).start()
+
+        pl.when(ch.z - step >= 0)(from_below)
+        pl.when(ch.z + step < ch.n)(from_above)
+
+    def wait_sibling(self, z):
+        self.wait_block(z, 1 - self.chain.c)
+
+    def finish(self):
+        ch = self.chain
+        for z in range(ch.n):
+            at = jnp.int32(z)
+            block = self.block(at, ch.c)
+            pl.when(ch.has_up & (ch.z >= z))(lambda: self.copy(block, at, 0, ch.up).wait_send())
+            pl.when(ch.has_down & (ch.z <= z))(lambda: self.copy(block, at, 1, ch.down).wait_send())
+            self.copy(block, at, 2, ch.sibling).wait_send()
+
+
+class Scatter:
+    def __init__(self, chain, parts, pair, flow, pair_send, pair_recv, flow_send, flow_recv):
+        self.chain, self.parts, self.pair, self.flow = chain, parts, pair, flow
+        self.pair_send, self.pair_recv = pair_send, pair_recv
+        self.flow_send, self.flow_recv = flow_send, flow_recv
+        self.rows = pair.shape[1]
+
+    @staticmethod
+    def buffers(n, rows, width):
+        return [
+            pltpu.VMEM((n, rows, width), low),
+            pltpu.VMEM((n + 1, rows, width), low),
+            pltpu.SemaphoreType.DMA((n,)),
+            pltpu.SemaphoreType.DMA((n,)),
+            pltpu.SemaphoreType.DMA((n,)),
+            pltpu.SemaphoreType.DMA((n + 1,)),
+        ]
+
+    def half(self, z, c):
+        return self.parts.at[z, pl.ds(pl.multiple_of(c * self.rows, self.rows), self.rows)]
+
+    def pair_copy(self, z):
+        ch = self.chain
+        return pltpu.make_async_remote_copy(
+            src_ref=self.half(z, 1 - ch.c),
+            dst_ref=self.pair.at[z],
+            send_sem=self.pair_send.at[z],
+            recv_sem=self.pair_recv.at[z],
+            device_id={"expert": ch.sibling},
+            device_id_type=MESH,
+        )
+
+    def flow_copy(self, z, slot, peer):
+        return pltpu.make_async_remote_copy(
+            src_ref=self.pair.at[z],
+            dst_ref=self.flow.at[slot],
+            send_sem=self.flow_send.at[z],
+            recv_sem=self.flow_recv.at[slot],
+            device_id={"expert": peer},
+            device_id_type=MESH,
+        )
+
+    def wait_flow(self, slot):
+        block = self.flow.at[slot]
+        pltpu.make_async_remote_copy(
+            src_ref=block,
+            dst_ref=block,
+            send_sem=self.flow_send.at[0],
+            recv_sem=self.flow_recv.at[slot],
+            device_id={"expert": self.chain.sibling},
+            device_id_type=MESH,
+        ).wait_recv()
+
+    def start_pair(self, z):
+        self.pair_copy(z).start()
+
+    def add_pair(self, z, relayed):
+        self.pair_copy(z).wait_recv()
+        half = self.half(z, self.chain.c)
+
+        def alone():
+            self.pair[z] = (half[...].astype(high) + self.pair[z].astype(high)).astype(low)
+
+        def with_flow():
+            self.wait_flow(z)
+            total = half[...].astype(high) + self.pair[z].astype(high) + self.flow[z].astype(high)
+            self.pair[z] = total.astype(low)
+
+        pl.when(relayed)(with_flow)
+        pl.when(jnp.logical_not(relayed))(alone)
+
+    def step(self, distance):
+        ch = self.chain
+
+        def upward():
+            z = ch.z + distance
+            self.add_pair(z, ch.has_down)
+            self.flow_copy(z, z, ch.up).start()
+
+        def downward():
+            z = ch.z - distance
+            self.add_pair(z, ch.has_up)
+            self.flow_copy(z, jnp.where(distance == 1, ch.n, z), ch.down).start()
+
+        pl.when(ch.z + distance < ch.n)(upward)
+        pl.when(ch.z - distance >= 0)(downward)
+
+    def total(self, result):
+        ch = self.chain
+        self.pair_copy(ch.z).wait_recv()
+        result[...] = self.half(ch.z, ch.c)[...].astype(high) + self.pair[ch.z].astype(high)
+
+        def add(slot):
+            self.wait_flow(slot)
+            result[...] += self.flow[slot].astype(high)
+
+        pl.when(ch.has_down)(lambda: add(ch.z))
+        pl.when(ch.has_up)(lambda: add(ch.n))
+
+    def finish(self):
+        ch = self.chain
+        for z in range(ch.n):
+            at = jnp.int32(z)
+            self.pair_copy(at).wait_send()
+            pl.when(ch.z != z)(lambda: self.flow_copy(at, at, ch.sibling).wait_send())
+
+
+class Ports:
+    def __init__(self, send, recv):
+        self.send, self.recv, self.used, self.started = send, recv, 0, []
+
+    def copy(self, source, target, device):
+        at = self.used
+        self.used += 1
+        copy = pltpu.make_async_remote_copy(
+            src_ref=source,
+            dst_ref=target,
+            send_sem=self.send.at[at],
+            recv_sem=self.recv.at[at],
+            device_id=device,
+            device_id_type=MESH,
+        )
+        self.started.append(copy)
+        return copy
+
+    def finish(self):
+        for copy in self.started:
+            copy.wait_send()
+
+
+def communicating(collective_id):
+    return pltpu.CompilerParams(
+        collective_id=collective_id, has_side_effects=True, vmem_limit_bytes=60 << 20
+    )
+
+
+def square():
+    group = lax.axis_index("dp")
+    y, x = group // 2, group % 2
+    from_x, from_y = 2 * y + 1 - x, 2 * (1 - y) + x
+    return group, y, x, from_x, from_y
+
+
+def gather_kernel(
+    tokens_ref, gain_ref, named_ref, query_ref, key_ref, value_ref,
+    hidden_ref, all_named_ref, projection_ref, raw_ref,
+    own, stage, wide_send, wide_recv, wide_local, thin_send, thin_recv, thin_local, swap_send, swap_recv,
+    x_send, x_recv, y_send, y_recv, far_send, far_recv,
+):
+    chain = Chain()
+    n = chain.n
+    peers = 2 * n
+    me = lax.axis_index("expert")
+    group, _, _, from_x, from_y = square()
+    far = 3 - group
+    beside, across = {"dp": from_x}, {"dp": from_y}
+    sources = [(2 * chain.nearest(step) + core, core, step) for step in range(n) for core in range(2)]
+    others = [chain.sibling] + [source for source, _, step in sources if step > 0]
+    barrier = pltpu.get_barrier_semaphore()
+    for device in [{"expert": peer} for peer in others] + [beside, across]:
+        pl.semaphore_signal(barrier, inc=1, device_id=device, device_id_type=MESH)
+    rows = stage.shape[1]
+    quarter = pl.ds(pl.multiple_of(group * rows, rows), rows)
+    query_width = query_ref.shape[1] // peers
+    head_size = key_ref.shape[1] // n
+    for peer in range(peers):
+        shared = pl.ds(peer // 2 * head_size, head_size)
+        stage[peer, :, :query_width] = query_ref[quarter, pl.ds(peer * query_width, query_width)]
+        stage[peer, :, query_width : query_width + head_size] = key_ref[quarter, shared]
+        stage[peer, :, query_width + head_size :] = value_ref[quarter, shared]
+    pl.semaphore_wait(barrier, peers + 1)
+
+    def remote(source, target, send, recv, device):
+        return pltpu.make_async_remote_copy(
+            src_ref=source, dst_ref=target, send_sem=send, recv_sem=recv, device_id=device, device_id_type=MESH
+        )
+
+    def block(source, place):
+        return projection_ref.at[source, place]
+
+    swaps = [
+        remote(stage.at[peer], block(me, group), swap_send.at[at], swap_recv.at[me], {"expert": peer})
+        for at, peer in enumerate(others)
+    ]
+    for copy in swaps:
+        copy.start()
+    own[...] = norm_rows(tokens_ref[...].astype(high), gain_ref[...]).astype(low)
+    wide = Gather(chain, own, hidden_ref, wide_send, wide_recv, wide_local)
+    thin = Gather(chain, named_ref, all_named_ref, thin_send, thin_recv, thin_local)
+    wide.begin()
+    thin.begin()
+    projection_ref[me, group] = stage[me]
+
+    def to_x(at, source, place):
+        part = block(source, place)
+        return remote(part, part, x_send.at[at], x_recv.at[source], beside)
+
+    def to_y(at, source, place):
+        part = block(source, place)
+        return remote(part, part, y_send.at[at], y_recv.at[source], across)
+
+    def to_far(at, core, source, place):
+        part = block(source, place)
+        return remote(part, part, far_send.at[at], far_recv.at[source], across if core == 0 else beside)
+
+    def wait_swap(source):
+        part = block(source, group)
+        remote(part, part, swap_send.at[0], swap_recv.at[source], {"expert": chain.sibling}).wait_recv()
+
+    for at, (source, core, step) in enumerate(sources):
+        if step == 0:
+            pl.when(chain.c != core)(lambda: wait_swap(source))
+        else:
+            wait_swap(source)
+        to_x(at, source, group).start()
+        to_y(at, source, group).start()
+        if step > 0 and core == 1:
+            wide.service(step)
+            thin.service(step)
+    for at, (source, core, _) in enumerate(sources):
+        to_x(at, source, from_x).wait_recv()
+        to_y(at, source, from_y).wait_recv()
+        to_far(at, core, source, from_x if core == 0 else from_y).start()
+    for gather in (thin, wide):
+        for z in range(n):
+            gather.wait_sibling(jnp.int32(z))
+        gather.keep().wait()
+    for at, (source, core, _) in enumerate(sources):
+        to_far(at, core, source, far).wait_recv()
+    pair_rows = 2 * own.shape[0]
+    shard_rows = 4 * rows
+
+    @pl.loop(0, n)
+    def each(step):
+        tokens = pl.ds(pl.multiple_of(step * pair_rows, pair_rows), pair_rows)
+        total = jnp.zeros((pair_rows, raw_ref.shape[1]), high)
+        for source in range(peers):
+            weight = projection_ref[source].reshape(shard_rows, raw_ref.shape[1])
+            total = total + dot(hidden_ref[tokens, source * shard_rows : (source + 1) * shard_rows], weight)
+        raw_ref[tokens] = total
+
+    for gather in (thin, wide):
+        gather.finish()
+    for at, (source, core, _) in enumerate(sources):
+        to_x(at, source, group).wait_send()
+        to_y(at, source, group).wait_send()
+        to_far(at, core, source, from_x if core == 0 else from_y).wait_send()
+    for copy in swaps:
+        copy.wait_send()
+
+
+def run_gather(tokens, gain, named, query_weight, key_matrix, value_matrix, peers, groups):
+    length, width = tokens.shape
+    n = peers // 2
+    shard_rows, query_columns = query_weight.shape
+    columns = query_columns // peers + 2 * key_matrix.shape[1] // n
+    rows = shard_rows // groups
+    dma = pltpu.SemaphoreType.DMA
+    hidden, all_named, projection, raw = pl.pallas_call(
+        gather_kernel,
+        out_shape=[
+            jax.ShapeDtypeStruct((length * peers, width), low),
+            jax.ShapeDtypeStruct((length * peers, named.shape[1]), named.dtype),
+            jax.ShapeDtypeStruct((peers, groups, rows, columns), low),
+            jax.ShapeDtypeStruct((length * peers, columns), high),
+        ],
+        in_specs=[VMEM] * 6,
+        out_specs=[VMEM] * 4,
+        scratch_shapes=[
+            pltpu.VMEM((length, width), low),
+            pltpu.VMEM((peers, rows, columns), low),
+            *Gather.semaphores(n),
+            *Gather.semaphores(n),
+            dma((peers - 1,)), dma((peers,)),
+            dma((peers,)), dma((peers,)), dma((peers,)), dma((peers,)), dma((peers,)), dma((peers,)),
+        ],
+        compiler_params=communicating(1),
+        cost_estimate=pl.CostEstimate(flops=0, bytes_accessed=64 << 20, transcendentals=0),
+        name="gather_hidden",
+    )(tokens, gain, named, query_weight, key_matrix, value_matrix)
+    return hidden, all_named, projection.reshape(width, columns), raw
+
+
+def project_kernel(mixed_ref, weight_ref, tokens_ref, gain_ref, resid_ref, ffn_ref, parts, pair, flow, *sems):
+    chain = Chain()
+    scatter = Scatter(chain, parts, pair, flow, *sems)
+    rows = parts.shape[1]
+
+    chain.greet()
+
+    @pl.loop(0, chain.n)
+    def each(step):
+        z = chain.nearest(chain.n - 1 - step)
+        parts[z] = dot(mixed_ref[pl.ds(pl.multiple_of(z * rows, rows), rows)], weight_ref[...]).astype(low)
+        scatter.start_pair(z)
+        pl.when(step < chain.n - 1)(lambda: scatter.step(chain.n - 1 - step))
+
+    scatter.total(resid_ref)
+    resid_ref[...] += tokens_ref[...].astype(high)
+    ffn_ref[...] = norm_rows(resid_ref[...], gain_ref[...]).astype(low)
+    scatter.finish()
+
+
+def run_project(mixed, weight, tokens, gain, peers):
+    length, width = tokens.shape
+    n = peers // 2
+    return pl.pallas_call(
+        project_kernel,
+        out_shape=[
+            jax.ShapeDtypeStruct((length, width), high),
+            jax.ShapeDtypeStruct((length, width), low),
+        ],
+        in_specs=[VMEM] * 4,
+        out_specs=[VMEM] * 2,
+        scratch_shapes=[pltpu.VMEM((n, 2 * length, width), low)] + Scatter.buffers(n, length, width),
+        compiler_params=communicating(2),
+        cost_estimate=pl.CostEstimate(flops=0, bytes_accessed=64 << 20, transcendentals=0),
+        name="project_and_sum",
+    )(mixed, weight, tokens, gain)
+
+
+def expert_block(rows, cots, gate_w, up_w, down_w, gate_col, gated, grad_gate, grad_up, block):
+    hidden = gate_w.shape[1]
+    chunk = hidden // 3 if hidden % 384 == 0 else hidden
+    gate_grad = jnp.zeros_like(gate_col)
+    for begin in range(0, hidden, chunk):
+        units = pl.ds(begin, chunk)
+        gate_pre = dot(rows[...], gate_w[:, units])
+        up_pre = dot(rows[...], up_w[:, units])
+        plain = dot_last(cots[...], down_w[units, :])
+        share = 1.0 / (1.0 + jnp.exp(-gate_pre))
+        silu = gate_pre * share
+        act = silu * up_pre
+        gate_grad = gate_grad + jnp.sum(act * plain, axis=-1, keepdims=True)
+        gated[block, units] = (act * gate_col).astype(low)
+        grad_act = plain * gate_col
+        slope = share + silu * (1.0 - share)
+        grad_gate[block, units] = (grad_act * up_pre * slope).astype(low)
+        grad_up[block, units] = (grad_act * silu).astype(low)
+    return gate_grad
+
+
+def gate_columns(lanes, expert, gate_grad):
+    sent = jnp.where(lanes == expert, gate_grad, 0.0)
+    upper = sent.astype(low).astype(high)
+    lower = (sent - upper).astype(low).astype(high)
+    return upper + pltpu.roll(lower, 64, 1)
+
+
+class Tiles:
+    def __init__(self, grads, stage, sems, gated, grad_gate, grad_up, rows_all, cots):
+        self.grads, self.stage, self.sems = grads, stage, sems
+        self.sources = ((grad_gate, rows_all), (grad_up, rows_all), (gated, cots))
+        self.groups = sems.shape[1]
+        self.hidden = gated.shape[1]
+        self.piece = self.hidden // self.groups
+        self.tile = stage.shape[2]
+
+    def copies(self, kind, at, slot):
+        piece = self.piece
+        made = []
+        for part in range(self.groups):
+            if kind < 2:
+                target = self.grads.at[part, pl.ds(pl.multiple_of((2 * at + kind) * piece, 16), piece)]
+            else:
+                begin = 2 * self.hidden + part * piece
+                target = self.grads.at[at, pl.ds(begin, piece)]
+            source = self.stage.at[slot, pl.ds(part * piece, piece)]
+            made.append(pltpu.make_async_copy(source, target, self.sems.at[slot, part]))
+        return made
+
+    def run(self, kind):
+        left, right = self.sources[kind]
+
+        @pl.loop(0, self.groups)
+        def each(at):
+            slot = at % 2
+            if kind == 0:
+                pl.when(at >= 2)(lambda: wait_all(self.copies(kind, at, slot)))
+            else:
+                wait_all(self.copies(kind, at, slot))
+            span = pl.ds(pl.multiple_of(at * self.tile, self.tile), self.tile)
+            self.stage[slot] = dot_first(left[...], right[:, span]).astype(low)
+            for copy in self.copies(kind, at, slot):
+                copy.start()
+
+    def finish(self):
+        for slot in range(2):
+            wait_all(self.copies(0, jnp.int32(slot), slot))
+
+
+def first_expert_kernel(
+    ffn_ref, named_ref, router_ref, cot_hbm, gate_hbm, up_hbm, down_hbm,
+    gates_ref, own_gates_ref, rows_hbm, mixture_hbm, parts_hbm, grads_hbm,
+    rows_all, cots, gate_w, up_w, down_w, gated, grad_gate, grad_up, mix_stage, part_stage, tile_stage,
+    load_sems, rows_sem, mix_sems, part_sems, tile_sems, gather_send, gather_recv, gather_local,
+):
+    chain = Chain()
+    n = chain.n
+    length, width = ffn_ref.shape
+    pair_rows = 2 * length
+    loads = [
+        pltpu.make_async_copy(source, target, load_sems.at[at])
+        for at, (source, target) in enumerate(
+            ((gate_hbm.at[0], gate_w), (up_hbm.at[0], up_w), (cot_hbm, cots), (down_hbm.at[0], down_w))
+        )
+    ]
+    for load in loads:
+        load.start()
+    chain.greet()
+    gather = Gather(chain, ffn_ref, rows_all, gather_send, gather_recv, gather_local)
+    gather.begin()
+    gather.keep().wait()
+    for load in loads:
+        load.wait()
+    lanes = lax.broadcasted_iota(jnp.int32, (pair_rows, 128), 1)
+    expert = lax.axis_index("expert") * gate_hbm.shape[0]
+    tile = tile_stage.shape[2]
+
+    def mix_copy(z, slot):
+        target = mixture_hbm.at[pl.ds(pl.multiple_of(z * pair_rows, pair_rows), pair_rows)]
+        return pltpu.make_async_copy(mix_stage.at[slot], target, mix_sems.at[slot])
+
+    def part_copy(z, slot):
+        return pltpu.make_async_copy(part_stage.at[slot], parts_hbm.at[z], part_sems.at[slot])
+
+    @pl.loop(0, n)
+    def each(step):
+        pl.when(step > 0)(lambda: gather.service(step))
+        z = chain.nearest(step)
+        gather.wait_sibling(z)
+        block = pl.ds(pl.multiple_of(z * pair_rows, pair_rows), pair_rows)
+        rows = rows_all.at[block]
+        logits = dot_last(rows[...], router_ref[...])
+        named = named_ref[block].astype(high) > 0.5
+        top = jnp.max(jnp.where(named, logits, -1e30), axis=-1, keepdims=True)
+        terms = jnp.where(named, jnp.exp(jnp.where(named, logits - top, 0.0)), 0.0)
+        gates = terms / jnp.sum(terms, axis=-1, keepdims=True)
+        gates_ref[block] = gates
+
+        @pl.when(step == 0)
+        def own_gates():
+            own_gates_ref[...] = jnp.where(chain.c == 0, gates[:length], gates[length:])
+
+        gate_col = jnp.sum(jnp.where(lanes == expert, gates, 0.0), axis=-1, keepdims=True)
+        gate_grad = expert_block(
+            rows, cots.at[block], gate_w, up_w, down_w, gate_col, gated, grad_gate, grad_up, block
+        )
+        slot = step % 2
+
+        @pl.when(step >= 2)
+        def free():
+            mix_copy(z, slot).wait()
+            part_copy(z, slot).wait()
+
+        @pl.loop(0, width // tile)
+        def columns(at):
+            span = pl.ds(pl.multiple_of(at * tile, tile), tile)
+            mix_stage[slot, :, span] = dot(gated[block], down_w[:, span]).astype(low)
+            grad_rows = dot_last(grad_gate[block], gate_w[span, :]) + dot_last(grad_up[block], up_w[span, :])
+            part_stage[slot, :, span] = grad_rows.astype(low)
+
+        part_stage[slot, :, width:] = gate_columns(lanes, expert, gate_grad).astype(low)
+        mix_copy(z, slot).start()
+        part_copy(z, slot).start()
+
+    rows_copy = pltpu.make_async_copy(rows_all, rows_hbm, rows_sem)
+    rows_copy.start()
+    tiles = Tiles(grads_hbm, tile_stage, tile_sems, gated, grad_gate, grad_up, rows_all, cots)
+    for kind in range(3):
+        tiles.run(kind)
+    gather.finish()
+    tiles.finish()
+    for slot in range(2):
+        mix_copy(jnp.int32(0), slot).wait()
+        part_copy(jnp.int32(0), slot).wait()
+    rows_copy.wait()
+
+
+def second_expert_kernel(
+    gates_ref, rows_hbm, cot_hbm, gate_hbm, up_hbm, down_hbm, mixture_in, parts_in,
+    sum_ref, mixture_hbm, grads_hbm,
+    rows_all, cots, gate_w, up_w, down_w, gated, grad_gate, grad_up, mixture, parts, tile_stage,
+    load_sems, mix_sems, tile_sems, pair, flow, *scatter_sems,
+):
+    chain = Chain()
+    n = chain.n
+    pair_rows, width = parts.shape[1], rows_all.shape[1]
+    loads = [
+        pltpu.make_async_copy(source, target, load_sems.at[at])
+        for at, (source, target) in enumerate(
+            (
+                (rows_hbm, rows_all), (gate_hbm.at[1], gate_w), (up_hbm.at[1], up_w), (cot_hbm, cots),
+                (down_hbm.at[1], down_w), (parts_in, parts), (mixture_in, mixture),
+            )
+        )
+    ]
+    for load in loads:
+        load.start()
+    chain.greet()
+    scatter = Scatter(chain, parts, pair, flow, *scatter_sems)
+    lanes = lax.broadcasted_iota(jnp.int32, (pair_rows, 128), 1)
+    expert = lax.axis_index("expert") * gate_hbm.shape[0] + 1
+    tile = tile_stage.shape[2]
+    for load in loads:
+        load.wait()
+
+    def mix_copy(z):
+        block = pl.ds(pl.multiple_of(z * pair_rows, pair_rows), pair_rows)
+        return pltpu.make_async_copy(mixture.at[block], mixture_hbm.at[block], mix_sems.at[z])
+
+    @pl.loop(0, n)
+    def each(step):
+        z = chain.nearest(n - 1 - step)
+        block = pl.ds(pl.multiple_of(z * pair_rows, pair_rows), pair_rows)
+        gate_col = jnp.sum(jnp.where(lanes == expert, gates_ref[block], 0.0), axis=-1, keepdims=True)
+        gate_grad = expert_block(
+            rows_all.at[block], cots.at[block], gate_w, up_w, down_w, gate_col, gated, grad_gate, grad_up, block
+        )
+
+        @pl.loop(0, width // tile)
+        def columns(at):
+            span = pl.ds(pl.multiple_of(at * tile, tile), tile)
+            grad_rows = dot_last(grad_gate[block], gate_w[span, :]) + dot_last(grad_up[block], up_w[span, :])
+            parts[z, :, span] = (parts[z, :, span].astype(high) + grad_rows).astype(low)
+
+        columns_sent = gate_columns(lanes, expert, gate_grad)
+        parts[z, :, width:] = (parts[z, :, width:].astype(high) + columns_sent).astype(low)
+        scatter.start_pair(z)
+
+        @pl.loop(0, width // tile)
+        def mixture_columns(at):
+            span = pl.ds(pl.multiple_of(at * tile, tile), tile)
+            added = dot(gated[block], down_w[:, span])
+            mixture[block, span] = (mixture[block, span].astype(high) + added).astype(low)
+
+        mix_copy(z).start()
+        pl.when(step < n - 1)(lambda: scatter.step(n - 1 - step))
+
+    tiles = Tiles(grads_hbm, tile_stage, tile_sems, gated, grad_gate, grad_up, rows_all, cots)
+    for kind in range(3):
+        tiles.run(kind)
+    scatter.total(sum_ref)
+    tiles.finish()
+    for z in range(n):
+        mix_copy(jnp.int32(z)).wait()
+    scatter.finish()
+
+
+def run_experts(ffn, named, router, cotangents, gate_weight, up_weight, down_weight, peers, groups):
+    length, width = ffn.shape
+    n = peers // 2
+    full = length * peers
+    _, _, hidden = gate_weight.shape
+    tile = width // groups
+    sent = width + 128
+    dma = pltpu.SemaphoreType.DMA
+    rows = pltpu.VMEM((full, width), low)
+    weights = [
+        pltpu.VMEM(gate_weight.shape[1:], low),
+        pltpu.VMEM(up_weight.shape[1:], low),
+        pltpu.VMEM(down_weight.shape[1:], low),
+    ]
+    acts = [pltpu.VMEM((full, hidden), low)] * 3
+    grads_shape = jax.ShapeDtypeStruct((groups, 3 * hidden, tile), low)
+    mixture_shape = jax.ShapeDtypeStruct((full, width), low)
+    stage = pltpu.VMEM((2, hidden, tile), low)
+    gates, own_gates, rows_all, mixture, parts, grads = pl.pallas_call(
+        first_expert_kernel,
+        out_shape=[
+            jax.ShapeDtypeStruct((full, 128), high),
+            jax.ShapeDtypeStruct((length, 128), high),
+            jax.ShapeDtypeStruct((full, width), low),
+            mixture_shape,
+            jax.ShapeDtypeStruct((n, 2 * length, sent), low),
+            grads_shape,
+        ],
+        in_specs=[VMEM, VMEM, VMEM, ANY, ANY, ANY, ANY],
+        out_specs=[VMEM, VMEM, ANY, ANY, ANY, ANY],
+        scratch_shapes=[
+            rows, rows, *weights, *acts,
+            pltpu.VMEM((2, 2 * length, width), low),
+            pltpu.VMEM((2, 2 * length, sent), low),
+            stage,
+            dma((4,)), dma(()), dma((2,)), dma((2,)), dma((2, groups)),
+            *Gather.semaphores(n),
+        ],
+        compiler_params=communicating(3),
+        cost_estimate=pl.CostEstimate(flops=0, bytes_accessed=120 << 20, transcendentals=0),
+        name="first_expert",
+    )(ffn, named, router, cotangents, gate_weight, up_weight, down_weight)
+    sums, mixture, more_grads = pl.pallas_call(
+        second_expert_kernel,
+        out_shape=[jax.ShapeDtypeStruct((length, sent), high), mixture_shape, grads_shape],
+        in_specs=[VMEM] + [ANY] * 7,
+        out_specs=[VMEM, ANY, ANY],
+        scratch_shapes=[
+            rows, rows, *weights, *acts,
+            rows,
+            pltpu.VMEM((n, 2 * length, sent), low),
+            stage,
+            dma((7,)), dma((n,)), dma((2, groups)),
+            *Scatter.buffers(n, length, sent),
+        ],
+        compiler_params=communicating(7),
+        cost_estimate=pl.CostEstimate(flops=0, bytes_accessed=120 << 20, transcendentals=0),
+        name="second_expert",
+    )(gates, rows_all, cotangents, gate_weight, up_weight, down_weight, mixture, parts)
+    return sums, own_gates, mixture, grads, more_grads
+
+
+def turn_kernel(
+    sum_ref, gates_ref, ffn_ref, resid_ref, cot_ref, gain_ref, router_ref, weight_ref,
+    grad_resid_ref, attn_ref, mixed_ref, router_grad_ref, gain_grad_ref,
+    own, gather_send, gather_recv, gather_local,
+):
+    chain = Chain()
+    n = chain.n
+    length, width = ffn_ref.shape
+    sent = sum_ref[:, width:]
+    grad_gates = jnp.where(
+        lax.broadcasted_iota(jnp.int32, sent.shape, 1) < 64, sent + pltpu.roll(sent, 64, 1), 0.0
+    )
+    gates = gates_ref[...]
+    inner = jnp.sum(gates * grad_gates, axis=-1, keepdims=True)
+    grad_logits = (gates * (grad_gates - inner)).astype(low)
+    router_grad_ref[...] = dot_first(grad_logits, ffn_ref[...])[: router_grad_ref.shape[0]]
+    grad_hidden = sum_ref[:, :width] + dot(grad_logits, router_ref[...])
+    grad_rows, gain_rows = norm_back(resid_ref[...], gain_ref[...], grad_hidden)
+    gain_grad_ref[...] = jnp.broadcast_to(jnp.sum(gain_rows, axis=0, keepdims=True), gain_grad_ref.shape)
+    grad_resid = cot_ref[...].astype(high) + grad_rows
+    grad_resid_ref[...] = grad_resid
+    own[...] = grad_resid.astype(low)
+    chain.greet()
+    gather = Gather(chain, own, attn_ref, gather_send, gather_recv, gather_local)
+    gather.begin()
+    gather.keep().wait()
+    pair_rows = 2 * length
+
+    @pl.loop(0, n)
+    def each(step):
+        pl.when(step > 0)(lambda: gather.service(step))
+        z = chain.nearest(step)
+        gather.wait_sibling(z)
+        block = pl.ds(pl.multiple_of(z * pair_rows, pair_rows), pair_rows)
+        mixed_ref[block] = dot_last(attn_ref[block], weight_ref[...]).astype(low)
+
+    gather.finish()
+
+
+def run_turn(sums, gates, ffn, resid, cotangent, gain, router, weight, experts, peers):
+    length, width = ffn.shape
+    n = peers // 2
+    full = length * peers
+    return pl.pallas_call(
+        turn_kernel,
+        out_shape=[
+            jax.ShapeDtypeStruct((length, width), high),
+            jax.ShapeDtypeStruct((full, width), low),
+            jax.ShapeDtypeStruct((full, weight.shape[0]), low),
+            jax.ShapeDtypeStruct((experts, width), high),
+            jax.ShapeDtypeStruct((8, width), high),
+        ],
+        in_specs=[VMEM] * 8,
+        out_specs=[VMEM] * 5,
+        scratch_shapes=[pltpu.VMEM((length, width), low), *Gather.semaphores(n)],
+        compiler_params=communicating(4),
+        cost_estimate=pl.CostEstimate(flops=0, bytes_accessed=64 << 20, transcendentals=0),
+        name="turn_to_attention",
+    )(sums, gates, ffn, resid, cotangent, gain, router, weight)
+
+
+def input_kernel(
+    key_part_ref, value_part_ref, raw_ref, key_gain_ref, cos_ref, sin_ref, grad_query_ref, projection_ref,
+    hidden_ref, mixed_ref, attn_ref, grad_resid_ref, tokens_ref, gain_ref,
+    input_grad_ref, projection_grad_ref, out_grad_ref, gain_grad_ref, key_gain_grad_ref,
+    own_pair, their_pair, columns, weight, total, parts, hidden_all, mixed_all, attn_all, load_sems,
+    swap_send, swap_recv, pair, flow, *scatter_sems,
+):
+    chain = Chain()
+    n = chain.n
+    loads = [
+        pltpu.make_async_copy(source, target, load_sems.at[at])
+        for at, (source, target) in enumerate(
+            ((mixed_ref, mixed_all), (attn_ref, attn_all), (hidden_ref, hidden_all))
+        )
+    ]
+    for load in loads:
+        load.start()
+    full, head_size = key_part_ref.shape
+    query_width = grad_query_ref.shape[1]
+    own_pair[:, :head_size] = key_part_ref[...].astype(low)
+    own_pair[:, head_size:] = value_part_ref[...].astype(low)
+    chain.greet()
+    swap = pltpu.make_async_remote_copy(
+        src_ref=own_pair,
+        dst_ref=their_pair,
+        send_sem=swap_send,
+        recv_sem=swap_recv,
+        device_id={"expert": chain.sibling},
+        device_id_type=MESH,
+    )
+    swap.start()
+    first = chain.c == 0
+    weight[:, :query_width] = projection_ref[:, :query_width]
+    weight[:, query_width:] = jnp.where(
+        first,
+        projection_ref[:, query_width : query_width + head_size],
+        projection_ref[:, query_width + head_size :],
+    )
+    columns[:, :query_width] = grad_query_ref[...]
+    swap.wait_recv()
+    grad_key = key_part_ref[...] + their_pair[:, :head_size].astype(high)
+    grad_value = value_part_ref[...] + their_pair[:, head_size:].astype(high)
+    grad_key, gain_rows = norm_back(
+        raw_ref[...], key_gain_ref[...], unrotate(grad_key, cos_ref[...], sin_ref[...])
+    )
+    columns[:, query_width:] = jnp.where(first, grad_key, grad_value).astype(low)
+    key_gain = jnp.where(first, jnp.sum(gain_rows, axis=0, keepdims=True), 0.0)
+    key_gain_grad_ref[...] = jnp.broadcast_to(key_gain, key_gain_grad_ref.shape)
+    scatter = Scatter(chain, parts, pair, flow, *scatter_sems)
+    pair_rows = parts.shape[1]
+
+    for load in loads:
+        load.wait()
+    projection_tile = projection_grad_ref.shape[0] // n
+    out_tile = out_grad_ref.shape[1] // n
+
+    @pl.loop(0, n)
+    def each(step):
+        z = chain.nearest(n - 1 - step)
+        rows = pl.ds(pl.multiple_of(z * pair_rows, pair_rows), pair_rows)
+        parts[z] = dot_last(columns[rows], weight[...]).astype(low)
+        scatter.start_pair(z)
+        pl.when(step < n - 1)(lambda: scatter.step(n - 1 - step))
+        span = pl.ds(pl.multiple_of(step * projection_tile, projection_tile), projection_tile)
+        projection_grad_ref[span] = dot_first(hidden_all[:, span], columns[...]).astype(low)
+        span = pl.ds(pl.multiple_of(step * out_tile, out_tile), out_tile)
+        out_grad_ref[:, span] = dot_first(mixed_all[...], attn_all[:, span]).astype(low)
+
+    scatter.total(total)
+    grad_rows, gain_rows = norm_back(tokens_ref[...].astype(high), gain_ref[...], total[...])
+    input_grad_ref[...] = grad_resid_ref[...] + grad_rows
+    gain_grad_ref[...] = jnp.broadcast_to(jnp.sum(gain_rows, axis=0, keepdims=True), gain_grad_ref.shape)
+    swap.wait_send()
+    scatter.finish()
+
+
+def run_input(
+    key_part, value_part, key_raw, key_gain, cosines, sines, grad_query, projection, hidden, mixed, grad_attn,
+    grad_resid, tokens, gain, peers,
+):
+    length, width = tokens.shape
+    n = peers // 2
+    full, head_size = key_part.shape
+    query_width = grad_query.shape[1]
+    return pl.pallas_call(
+        input_kernel,
+        out_shape=[
+            jax.ShapeDtypeStruct((length, width), high),
+            jax.ShapeDtypeStruct((width, query_width + head_size), low),
+            jax.ShapeDtypeStruct((query_width, width), low),
+            jax.ShapeDtypeStruct((8, width), high),
+            jax.ShapeDtypeStruct((8, head_size), high),
+        ],
+        in_specs=[VMEM] * 8 + [ANY] * 3 + [VMEM] * 3,
+        out_specs=[VMEM] * 5,
+        scratch_shapes=[
+            pltpu.VMEM((full, 2 * head_size), low),
+            pltpu.VMEM((full, 2 * head_size), low),
+            pltpu.VMEM((full, query_width + head_size), low),
+            pltpu.VMEM((width, query_width + head_size), low),
+            pltpu.VMEM((length, width), high),
+            pltpu.VMEM((n, 2 * length, width), low),
+            pltpu.VMEM(hidden.shape, low),
+            pltpu.VMEM(mixed.shape, low),
+            pltpu.VMEM(grad_attn.shape, low),
+            pltpu.SemaphoreType.DMA((3,)),
+            pltpu.SemaphoreType.DMA(()),
+            pltpu.SemaphoreType.DMA(()),
+            *Scatter.buffers(n, length, width),
+        ],
+        compiler_params=communicating(5),
+        cost_estimate=pl.CostEstimate(flops=0, bytes_accessed=64 << 20, transcendentals=0),
+        name="input_gradient",
+    )(
+        key_part, value_part, key_raw, key_gain, cosines, sines, grad_query, projection, hidden, mixed,
+        grad_attn, grad_resid, tokens, gain,
+    )
+def weights_kernel(
+    proj_ref, out_ref, attn_gain_ref, ffn_gain_ref, query_gain_ref, key_gain_ref, router_ref, resid_ref,
+    mixture_ref,
+    query_grad_ref, key_grad_ref, value_grad_ref, out_grad_ref, small_out_ref, output_ref,
+    all_proj, first_a, first_b, out_first_a, out_first_b, second_a, second_b, out_second_a, out_second_b,
+    send_a, send_b, out_send_a, out_send_b, quarter, small, got, part, small_sum, total_mixture,
+    port_send, port_recv, swap_send, swap_recv, send_1, recv_1, send_2, recv_2, send_3, recv_3,
+    pair, flow, *scatter_sems,
+):
+    peers = lax.axis_size("expert")
+    me = lax.axis_index("expert")
+    group, y, x, from_x, from_y = square()
+    beside, across = {"dp": from_x}, {"dp": from_y}
+    chain = Chain()
+    scatter = Scatter(chain, mixture_ref, pair, flow, *scatter_sems)
+    width = out_ref.shape[1]
+    head_size = query_gain_ref.shape[1]
+    small[...] = jnp.zeros_like(small)
+    small[0:1] = attn_gain_ref[0:1]
+    small[1:2] = ffn_gain_ref[0:1]
+    small[2:3, :head_size] = query_gain_ref[0:1]
+    small[3:4, :head_size] = key_gain_ref[0:1]
+    small[8:] = router_ref[...]
+    piece = width // peers
+
+    def small_piece(ref, peer):
+        return ref.at[:, pl.ds(pl.multiple_of(peer * piece, piece), piece)]
+
+    barrier = pltpu.get_barrier_semaphore()
+    others = [(me + shift) % peers for shift in range(1, peers)]
+    groups = [(group + shift) % 4 for shift in range(1, 4)]
+    for peer in others:
+        pl.semaphore_signal(barrier, inc=1, device_id={"expert": peer}, device_id_type=MESH)
+    for other in groups:
+        pl.semaphore_signal(barrier, inc=1, device_id={"dp": other}, device_id_type=MESH)
+    pl.semaphore_wait(barrier, peers + 2)
+
+    shard_rows, columns = proj_ref.shape[1:]
+    rows, half = shard_rows // 4, peers // 2
+    out_rows = out_ref.shape[0] // 4
+    middle = width // 2
+    ports = Ports(port_send, port_recv)
+
+    def proj_part(side, q):
+        return proj_ref.at[pl.ds(side * half, half), pl.ds(pl.multiple_of(q * rows, rows), rows)]
+
+    def out_part(ref, side, q):
+        return ref.at[pl.ds(pl.multiple_of(q * out_rows, out_rows), out_rows), pl.ds(side * middle, middle)]
+
+    def remote(source, target, send, recv, device):
+        return pltpu.make_async_remote_copy(
+            src_ref=source, dst_ref=target, send_sem=send, recv_sem=recv, device_id=device, device_id_type=MESH
+        )
+
+    along_x = [2 * other + 1 - x for other in range(2)]
+    along_y = [2 * (1 - y) + other for other in range(2)]
+    out_1a = [ports.copy(out_part(out_ref, 0, along_x[k]), out_first_a.at[k], beside) for k in range(2)]
+    out_1b = [ports.copy(out_part(out_ref, 1, along_y[k]), out_first_b.at[k], across) for k in range(2)]
+    proj_1a = [ports.copy(proj_part(0, along_x[k]), first_a.at[k], beside) for k in range(2)]
+    proj_1b = [ports.copy(proj_part(1, along_y[k]), first_b.at[k], across) for k in range(2)]
+    for copy in out_1a + out_1b + proj_1a + proj_1b:
+        copy.start()
+
+    small_1 = [
+        remote(small_piece(small, peer), got.at[me], send_1.at[at], recv_1.at[me], {"expert": peer})
+        for at, peer in enumerate(others)
+    ]
+    for copy in small_1:
+        copy.start()
+    got[me] = small_piece(small, me)[...]
+    for z in range(chain.n):
+        scatter.start_pair(jnp.int32(z))
+
+    own = group
+    for copy in out_1a + out_1b:
+        copy.wait_recv()
+    for_y, for_x = 2 * (1 - y) + x, 2 * y + 1 - x
+    out_send_a[...] = (
+        out_part(out_ref, 0, for_y)[...].astype(high) + out_first_a[1 - y].astype(high)
+    ).astype(low)
+    out_send_b[...] = (
+        out_part(out_ref, 1, for_x)[...].astype(high) + out_first_b[1 - x].astype(high)
+    ).astype(low)
+    out_2a = ports.copy(out_send_a, out_second_a, across)
+    out_2b = ports.copy(out_send_b, out_second_b, beside)
+    out_2a.start()
+    out_2b.start()
+    scatter.step(3) if chain.n > 3 else None
+    for copy in proj_1a + proj_1b:
+        copy.wait_recv()
+    send_a[...] = (proj_part(0, for_y)[...].astype(high) + first_a[1 - y].astype(high)).astype(low)
+    send_b[...] = (proj_part(1, for_x)[...].astype(high) + first_b[1 - x].astype(high)).astype(low)
+    proj_2a = ports.copy(send_a, second_a, across)
+    proj_2b = ports.copy(send_b, second_b, beside)
+    proj_2a.start()
+    proj_2b.start()
+    scatter.step(2) if chain.n > 2 else None
+
+    for at, peer in enumerate(others):
+        remote(got.at[peer], got.at[peer], send_1.at[at], recv_1.at[peer], {"expert": peer}).wait_recv()
+    total = got[0]
+    for at in range(1, peers):
+        total = total + got[at]
+    part[group] = total
+    small_2 = [
+        remote(part.at[group], part.at[group], send_2.at[at], recv_2.at[group], {"dp": other})
+        for at, other in enumerate(groups)
+    ]
+    for copy in small_2:
+        copy.start()
+
+    out_2a.wait_recv()
+    out_2b.wait_recv()
+    for side, first, second, at in ((0, out_first_a, out_second_a, y), (1, out_first_b, out_second_b, x)):
+        out_part(out_grad_ref, side, own)[...] = (
+            out_part(out_ref, side, own)[...].astype(high) + first[at].astype(high) + second[...].astype(high)
+        ).astype(low)
+
+    def out_quarter(q):
+        return out_grad_ref.at[pl.ds(pl.multiple_of(q * out_rows, out_rows), out_rows)]
+
+    out_gx = ports.copy(out_quarter(own), out_quarter(own), beside)
+    out_gy = ports.copy(out_quarter(own), out_quarter(own), across)
+
+    proj_2a.wait_recv()
+    proj_2b.wait_recv()
+    for side, first, second, at in ((0, first_a, second_a, y), (1, first_b, second_b, x)):
+        quarter[pl.ds(side * half, half)] = (
+            proj_part(side, own)[...].astype(high) + first[at].astype(high) + second[...].astype(high)
+        ).astype(low)
+    swaps = [
+        remote(quarter.at[peer], all_proj.at[own, me], swap_send.at[at], swap_recv.at[me], {"expert": peer})
+        for at, peer in enumerate(others)
+    ]
+    for copy in swaps:
+        copy.start()
+    out_gx.start()
+    out_gy.start()
+    all_proj[own, me] = quarter[me]
+
+    for at, other in enumerate(groups):
+        remote(part.at[other], part.at[other], send_2.at[at], recv_2.at[other], {"dp": other}).wait_recv()
+    total = part[0]
+    for at in range(1, 4):
+        total = total + part[at]
+    small_sum[me] = total
+    small_3 = [
+        remote(small_sum.at[me], small_sum.at[me], send_3.at[at], recv_3.at[me], {"expert": peer})
+        for at, peer in enumerate(others)
+    ]
+    for copy in small_3:
+        copy.start()
+
+    for at, peer in enumerate(others):
+        block = all_proj.at[own, peer]
+        remote(block, block, swap_send.at[at], swap_recv.at[peer], {"expert": peer}).wait_recv()
+    proj_gx = ports.copy(all_proj.at[own], all_proj.at[own], beside)
+    proj_gy = ports.copy(all_proj.at[own], all_proj.at[own], across)
+    proj_gx.start()
+    proj_gy.start()
+    out_gx.wait_recv()
+    out_gy.wait_recv()
+    far = 3 - group
+    out_fa = ports.copy(out_part(out_grad_ref, 0, from_x), out_part(out_grad_ref, 0, from_x), across)
+    out_fb = ports.copy(out_part(out_grad_ref, 1, from_y), out_part(out_grad_ref, 1, from_y), beside)
+    out_fa.start()
+    out_fb.start()
+    scatter.step(1) if chain.n > 1 else None
+
+    def proj_half(q, side):
+        return all_proj.at[q, pl.ds(side * half, half)]
+
+    proj_gx.wait_recv()
+    proj_gy.wait_recv()
+    proj_fa = ports.copy(proj_half(from_x, 0), proj_half(from_x, 0), across)
+    proj_fb = ports.copy(proj_half(from_y, 1), proj_half(from_y, 1), beside)
+    proj_fa.start()
+    proj_fb.start()
+    query_width = columns - head_size
+
+    def spread(q):
+        block = pl.ds(pl.multiple_of(q * rows, rows), rows)
+        for peer in range(peers):
+            query_grad_ref[block, peer * query_width : (peer + 1) * query_width] = all_proj[q, peer, :, :query_width]
+            shared = key_grad_ref if peer % 2 == 0 else value_grad_ref
+            at = peer // 2 * head_size
+            shared[block, at : at + head_size] = all_proj[q, peer, :, query_width:]
+
+    spread(own)
+    spread(from_x)
+    spread(from_y)
+    for at, peer in enumerate(others):
+        block = small_sum.at[peer]
+        remote(block, block, send_3.at[at], recv_3.at[peer], {"expert": peer}).wait_recv()
+    for peer in range(peers):
+        small_out_ref[:, peer * piece : (peer + 1) * piece] = small_sum[peer]
+    scatter.total(total_mixture)
+    output_ref[...] = (resid_ref[...] + total_mixture[...]).astype(low)
+    out_fa.wait_recv()
+    out_fb.wait_recv()
+    proj_fa.wait_recv()
+    proj_fb.wait_recv()
+    spread(far)
+    ports.finish()
+    scatter.finish()
+    for copy in small_1 + small_2 + small_3 + swaps:
+        copy.wait_send()
+
+
+def run_weights(
+    grad_projection, grad_out, attn_gain, ffn_gain, query_gain, key_gain, router, resid, mixture, peers, kv_heads
+):
+    width, columns = grad_projection.shape
+    head_size = query_gain.shape[1]
+    length = resid.shape[0]
+    n = peers // 2
+    shard_rows = width // peers
+    rows, half = shard_rows // 4, peers // 2
+    out_rows, middle = grad_out.shape[0] // 4, grad_out.shape[1] // 2
+    small_rows = 8 + router.shape[0]
+    piece = (small_rows, width // peers)
+    dma = pltpu.SemaphoreType.DMA
+    kv_width = kv_heads * head_size
+    query_width = columns - head_size
+
+    def low_buffer(*shape):
+        return pltpu.VMEM(shape, low)
+
+    return pl.pallas_call(
+        weights_kernel,
+        out_shape=[
+            jax.ShapeDtypeStruct((shard_rows, peers * query_width), low),
+            jax.ShapeDtypeStruct((shard_rows, kv_width), low),
+            jax.ShapeDtypeStruct((shard_rows, kv_width), low),
+            jax.ShapeDtypeStruct(grad_out.shape, low),
+            jax.ShapeDtypeStruct((small_rows, width), high),
+            jax.ShapeDtypeStruct((length, width), low),
+        ],
+        in_specs=[VMEM] * 9,
+        out_specs=[VMEM] * 6,
+        scratch_shapes=[
+            low_buffer(4, peers, rows, columns),
+            low_buffer(2, half, rows, columns),
+            low_buffer(2, half, rows, columns),
+            low_buffer(2, out_rows, middle),
+            low_buffer(2, out_rows, middle),
+            low_buffer(half, rows, columns),
+            low_buffer(half, rows, columns),
+            low_buffer(out_rows, middle),
+            low_buffer(out_rows, middle),
+            low_buffer(half, rows, columns),
+            low_buffer(half, rows, columns),
+            low_buffer(out_rows, middle),
+            low_buffer(out_rows, middle),
+            low_buffer(peers, rows, columns),
+            pltpu.VMEM((small_rows, width), high),
+            pltpu.VMEM((peers, *piece), high),
+            pltpu.VMEM((4, *piece), high),
+            pltpu.VMEM((peers, *piece), high),
+            pltpu.VMEM((length, width), high),
+            dma((20,)), dma((20,)),
+            dma((peers - 1,)), dma((peers,)),
+            dma((peers - 1,)), dma((peers,)),
+            dma((3,)), dma((4,)),
+            dma((peers - 1,)), dma((peers,)),
+            *Scatter.buffers(n, length, width),
+        ],
+        compiler_params=communicating(6),
+        cost_estimate=pl.CostEstimate(flops=0, bytes_accessed=64 << 20, transcendentals=0),
+        name="sum_weight_gradients",
+    )(
+        grad_projection.reshape(peers, shard_rows, columns), grad_out, attn_gain, ffn_gain, query_gain, key_gain,
+        router, resid, mixture.reshape(n, 2 * length, width),
+    )
+
+
+def widen_kernel(
+    wide_0, down_0, wide_1, down_1, query_in, key_in, value_in, out_in,
+    gate_ref, up_ref, down_ref, query_ref, key_ref, value_ref, out_ref,
+):
+    for expert, (wide, down) in enumerate(((wide_0, down_0), (wide_1, down_1))):
+
+        @pl.when(pl.program_id(0) == expert)
+        def place():
+            gate_ref[0] = wide[0, 0].astype(high)
+            up_ref[0] = wide[0, 1].astype(high)
+            down_ref[0] = down[...].astype(high)
+
+    for source, target in ((query_in, query_ref), (key_in, key_ref), (value_in, value_ref), (out_in, out_ref)):
+        target[...] = source[...].astype(high)
+
+
+def run_widen(grads, weight_grads, hidden_units, model_width, groups):
+    piece, tile = hidden_units // groups, model_width // groups
+    operands, specs = [], []
+
+    def of_expert(expert):
+        return lambda x, j: jnp.where(x == expert, j, 0 if expert else groups - 1)
+
+    for expert, rows in enumerate(grads):
+        turn = of_expert(expert)
+        operands += [rows[: 2 * hidden_units].reshape(groups, 2, piece, tile), rows[2 * hidden_units :]]
+        specs += [
+            pl.BlockSpec((1, 2, piece, tile), lambda x, j, turn=turn: (turn(x, j), 0, 0, 0)),
+            pl.BlockSpec((piece, tile), lambda x, j, turn=turn: (turn(x, j), 0)),
+        ]
+    steps = 2 * groups
+
+    def rows_of(array):
+        return pl.BlockSpec((array.shape[0] // steps, array.shape[1]), lambda x, j: (x * groups + j, 0))
+
+    return pl.pallas_call(
+        widen_kernel,
+        grid=(2, groups),
+        out_shape=[
+            jax.ShapeDtypeStruct((2, piece, model_width), high),
+            jax.ShapeDtypeStruct((2, piece, model_width), high),
+            jax.ShapeDtypeStruct((2, hidden_units, tile), high),
+            *[jax.ShapeDtypeStruct(array.shape, high) for array in weight_grads],
+        ],
+        in_specs=specs + [rows_of(array) for array in weight_grads],
+        out_specs=[
+            pl.BlockSpec((1, piece, tile), lambda x, j: (x, 0, j)),
+            pl.BlockSpec((1, piece, tile), lambda x, j: (x, 0, j)),
+            pl.BlockSpec((1, piece, tile), lambda x, j: (x, j, 0)),
+            *[rows_of(array) for array in weight_grads],
+        ],
+        compiler_params=pltpu.CompilerParams(vmem_limit_bytes=40 << 20),
+        name="widen",
+    )(*operands, *weight_grads)
+
+
 def gather_tokens(rows):
     return lax.all_gather(rows, "expert", axis=0, tiled=True)
 
 
 def scatter_sum(partial):
     return lax.psum_scatter(partial, "expert", scatter_dimension=0, tiled=True)
+
+
+def projection_gradients(grad_projection, peers, kv_heads, head_size):
+    width, columns = grad_projection.shape
+    shard_rows = width // peers
+    local_width = columns - head_size
+    sharers = peers // kv_heads
+    grad_projection = grad_projection.reshape(peers, shard_rows, columns)
+    grad_projection = lax.psum_scatter(grad_projection, "dp", scatter_dimension=1, tiled=True)
+    grad_projection = lax.all_to_all(
+        grad_projection, "expert", split_axis=0, concat_axis=0, tiled=True
+    )
+    grad_projection = lax.all_gather(grad_projection, "dp", axis=1, tiled=True)
+    grad_query_w = (
+        grad_projection[:, :, :local_width].transpose(1, 0, 2).reshape(shard_rows, peers * local_width)
+    ).astype(high)
+    shared = grad_projection[:, :, local_width:].reshape(kv_heads, sharers, shard_rows, head_size)
+    kv_width = kv_heads * head_size
+    grad_key_w = shared[:, 0].transpose(1, 0, 2).reshape(shard_rows, kv_width).astype(high)
+    grad_value_w = shared[:, 1].transpose(1, 0, 2).reshape(shard_rows, kv_width).astype(high)
+    return grad_query_w, grad_key_w, grad_value_w
+
+
+def out_gradient(grad_out):
+    summed = lax.psum_scatter(grad_out, "dp", scatter_dimension=0, tiled=True)
+    return lax.all_gather(summed, "dp", axis=0, tiled=True).astype(high)
+
+
+def constant_tables(length, head_size):
+    half = head_size // 2
+    freqs = np.float32(rope_base) ** (-np.arange(half, dtype=np.float32) * np.float32(2.0 / head_size))
+    angles = np.arange(length, dtype=np.float32)[:, None] * freqs[None, :]
+    cosines, sines = np.cos(angles), np.sin(angles)
+    return (
+        jnp.asarray(np.concatenate([cosines, cosines], 1), high),
+        jnp.asarray(np.concatenate([-sines, sines], 1), high),
+    )
+
+
+def fits_kernels(peers, groups, sharers, experts, full_length, width):
+    return groups == 4 and peers % 2 == 0 and peers <= 8 and sharers == 2 and experts == 2 * peers and full_length * width <= 1 << 21
+
+
+def fused_layer(
+    tokens, segments, routes, cotangent, norm_gain_attn, query_weight, key_matrix, value_matrix, query_gain,
+    key_gain, out_weight, norm_gain_ffn, router_weight, gate_weight, up_weight, down_weight, heads,
+):
+    length, model_width = tokens.shape
+    head_size = query_gain.shape[0]
+    peers = lax.axis_size("expert")
+    groups = lax.axis_size("dp")
+    local_experts, _, hidden_units = gate_weight.shape
+    experts = local_experts * peers
+    full_length = length * peers
+    kv_heads = peers // 2
+    local_width = heads * head_size
+    gain_attn_row = norm_gain_attn.reshape(1, model_width)
+    gain_ffn_row = norm_gain_ffn.reshape(1, model_width)
+
+    named = jnp.any(routes[:, :, None] == jnp.arange(128, dtype=jnp.int32)[None, None, :], axis=1).astype(low)
+    hidden, all_named, projection, raw = run_gather(
+        tokens, gain_attn_row, named, query_weight, key_matrix, value_matrix, peers, groups
+    )
+    cotangent_ready, hidden = lax.optimization_barrier((cotangent, hidden))
+    cotangents = lax.all_gather(cotangent_ready, "expert", axis=0, tiled=True)
+    cosines, sines = constant_tables(full_length, head_size)
+    seg_col = jnp.broadcast_to(segments.reshape(full_length, 1), (full_length, head_size))
+    seg_row = jnp.broadcast_to(segments.reshape(1, full_length), (8, full_length))
+    query_gain_row = query_gain.reshape(1, head_size)
+    key_gain_row = key_gain.reshape(1, head_size)
+    mixed, query_low, key_low, value_low, inverse = run_attention_forward(
+        raw, heads, head_size, query_gain_row, key_gain_row, cosines, sines, seg_col, seg_row
+    )
+    resid, ffn_local = run_project(mixed, out_weight, tokens, gain_ffn_row, peers)
+    router = jnp.concatenate([router_weight.T, jnp.zeros((128 - experts, model_width), low)], axis=0)
+    sums, gates, mixture, *grads = run_experts(
+        ffn_local, all_named, router, cotangents, gate_weight, up_weight, down_weight, peers, groups
+    )
+    grads = [
+        lax.psum_scatter(each.reshape(-1, each.shape[2]), "dp", scatter_dimension=0, tiled=True) for each in grads
+    ]
+    grad_resid, grad_attn, grad_mixed, grad_router, gain_ffn_part = run_turn(
+        sums, gates, ffn_local, resid, cotangent, gain_ffn_row, router, out_weight, experts, peers
+    )
+    grad_query_low, grad_key_part, grad_value_part, query_gain_part = run_attention_backward(
+        raw, query_low, key_low, value_low, inverse, mixed, grad_mixed, heads, head_size,
+        query_gain_row, cosines, sines, seg_col, seg_row,
+    )
+    input_grad, grad_projection, grad_out, gain_attn_part, key_gain_part = run_input(
+        grad_key_part, grad_value_part, raw[:, local_width : local_width + head_size], key_gain_row, cosines,
+        sines, grad_query_low, projection, hidden, mixed, grad_attn, grad_resid, tokens, gain_attn_row, peers,
+    )
+    *weight_grads, small, output = run_weights(
+        grad_projection, grad_out, gain_attn_part, gain_ffn_part, query_gain_part, key_gain_part, grad_router,
+        resid, mixture, peers, kv_heads,
+    )
+    gate_w, up_w, down_w, query_w, key_w, value_w, out_w = run_widen(
+        grads, weight_grads, hidden_units, model_width, groups
+    )
+    return (
+        output,
+        input_grad,
+        small[0],
+        query_w,
+        key_w,
+        value_w,
+        small[2, :head_size],
+        small[3, :head_size],
+        out_w,
+        small[1],
+        small[8:].T,
+        gate_w.transpose(0, 2, 1),
+        up_w.transpose(0, 2, 1),
+        down_w,
+    )
 
 
 def on_device(
@@ -243,6 +1599,12 @@
     full_length = length * peers
     piece = shard_rows // groups
 
+    if fits_kernels(peers, groups, sharers, experts, full_length, model_width):
+        return fused_layer(
+            tokens, segments, routes, cotangent, norm_gain_attn, query_weight, key_matrix, value_matrix,
+            query_gain, key_gain, out_weight, norm_gain_ffn, router_weight, gate_weight, up_weight, down_weight, heads,
+        )
+
     def own_rows(matrix):
         return lax.dynamic_slice_in_dim(matrix, group * piece, piece, 0)
 
@@ -379,21 +1741,10 @@
     grad_inputs_norm, gain_rows_attn = norm_back(inputs, norm_gain_attn, grad_hidden_attn)
     input_grad = grad_resid + grad_inputs_norm
 
-    grad_projection = dot_first(hidden, own_columns).astype(low)
-    grad_projection = grad_projection.reshape(peers, shard_rows, -1)
-    grad_projection = lax.psum_scatter(grad_projection, "dp", scatter_dimension=1, tiled=True)
-    grad_projection = lax.all_to_all(
-        grad_projection, "expert", split_axis=0, concat_axis=0, tiled=True
-    )
-    grad_projection = lax.all_gather(grad_projection, "dp", axis=1, tiled=True)
-    grad_query_w = (
-        grad_projection[:, :, :local_width].transpose(1, 0, 2).reshape(shard_rows, query_width)
-    ).astype(high)
-    shared = grad_projection[:, :, local_width:].reshape(kv_heads, sharers, shard_rows, head_size)
-    grad_key_w = shared[:, 0].transpose(1, 0, 2).reshape(shard_rows, kv_width).astype(high)
-    grad_value_w = shared[:, 1].transpose(1, 0, 2).reshape(shard_rows, kv_width).astype(high)
-    grad_out_w = lax.psum_scatter(grad_out.astype(low), "dp", scatter_dimension=0, tiled=True)
-    grad_out_w = lax.all_gather(grad_out_w, "dp", axis=0, tiled=True).astype(high)
+    grad_query_w, grad_key_w, grad_value_w = projection_gradients(
+        dot_first(hidden, own_columns).astype(low), peers, kv_heads, head_size
+    )
+    grad_out_w = out_gradient(grad_out.astype(low))
 
     wide = jnp.concatenate(grad_gate_w + grad_up_w, axis=1)
     wide = lax.psum_scatter(wide, "dp", scatter_dimension=0, tiled=True)

time: 1100 us -> 535 us (0.49)
  waiting for transfers between devices: 754 us -> 0.09 us
  Pallas kernels: 24.2 us -> 495 us
  matrix products: 164 us -> 0 us
  other arithmetic: 44.2 us -> 0.89 us
  blocking collectives: 41.4 us -> 0 us
  local copies, waits for them, and re-layouts: 43.4 us -> 18.8 us
    pallas_call x0 -> x8, Pallas kernels: none -> 471 us  [the longest x1 90.9 us: run_weights(): pl.pallas_call(weights_kernel, out_shape=[jax.ShapeDtypeStruct((shard_row...]
    all_gather x7 -> x1, waiting for transfers between devices: 251 us -> 0.02 us  [fused_layer(): cotangents = lax.all_gather(cotangent_ready, 'expert', axis=0, tiled=True)]
    unnamed x18 -> x3, waiting for transfers between devices: 192 us -> 0.05 us
    reduce_scatter x6 -> x2, waiting for transfers between devices: 188 us -> 0.02 us  [fused_layer(): lax.psum_scatter(each.reshape(-1, each.shape[2]), 'dp', scatter_dimension...]
    dot_general x34 -> x0, matrix products: 164 us -> none  [the longest x9 69.1 us: dot_last(): lax.dot_general(left, right, (((1,), (1,)), ((), ())), preferred_element_...]
    psum x1 -> x0, waiting for transfers between devices: 122 us -> none  [on_device(): small = lax.psum(small, ('dp', 'expert'))]
    all_to_all x1 -> x0, blocking collectives: 27.1 us -> none  [on_device(): lax.all_to_all(outgoing, 'expert', split_axis=0, concat_axis=0, tiled=True)]
    convert_element_type x9 -> x1, other arithmetic: 16.1 us -> 0.63 us  [fused_layer(): jnp.any(routes[:, :, None] == jnp.arange(128, dtype=jnp.int32)[None, None...]
  transfers between devices with their start and end apart: 18 -> 3, of which waited for: 15 -> 0; matrix products, arithmetic and copies ran while one was open for 13% -> 2% of each run, Pallas kernels for 1% -> 66%
where the time goes in v2:
time: 535 us; the launch traced here: 529 us
  Pallas kernels  495 us (93%)
  local copies, waits for them, and re-layouts  18.8 us (4%)
  between operations  14 us (3%)
    pallas_call x1, Pallas kernels, run_weights(): pl.pallas_call(weights_kernel, out_shape=[jax.ShapeDtypeStruct((shard_row...  90.9 us
    pallas_call x1, Pallas kernels, run_gather(): pl.pallas_call(gather_kernel, out_shape=[jax.ShapeDtypeStruct((length * p...  78.9 us
    pallas_call x1, Pallas kernels, run_project(): pl.pallas_call(project_kernel, out_shape=[jax.ShapeDtypeStruct((length, w...  66.7 us
    pallas_call x1, Pallas kernels, run_experts(): pl.pallas_call(first_expert_kernel, out_shape=[jax.ShapeDtypeStruct((full...  62.9 us
    pallas_call x1, Pallas kernels, run_experts(): pl.pallas_call(second_expert_kernel, out_shape=[jax.ShapeDtypeStruct((len...  61 us
    pallas_call x1, Pallas kernels, run_turn(): pl.pallas_call(turn_kernel, out_shape=[jax.ShapeDtypeStruct((length, widt...  53.4 us
    pallas_call x1, Pallas kernels, run_input(): pl.pallas_call(input_kernel, out_shape=[jax.ShapeDtypeStruct((length, wid...  51 us
    pallas_call x1, Pallas kernels, run_attention_backward(): pl.pallas_call(attention_backward, grid=(heads,), in_specs=[per_head, per...  14.3 us
  transfers between devices with their start and end apart: 3, of which 0 were waited for; matrix products, arithmetic and copies ran while one was open for 2% of the time, Pallas kernels for 66%

profile of v2, /device:TPU:0, one launch (start us, length us, event | category | flops | bytes accessed | tf_op | source)
XLA Modules:
  0.0 529.3 jit_solution(834287978734602734)
XLA Ops:
  7.3 0.9 copy.33
  9.1 78.9 %gather_hidden.1 = (bf16[1024,2048]{1,0:T(8,128)(2,1)}, bf16[1024,128]{1,0:T(8,128)(2,1)}, bf16[8,4,64,768]{3,2,1,0:T(8,128)(2,1)}, f32[1024,768]{1,0:T(8,128)}) custom-call(bf16[128,2048]{1,0:T(8,128)(2,1)} %tokens_ref.5, f32[1,2048]{1,0:T(1,128)} %bitcast.37, bf16[128,128]{1,0:T(8,128)(2,1)} %convert_element_type.3.named_ref, bf16[256,4096]{1,0:T(8,128)(2,1)} %query_ref.1, ...), custom_call_target="tpu_custom_call" | custom-call | bytes 67108864 | tf_op jit(solution)/shard_map/gather_hidden/pallas_call | solution.py:581
  88.1 0.8 concatenate.3.router_ref
  89.2 9.6 %shard_map.281 = (bf16[1024,512]{1,0:T(8,128)(2,1)S(1)}, bf16[1024,512]{1,0:T(8,128)(2,1)}, bf16[1024,128]{1,0:T(8,128)(2,1)S(1)}, bf16[1024,128]{1,0:T(8,128)(2,1)S(1)}, f32[1024,512]{1,0:T(8,128)}) custom-call(f32[1024,768]{1,0:T(8,128)} %get-tuple-element.63.query_ref.key_ref.value_ref, f32[1024,768]{1,0:T(8,128)} %get-tuple-element.63.query_ref.key_ref.value_ref, ...), custom_call_target="tpu_custom_call" | custom-call | flops 1610612736 | bytes 4194304 | tf_op jit(solution)/shard_map/pallas_call | solution.py:147
  98.8 1.0 copy-done
  99.8 66.7 %project_and_sum.1 = (f32[128,2048]{1,0:T(8,128)}, bf16[128,2048]{1,0:T(8,128)(2,1)}) custom-call(bf16[1024,512]{1,0:T(8,128)(2,1)} %copy-done, bf16[512,2048]{1,0:T(8,128)(2,1)} %weight_ref.3, bf16[128,2048]{1,0:T(8,128)(2,1)} %tokens_ref.5, f32[1,2048]{1,0:T(1,128)} %bitcast.35), custom_call_target="tpu_custom_call" | custom-call | bytes 67108864 | tf_op jit(solution)/shard_map/project_and_sum/pallas_call | solution.py:629
  166.4 62.9 %first_expert.1 = (f32[1024,128]{1,0:T(8,128)}, f32[128,128]{1,0:T(8,128)}, bf16[1024,2048]{1,0:T(8,128)(2,1)}, bf16[1024,2048]{1,0:T(8,128)(2,1)}, bf16[4,256,2...) custom-call(bf16[128,2048]{1,0:T(8,128)(2,1)} %get-tuple-element.69.ffn_ref, ...), custom_call_target="tpu_custom_call" | custom-call | bytes 125829120 | tf_op jit(solution)/shard_map/first_expert/pallas_call | solution.py:890
  229.4 61.0 %second_expert.1 = (f32[128,2176]{1,0:T(8,128)}, bf16[1024,2048]{1,0:T(8,128)(2,1)}, bf16[4,2304,512]{2,1,0:T(8,128)(2,1)}) custom-call(f32[1024,128]{1,0:T(8,128)} %get-tuple-element.73.gates_ref, bf16[1024,2048]{1,0:T(8,128)(2,1)} %get-tuple-element.74.rows_hbm, bf16[1024,2048]{1,0:T(8,128)(2,1)} %all-gather.2.cloned.1.call-done.cot_hbm, ...), custom_call_target="tpu_custom_call" | custom-call | bytes 125829120 | tf_op jit(solution)/shard_map/second_expert/pallas_call | solution.py:914
  290.4 1.9 slice.30.raw_ref
  292.3 53.4 %turn_to_attention.1 = (f32[128,2048]{1,0:T(8,128)}, bf16[1024,2048]{1,0:T(8,128)(2,1)}, bf16[1024,512]{1,0:T(8,128)(2,1)}, f32[16,2048]{1,0:T(8,128)}, f32[8,2048]{1,0:T(8,128)}) custom-call(f32[128,2176]{1,0:T(8,128)} %get-tuple-element.77.sum_ref, f32[128,128]{1,0:T(8,128)} %get-tuple-element.78.gates_ref, bf16[128,2048]{1,0:T(8,128)(2,1)} %get-tuple-element.69.ffn_ref, ...), custom_call_target="tpu_custom_call" | custom-call | bytes 67108864 | tf_op jit(solution)/shard_map/turn_to_attention/pallas_call | solution.py:977
  345.7 14.3 %shard_map.282 = (bf16[1024,512]{1,0:T(8,128)(2,1)}, f32[1024,128]{1,0:T(8,128)S(1)}, f32[1024,128]{1,0:T(8,128)S(1)}, f32[8,128]{1,0:T(8,128)S(1)}) custom-call(f32[1024,768]{1,0:T(8,128)} %get-tuple-element.63.query_ref.key_ref.value_ref, bf16[1024,512]{1,0:T(8,128)(2,1)} %get-tuple-element.64.query_low_ref, ...), custom_call_target="tpu_custom_call" | custom-call | flops 3221225472 | bytes 8388608 | tf_op jit(solution)/shard_map/pallas_call | solution.py:179
  360.0 0.8 copy-done.5
  362.2 51.0 %input_gradient.1 = (f32[128,2048]{1,0:T(8,128)}, bf16[2048,640]{1,0:T(8,128)(2,1)}, bf16[512,2048]{1,0:T(8,128)(2,1)}, f32[8,2048]{1,0:T(8,128)}, f32[8,128]{1,0:T(8,128)}) custom-call(f32[1024,128]{1,0:T(8,128)} %copy-done.5, f32[1024,128]{1,0:T(8,128)} %copy-done.6, f32[1024,128]{1,0:T(8,128)} %slice.30.raw_ref, f32[1,128]{1,0:T(1,128)} %bitcast.25, ...), custom_call_target="tpu_custom_call" | custom-call | bytes 67108864 | tf_op jit(solution)/shard_map/input_gradient/pallas_call | solution.py:1079
  413.2 90.9 %sum_weight_gradients.1 = (bf16[256,4096]{1,0:T(8,128)(2,1)}, bf16[256,512]{1,0:T(8,128)(2,1)}, bf16[256,512]{1,0:T(8,128)(2,1)}, bf16[512,2048]{1,0:T(8,128)(2,...) custom-call(bf16[8,256,640]{2,1,0:T(8,128)(2,1)} %bitcast.33, bf16[512,2048]{1,0:T(8,128)(2,1)} %get-tuple-element.89.out_ref, ...), custom_call_target="tpu_custom_call" | custom-call | bytes 67108864 | tf_op jit(solution)/shard_map/sum_weight_gradients/pallas_call | solution.py:1340
  504.1 1.3 slice_bitcast_fusion.1
  505.4 1.5 fusion.1
  506.9 1.6 slice_bitcast_fusion
  508.5 1.5 slice.40
  510.0 1.2 slice.41.down_0
  511.3 1.7 slice.42
  513.0 1.2 slice.43.down_1
  514.2 6.8 %widen.1 = (f32[2,192,2048]{2,1,0:T(8,128)}, f32[2,192,2048]{2,1,0:T(8,128)}, f32[2,768,512]{2,1,0:T(8,128)}, f32[256,4096]{1,0:T(8,128)}, f32[256,512]{1,0:T(8,...) custom-call(bf16[4,2,192,512]{3,2,1,0:T(8,128)(2,1)S(1)} %bitcast.23, bf16[768,512]{1,0:T(8,128)(2,1)S(1)} %slice.41.down_0, ...), custom_call_target="tpu_custom_call" | custom-call | tf_op jit(solution)/shard_map/widen/pallas_call | solution.py:1423
  521.0 0.8 copy.36
  521.8 1.0 copy.37
  (43 shorter events, 2.7 us)
Async XLA Ops:
  7.2 81.9 %copy-start.1 = (f32[1024,128]{1,0:T(8,128)S(1)}, f32[1024,128]{1,0:T(8,128)}, u32[]{:S(2)}) copy-start(f32[1024,128]{1,0:T(8,128)} %constant.8.clone.cos_ref) | copy-start | bytes 1572868
  7.2 81.9 %copy-start.2 = (f32[1024,128]{1,0:T(8,128)S(1)}, f32[1024,128]{1,0:T(8,128)}, u32[]{:S(2)}) copy-start(f32[1024,128]{1,0:T(8,128)} %constant.9.clone.sin_ref) | copy-start | bytes 1572868
  7.2 80.9 %copy-start.14 = (bf16[2048,16]{0,1:T(8,128)(2,1)S(1)}, bf16[2048,16]{0,1:T(8,128)(2,1)}, u32[]{:S(2)}) copy-start(bf16[2048,16]{0,1:T(8,128)(2,1)} %param.30) | copy-start | bytes 196612
  7.2 81.9 %copy-start.11 = (f32[128]{0:T(128)S(1)}, f32[128]{0:T(128)}, u32[]{:S(2)}) copy-start(f32[128]{0:T(128)} %param.26) | copy-start | bytes 1540
  7.2 81.9 %copy-start.10 = (f32[128]{0:T(128)S(1)}, f32[128]{0:T(128)}, u32[]{:S(2)}) copy-start(f32[128]{0:T(128)} %param.27) | copy-start | bytes 1540
  7.2 81.7 %copy-start.15 = (s32[1,1024]{1,0:T(1,128)S(1)}, s32[1,1024]{1,0:T(1,128)}, u32[]{:S(2)}) copy-start(s32[1,1024]{1,0:T(1,128)} %param.19) | copy-start | bytes 12292
  7.2 159.2 %all-gather.2.cloned.1.call-start = ((), (), s32[]{:S(2)}) async-start(), calls=%async_computation.2 | async-start | bytes 4718592 | tf_op jit(solution)/shard_map/all_gather | solution.py:1514
  88.0 420.5 %reduce-scatter.3.cloned.1.call-start = ((), (), s32[]{:S(2)}) async-start(), calls=%async_computation.3 | async-start | bytes 11796480 | tf_op jit(solution)/shard_map/reduce_scatter | solution.py:1529
  98.8 1.0 copy-start
  229.3 281.9 %reduce-scatter.5.cloned.1.call-start = ((), (), s32[]{:S(2)}) async-start(), calls=%async_computation.4 | async-start | bytes 11796480 | tf_op jit(solution)/shard_map/reduce_scatter | solution.py:1529
  360.0 0.8 copy-start.5
  360.8 0.8 copy-start.6
  361.6 0.6 copy-start.9
  510.0 4.2 copy-start.7
  510.0 4.2 copy-start.8
  511.3 2.9 copy-start.3
  511.3 2.9 copy-start.4
  514.2 6.8 %copy-start.13 = (bf16[128,2048]{1,0:T(8,128)(2,1)S(1)}, bf16[128,2048]{1,0:T(8,128)(2,1)}, u32[]{:S(2)}) copy-start(bf16[128,2048]{1,0:T(8,128)(2,1)} %get-tuple-element.130) | copy-start | bytes 1572868
  514.2 7.6 %copy-start.12 = (f32[128,2048]{1,0:T(8,128)S(1)}, f32[128,2048]{1,0:T(8,128)}, u32[]{:S(2)}) copy-start(f32[128,2048]{1,0:T(8,128)} %get-tuple-element.131) | copy-start | bytes 3145732
Sparse Core Ops, SparseCore 0:
  88.1 67.3 all-gather.1
  229.5 95.8 reduce-scatter.2
  328.4 95.4 reduce-scatter.4

commit v3 on v2

--- a/solution.py
+++ b/solution.py
@@ -241,10 +241,9 @@
 
 
 class Gather:
-    def __init__(self, chain, own, whole, send, recv, local):
-        self.chain, self.own, self.whole = chain, own, whole
+    def __init__(self, chain, own, block, send, recv, local):
+        self.chain, self.own, self.block = chain, own, block
         self.send, self.recv, self.local = send, recv, local
-        self.rows = own.shape[0]
 
     @staticmethod
     def semaphores(n):
@@ -253,9 +252,6 @@
             pltpu.SemaphoreType.DMA((2 * n,)),
             pltpu.SemaphoreType.DMA(()),
         ]
-
-    def block(self, z, c):
-        return self.whole.at[pl.ds(pl.multiple_of((2 * z + c) * self.rows, self.rows), self.rows)]
 
     def copy(self, source, z, way, peer):
         c = self.chain.c
@@ -320,12 +316,60 @@
             self.copy(block, at, 2, ch.sibling).wait_send()
 
 
+class NearGather(Gather):
+    def __init__(self, chain, own, near, block, send, recv, local):
+        super().__init__(chain, own, block, send, recv, local)
+        self.near = near
+
+    @staticmethod
+    def semaphores(n):
+        return Gather.semaphores(n)[:2] + [pltpu.SemaphoreType.DMA((4,))]
+
+    def place(self, at):
+        ch = self.chain
+        source = self.own if at == 3 else self.near.at[at]
+        z, c = ((ch.z - 1, ch.c), (ch.z + 1, ch.c), (ch.z, 1 - ch.c), (ch.z, ch.c))[at]
+        return pltpu.make_async_copy(source, self.block(z, c), self.local.at[at])
+
+    def begin(self):
+        ch = self.chain
+
+        def below():
+            pl.when(ch.has_up)(lambda: self.copy(self.near.at[0], ch.z - 1, 0, ch.up).start())
+            self.copy(self.near.at[0], ch.z - 1, 2, ch.sibling).start()
+            self.place(0).start()
+
+        def above():
+            pl.when(ch.has_down)(lambda: self.copy(self.near.at[1], ch.z + 1, 1, ch.down).start())
+            self.copy(self.near.at[1], ch.z + 1, 2, ch.sibling).start()
+            self.place(1).start()
+
+        pl.when(ch.has_down)(below)
+        pl.when(ch.has_up)(above)
+        self.place(2).start()
+        self.place(3).start()
+
+    def wait_placed(self):
+        pl.when(self.chain.has_down)(lambda: self.place(0).wait())
+        pl.when(self.chain.has_up)(lambda: self.place(1).wait())
+        self.place(2).wait()
+        self.place(3).wait()
+
+    def finish(self):
+        ch = self.chain
+        for z in range(ch.n):
+            at = jnp.int32(z)
+            block = self.block(at, ch.c)
+            pl.when(ch.has_up & (ch.z > z))(lambda: self.copy(block, at, 0, ch.up).wait_send())
+            pl.when(ch.has_down & (ch.z < z))(lambda: self.copy(block, at, 1, ch.down).wait_send())
+            pl.when(ch.z != z)(lambda: self.copy(block, at, 2, ch.sibling).wait_send())
+
+
 class Scatter:
-    def __init__(self, chain, parts, pair, flow, pair_send, pair_recv, flow_send, flow_recv):
-        self.chain, self.parts, self.pair, self.flow = chain, parts, pair, flow
+    def __init__(self, chain, half, pair, flow, pair_send, pair_recv, flow_send, flow_recv):
+        self.chain, self.half, self.pair, self.flow = chain, half, pair, flow
         self.pair_send, self.pair_recv = pair_send, pair_recv
         self.flow_send, self.flow_recv = flow_send, flow_recv
-        self.rows = pair.shape[1]
 
     @staticmethod
     def buffers(n, rows, width):
@@ -337,9 +381,6 @@
             pltpu.SemaphoreType.DMA((n,)),
             pltpu.SemaphoreType.DMA((n + 1,)),
         ]
-
-    def half(self, z, c):
-        return self.parts.at[z, pl.ds(pl.multiple_of(c * self.rows, self.rows), self.rows)]
 
     def pair_copy(self, z):
         ch = self.chain
@@ -450,6 +491,14 @@
             copy.wait_send()
 
 
+def row_block(ref, rows):
+    return lambda z, c: ref.at[pl.ds(pl.multiple_of((2 * z + c) * rows, rows), rows)]
+
+
+def chip_block(ref, rows):
+    return lambda z, c: ref.at[z, pl.ds(pl.multiple_of(c * rows, rows), rows)]
+
+
 def communicating(collective_id):
     return pltpu.CompilerParams(
         collective_id=collective_id, has_side_effects=True, vmem_limit_bytes=60 << 20
@@ -464,10 +513,12 @@
 
 
 def gather_kernel(
-    tokens_ref, gain_ref, named_ref, query_ref, key_ref, value_ref,
-    hidden_ref, all_named_ref, projection_ref, raw_ref,
-    own, stage, wide_send, wide_recv, wide_local, thin_send, thin_recv, thin_local, swap_send, swap_recv,
-    x_send, x_recv, y_send, y_recv, far_send, far_recv,
+    tokens_ref, gain_ref, named_ref, cot_ref, query_hbm, key_hbm, value_hbm,
+    hidden_hbm, all_named_ref, near_ref, projection_hbm, raw_hbm,
+    own, stage, hidden_ref, projection_ref, raw_ref, query_ref, key_ref, value_ref,
+    send_a, recv_a, local_a, send_b, recv_b, local_b, name_send, name_recv,
+    swap_send, swap_recv, x_send, x_recv, y_send, y_recv, far_send, far_recv, out_sems, load_sems,
+    near_send, near_recv,
 ):
     chain = Chain()
     n = chain.n
@@ -483,13 +534,24 @@
         pl.semaphore_signal(barrier, inc=1, device_id=device, device_id_type=MESH)
     rows = stage.shape[1]
     quarter = pl.ds(pl.multiple_of(group * rows, rows), rows)
+    loads = [
+        pltpu.make_async_copy(source.at[quarter], target, load_sems.at[at])
+        for at, (source, target) in enumerate(
+            ((query_hbm, query_ref), (key_hbm, key_ref), (value_hbm, value_ref))
+        )
+    ]
+    for load in loads:
+        load.start()
     query_width = query_ref.shape[1] // peers
     head_size = key_ref.shape[1] // n
+    own[...] = norm_rows(tokens_ref[...].astype(high), gain_ref[...]).astype(low)
+    for load in loads:
+        load.wait()
     for peer in range(peers):
         shared = pl.ds(peer // 2 * head_size, head_size)
-        stage[peer, :, :query_width] = query_ref[quarter, pl.ds(peer * query_width, query_width)]
-        stage[peer, :, query_width : query_width + head_size] = key_ref[quarter, shared]
-        stage[peer, :, query_width + head_size :] = value_ref[quarter, shared]
+        stage[peer, :, :query_width] = query_ref[:, pl.ds(peer * query_width, query_width)]
+        stage[peer, :, query_width : query_width + head_size] = key_ref[:, shared]
+        stage[peer, :, query_width + head_size :] = value_ref[:, shared]
     pl.semaphore_wait(barrier, peers + 1)
 
     def remote(source, target, send, recv, device):
@@ -506,11 +568,28 @@
     ]
     for copy in swaps:
         copy.start()
-    own[...] = norm_rows(tokens_ref[...].astype(high), gain_ref[...]).astype(low)
-    wide = Gather(chain, own, hidden_ref, wide_send, wide_recv, wide_local)
-    thin = Gather(chain, named_ref, all_named_ref, thin_send, thin_recv, thin_local)
-    wide.begin()
-    thin.begin()
+    length = own.shape[0]
+    piece = length // 2
+
+    def half_block(half):
+        def block_of(z, c):
+            return hidden_ref.at[pl.ds(pl.multiple_of((2 * z + c) * length + half * piece, piece), piece)]
+
+        return block_of
+
+    wide = [
+        Gather(chain, own.at[pl.ds(half * piece, piece)], half_block(half), *sems)
+        for half, sems in enumerate(((send_a, recv_a, local_a), (send_b, recv_b, local_b)))
+    ]
+    for gather in wide:
+        gather.begin()
+    names = [
+        remote(named_ref, all_named_ref.at[me], name_send.at[at], name_recv.at[me], {"expert": peer})
+        for at, peer in enumerate(others)
+    ]
+    for copy in names:
+        copy.start()
+    all_named_ref[me] = named_ref[...]
     projection_ref[me, group] = stage[me]
 
     def to_x(at, source, place):
@@ -537,20 +616,34 @@
         to_x(at, source, group).start()
         to_y(at, source, group).start()
         if step > 0 and core == 1:
-            wide.service(step)
-            thin.service(step)
+            for gather in wide:
+                gather.service(step)
+    def near(slot, peer):
+        return remote(cot_ref, near_ref.at[slot], near_send.at[slot], near_recv.at[slot], {"expert": peer})
+
+    pl.when(chain.has_up)(lambda: near(0, chain.up).start())
+    pl.when(chain.has_down)(lambda: near(1, chain.down).start())
+    near(2, chain.sibling).start()
     for at, (source, core, _) in enumerate(sources):
         to_x(at, source, from_x).wait_recv()
         to_y(at, source, from_y).wait_recv()
         to_far(at, core, source, from_x if core == 0 else from_y).start()
-    for gather in (thin, wide):
+    for gather in wide:
         for z in range(n):
             gather.wait_sibling(jnp.int32(z))
         gather.keep().wait()
+    hidden_out = pltpu.make_async_copy(hidden_ref, hidden_hbm, out_sems.at[0])
+    hidden_out.start()
     for at, (source, core, _) in enumerate(sources):
         to_far(at, core, source, far).wait_recv()
+    projection_out = pltpu.make_async_copy(projection_ref, projection_hbm, out_sems.at[1])
+    projection_out.start()
     pair_rows = 2 * own.shape[0]
     shard_rows = 4 * rows
+
+    def raw_out(step):
+        tokens = pl.ds(pl.multiple_of(step * pair_rows, pair_rows), pair_rows)
+        return pltpu.make_async_copy(raw_ref.at[tokens], raw_hbm.at[tokens], out_sems.at[2 + step])
 
     @pl.loop(0, n)
     def each(step):
@@ -560,105 +653,136 @@
             weight = projection_ref[source].reshape(shard_rows, raw_ref.shape[1])
             total = total + dot(hidden_ref[tokens, source * shard_rows : (source + 1) * shard_rows], weight)
         raw_ref[tokens] = total
-
-    for gather in (thin, wide):
+        raw_out(step).start()
+
+    for gather in wide:
         gather.finish()
+    for at, peer in enumerate(others):
+        part = all_named_ref.at[peer]
+        remote(part, part, name_send.at[at], name_recv.at[peer], {"expert": peer}).wait_recv()
+        names[at].wait_send()
     for at, (source, core, _) in enumerate(sources):
         to_x(at, source, group).wait_send()
         to_y(at, source, group).wait_send()
         to_far(at, core, source, from_x if core == 0 else from_y).wait_send()
     for copy in swaps:
         copy.wait_send()
-
-
-def run_gather(tokens, gain, named, query_weight, key_matrix, value_matrix, peers, groups):
+    pl.when(chain.has_up)(lambda: near(0, chain.up).wait_send())
+    pl.when(chain.has_down)(lambda: near(1, chain.down).wait_send())
+    near(2, chain.sibling).wait_send()
+    pl.when(chain.has_down)(lambda: near(0, chain.sibling).wait_recv())
+    pl.when(chain.has_up)(lambda: near(1, chain.sibling).wait_recv())
+    near(2, chain.sibling).wait_recv()
+    hidden_out.wait()
+    projection_out.wait()
+    for step in range(n):
+        raw_out(step).wait()
+
+
+def run_gather(tokens, gain, named, cotangent, query_weight, key_matrix, value_matrix, peers, groups):
     length, width = tokens.shape
     n = peers // 2
     shard_rows, query_columns = query_weight.shape
     columns = query_columns // peers + 2 * key_matrix.shape[1] // n
     rows = shard_rows // groups
     dma = pltpu.SemaphoreType.DMA
-    hidden, all_named, projection, raw = pl.pallas_call(
+    hidden, all_named, near, projection, raw = pl.pallas_call(
         gather_kernel,
         out_shape=[
             jax.ShapeDtypeStruct((length * peers, width), low),
-            jax.ShapeDtypeStruct((length * peers, named.shape[1]), named.dtype),
+            jax.ShapeDtypeStruct((peers, *named.shape), named.dtype),
+            jax.ShapeDtypeStruct((3, length, width), low),
             jax.ShapeDtypeStruct((peers, groups, rows, columns), low),
             jax.ShapeDtypeStruct((length * peers, columns), high),
         ],
-        in_specs=[VMEM] * 6,
-        out_specs=[VMEM] * 4,
+        in_specs=[VMEM] * 4 + [ANY] * 3,
+        out_specs=[ANY, VMEM, VMEM, ANY, ANY],
         scratch_shapes=[
             pltpu.VMEM((length, width), low),
             pltpu.VMEM((peers, rows, columns), low),
+            pltpu.VMEM((length * peers, width), low),
+            pltpu.VMEM((peers, groups, rows, columns), low),
+            pltpu.VMEM((length * peers, columns), high),
+            pltpu.VMEM((rows, query_columns), low),
+            pltpu.VMEM((rows, key_matrix.shape[1]), low),
+            pltpu.VMEM((rows, key_matrix.shape[1]), low),
             *Gather.semaphores(n),
             *Gather.semaphores(n),
             dma((peers - 1,)), dma((peers,)),
+            dma((peers - 1,)), dma((peers,)),
             dma((peers,)), dma((peers,)), dma((peers,)), dma((peers,)), dma((peers,)), dma((peers,)),
+            dma((2 + n,)),
+            dma((3,)), dma((3,)), dma((3,)),
         ],
         compiler_params=communicating(1),
         cost_estimate=pl.CostEstimate(flops=0, bytes_accessed=64 << 20, transcendentals=0),
         name="gather_hidden",
-    )(tokens, gain, named, query_weight, key_matrix, value_matrix)
-    return hidden, all_named, projection.reshape(width, columns), raw
-
-
-def project_kernel(mixed_ref, weight_ref, tokens_ref, gain_ref, resid_ref, ffn_ref, parts, pair, flow, *sems):
-    chain = Chain()
-    scatter = Scatter(chain, parts, pair, flow, *sems)
-    rows = parts.shape[1]
-
-    chain.greet()
-
-    @pl.loop(0, chain.n)
-    def each(step):
-        z = chain.nearest(chain.n - 1 - step)
-        parts[z] = dot(mixed_ref[pl.ds(pl.multiple_of(z * rows, rows), rows)], weight_ref[...]).astype(low)
-        scatter.start_pair(z)
-        pl.when(step < chain.n - 1)(lambda: scatter.step(chain.n - 1 - step))
-
-    scatter.total(resid_ref)
-    resid_ref[...] += tokens_ref[...].astype(high)
-    ffn_ref[...] = norm_rows(resid_ref[...], gain_ref[...]).astype(low)
-    scatter.finish()
-
-
-def run_project(mixed, weight, tokens, gain, peers):
-    length, width = tokens.shape
-    n = peers // 2
-    return pl.pallas_call(
-        project_kernel,
-        out_shape=[
-            jax.ShapeDtypeStruct((length, width), high),
-            jax.ShapeDtypeStruct((length, width), low),
-        ],
-        in_specs=[VMEM] * 4,
-        out_specs=[VMEM] * 2,
-        scratch_shapes=[pltpu.VMEM((n, 2 * length, width), low)] + Scatter.buffers(n, length, width),
-        compiler_params=communicating(2),
-        cost_estimate=pl.CostEstimate(flops=0, bytes_accessed=64 << 20, transcendentals=0),
-        name="project_and_sum",
-    )(mixed, weight, tokens, gain)
-
-
-def expert_block(rows, cots, gate_w, up_w, down_w, gate_col, gated, grad_gate, grad_up, block):
+    )(tokens, gain, named, cotangent, query_weight, key_matrix, value_matrix)
+    return hidden, all_named, near, projection.reshape(width, columns), raw
+
+
+def attention_heads(
+    raw_ref, query_gain_ref, key_gain_ref, cos_ref, sin_ref, col_ref, row_ref,
+    mixed_ref, query_low_ref, key_low_ref, value_low_ref, inverse_ref, value_wide,
+):
+    head_size = cos_ref.shape[1]
+    heads = mixed_ref.shape[1] // head_size
+    key_raw = raw_ref[:, heads * head_size : (heads + 1) * head_size]
+    key_low_ref[...] = rotate(norm_rows(key_raw, key_gain_ref[...]), cos_ref[...], sin_ref[...]).astype(low)
+    value_low_ref[...] = raw_ref[:, (heads + 1) * head_size :].astype(low)
+    value_wide[:, :head_size] = value_low_ref[...]
+    value_wide[:, head_size:] = jnp.ones_like(value_low_ref)
+
+    @pl.loop(0, heads)
+    def each(head):
+        columns = pl.ds(pl.multiple_of(head * head_size, head_size), head_size)
+        rotated = rotate(norm_rows(raw_ref[:, columns], query_gain_ref[...]), cos_ref[...], sin_ref[...])
+        query_low_ref[:, columns] = (rotated * (head_size**-0.5 * log2e)).astype(low)
+        for begin, rows, first, keys in key_spans(raw_ref.shape[0]):
+            block = pl.ds(begin, rows)
+            scores = dot_last(query_low_ref[block, columns], key_low_ref[pl.ds(first, keys)])
+            allowed = tile_mask(col_ref, row_ref, begin, rows, first, keys)
+            terms = jnp.where(allowed, jnp.exp2(scores), 0.0).astype(low)
+            sums = dot(terms, value_wide[pl.ds(first, keys)])
+            inverse = 1.0 / sums[:, head_size:]
+            mixed_ref[block, columns] = (sums[:, :head_size] * inverse).astype(low)
+            inverse_ref[block, columns] = inverse
+
+
+class Split:
+    @staticmethod
+    def take(ref, z, half, columns=slice(None)):
+        block = ref[pl.ds(2 * z, 2), half, :, columns]
+        return block.reshape(block.shape[0] * block.shape[1], block.shape[2])
+
+    @staticmethod
+    def put(ref, z, half, value, columns=slice(None)):
+        ref[pl.ds(2 * z, 2), half, :, columns] = value.reshape(2, value.shape[0] // 2, value.shape[1])
+
+    @staticmethod
+    def every(ref, columns=slice(None)):
+        block = ref[:, :, :, columns]
+        return block.reshape(block.shape[0] * block.shape[1] * block.shape[2], block.shape[3])
+
+
+def expert_block(rows_all, plain_of, gate_w, up_w, gate_col, gated, grad_gate, grad_up, z, half):
     hidden = gate_w.shape[1]
     chunk = hidden // 3 if hidden % 384 == 0 else hidden
     gate_grad = jnp.zeros_like(gate_col)
     for begin in range(0, hidden, chunk):
         units = pl.ds(begin, chunk)
-        gate_pre = dot(rows[...], gate_w[:, units])
-        up_pre = dot(rows[...], up_w[:, units])
-        plain = dot_last(cots[...], down_w[units, :])
+        gate_pre = dot(Split.take(rows_all, z, half), gate_w[:, units])
+        up_pre = dot(Split.take(rows_all, z, half), up_w[:, units])
+        plain = plain_of(units)
         share = 1.0 / (1.0 + jnp.exp(-gate_pre))
         silu = gate_pre * share
         act = silu * up_pre
         gate_grad = gate_grad + jnp.sum(act * plain, axis=-1, keepdims=True)
-        gated[block, units] = (act * gate_col).astype(low)
+        Split.put(gated, z, half, (act * gate_col).astype(low), units)
         grad_act = plain * gate_col
         slope = share + silu * (1.0 - share)
-        grad_gate[block, units] = (grad_act * up_pre * slope).astype(low)
-        grad_up[block, units] = (grad_act * silu).astype(low)
+        Split.put(grad_gate, z, half, (grad_act * up_pre * slope).astype(low), units)
+        Split.put(grad_up, z, half, (grad_act * silu).astype(low), units)
     return gate_grad
 
 
@@ -674,7 +798,7 @@
         self.grads, self.stage, self.sems = grads, stage, sems
         self.sources = ((grad_gate, rows_all), (grad_up, rows_all), (gated, cots))
         self.groups = sems.shape[1]
-        self.hidden = gated.shape[1]
+        self.hidden = gated.shape[3]
         self.piece = self.hidden // self.groups
         self.tile = stage.shape[2]
 
@@ -702,7 +826,7 @@
             else:
                 wait_all(self.copies(kind, at, slot))
             span = pl.ds(pl.multiple_of(at * self.tile, self.tile), self.tile)
-            self.stage[slot] = dot_first(left[...], right[:, span]).astype(low)
+            self.stage[slot] = dot_first(Split.every(left), Split.every(right, span)).astype(low)
             for copy in self.copies(kind, at, slot):
                 copy.start()
 
@@ -711,308 +835,547 @@
             wait_all(self.copies(0, jnp.int32(slot), slot))
 
 
-def first_expert_kernel(
-    ffn_ref, named_ref, router_ref, cot_hbm, gate_hbm, up_hbm, down_hbm,
-    gates_ref, own_gates_ref, rows_hbm, mixture_hbm, parts_hbm, grads_hbm,
-    rows_all, cots, gate_w, up_w, down_w, gated, grad_gate, grad_up, mix_stage, part_stage, tile_stage,
-    load_sems, rows_sem, mix_sems, part_sems, tile_sems, gather_send, gather_recv, gather_local,
+def first_kernel(
+    query_gain_ref, key_gain_ref, row_ref, tokens_ref, gain_ref, named_ref, router_in, cot_ref, near_ref,
+    raw_hbm, cos_hbm, sin_hbm, col_hbm, weight_hbm, gate_hbm, up_hbm, down_hbm,
+    key_low_ref, value_low_ref, resid_ref, ffn_ref, gates_ref, own_gates_ref,
+    mixed_hbm, query_low_hbm, inverse_hbm, rows_hbm, cots_hbm, mixture_hbm, parts_hbm, grads_hbm,
+    raw_ref, cos_ref, sin_ref, col_ref, weight_ref, mixed_ref, query_low_ref, inverse_ref, value_wide, router_ref, plain, attn_parts, rows_all, cots, gate_w, up_w, down_w, gated, grad_gate, grad_up,
+    mix_stage, part_stage, tile_stage, load_sems, rows_sems, mix_sems, part_sems, tile_sems, cot_send, cot_recv, cot_local, *transfers,
 ):
     chain = Chain()
     n = chain.n
-    length, width = ffn_ref.shape
-    pair_rows = 2 * length
-    loads = [
-        pltpu.make_async_copy(source, target, load_sems.at[at])
-        for at, (source, target) in enumerate(
-            ((gate_hbm.at[0], gate_w), (up_hbm.at[0], up_w), (cot_hbm, cots), (down_hbm.at[0], down_w))
-        )
-    ]
-    for load in loads:
-        load.start()
-    chain.greet()
-    gather = Gather(chain, ffn_ref, rows_all, gather_send, gather_recv, gather_local)
-    gather.begin()
-    gather.keep().wait()
-    for load in loads:
-        load.wait()
-    lanes = lax.broadcasted_iota(jnp.int32, (pair_rows, 128), 1)
-    expert = lax.axis_index("expert") * gate_hbm.shape[0]
-    tile = tile_stage.shape[2]
-
-    def mix_copy(z, slot):
-        target = mixture_hbm.at[pl.ds(pl.multiple_of(z * pair_rows, pair_rows), pair_rows)]
-        return pltpu.make_async_copy(mix_stage.at[slot], target, mix_sems.at[slot])
-
-    def part_copy(z, slot):
-        return pltpu.make_async_copy(part_stage.at[slot], parts_hbm.at[z], part_sems.at[slot])
-
-    @pl.loop(0, n)
-    def each(step):
-        pl.when(step > 0)(lambda: gather.service(step))
-        z = chain.nearest(step)
-        gather.wait_sibling(z)
-        block = pl.ds(pl.multiple_of(z * pair_rows, pair_rows), pair_rows)
-        rows = rows_all.at[block]
-        logits = dot_last(rows[...], router_ref[...])
-        named = named_ref[block].astype(high) > 0.5
-        top = jnp.max(jnp.where(named, logits, -1e30), axis=-1, keepdims=True)
-        terms = jnp.where(named, jnp.exp(jnp.where(named, logits - top, 0.0)), 0.0)
-        gates = terms / jnp.sum(terms, axis=-1, keepdims=True)
-        gates_ref[block] = gates
-
-        @pl.when(step == 0)
-        def own_gates():
-            own_gates_ref[...] = jnp.where(chain.c == 0, gates[:length], gates[length:])
-
-        gate_col = jnp.sum(jnp.where(lanes == expert, gates, 0.0), axis=-1, keepdims=True)
-        gate_grad = expert_block(
-            rows, cots.at[block], gate_w, up_w, down_w, gate_col, gated, grad_gate, grad_up, block
-        )
-        slot = step % 2
-
-        @pl.when(step >= 2)
-        def free():
-            mix_copy(z, slot).wait()
-            part_copy(z, slot).wait()
-
-        @pl.loop(0, width // tile)
-        def columns(at):
-            span = pl.ds(pl.multiple_of(at * tile, tile), tile)
-            mix_stage[slot, :, span] = dot(gated[block], down_w[:, span]).astype(low)
-            grad_rows = dot_last(grad_gate[block], gate_w[span, :]) + dot_last(grad_up[block], up_w[span, :])
-            part_stage[slot, :, span] = grad_rows.astype(low)
-
-        part_stage[slot, :, width:] = gate_columns(lanes, expert, gate_grad).astype(low)
-        mix_copy(z, slot).start()
-        part_copy(z, slot).start()
-
-    rows_copy = pltpu.make_async_copy(rows_all, rows_hbm, rows_sem)
-    rows_copy.start()
-    tiles = Tiles(grads_hbm, tile_stage, tile_sems, gated, grad_gate, grad_up, rows_all, cots)
-    for kind in range(3):
-        tiles.run(kind)
-    gather.finish()
-    tiles.finish()
-    for slot in range(2):
-        mix_copy(jnp.int32(0), slot).wait()
-        part_copy(jnp.int32(0), slot).wait()
-    rows_copy.wait()
-
-
-def second_expert_kernel(
-    gates_ref, rows_hbm, cot_hbm, gate_hbm, up_hbm, down_hbm, mixture_in, parts_in,
-    sum_ref, mixture_hbm, grads_hbm,
-    rows_all, cots, gate_w, up_w, down_w, gated, grad_gate, grad_up, mixture, parts, tile_stage,
-    load_sems, mix_sems, tile_sems, pair, flow, *scatter_sems,
-):
-    chain = Chain()
-    n = chain.n
-    pair_rows, width = parts.shape[1], rows_all.shape[1]
+    _, _, rows, width = rows_all.shape
+    block_rows = 2 * rows
     loads = [
         pltpu.make_async_copy(source, target, load_sems.at[at])
         for at, (source, target) in enumerate(
             (
-                (rows_hbm, rows_all), (gate_hbm.at[1], gate_w), (up_hbm.at[1], up_w), (cot_hbm, cots),
-                (down_hbm.at[1], down_w), (parts_in, parts), (mixture_in, mixture),
+                (raw_hbm, raw_ref), (cos_hbm, cos_ref), (sin_hbm, sin_ref), (col_hbm, col_ref),
+                (weight_hbm, weight_ref), (down_hbm.at[0], down_w), (gate_hbm.at[0], gate_w),
+                (up_hbm.at[0], up_w),
             )
         )
     ]
     for load in loads:
         load.start()
     chain.greet()
-    scatter = Scatter(chain, parts, pair, flow, *scatter_sems)
-    lanes = lax.broadcasted_iota(jnp.int32, (pair_rows, 128), 1)
-    expert = lax.axis_index("expert") * gate_hbm.shape[0] + 1
+    cot_gather = NearGather(
+        chain, cot_ref, near_ref, lambda z, c: cots.at[2 * z + c], cot_send, cot_recv, cot_local
+    )
+    cot_gather.begin()
+    wait_all(loads[:4])
+    router_ref[...] = jnp.zeros_like(router_ref)
+    router_ref[: router_in.shape[0]] = router_in[...]
+    attention_heads(
+        raw_ref, query_gain_ref, key_gain_ref, cos_ref, sin_ref, col_ref, row_ref,
+        mixed_ref, query_low_ref, key_low_ref, value_low_ref, inverse_ref, value_wide,
+    )
+    attention_copies = [
+        pltpu.make_async_copy(source, target, rows_sems.at[2 + at])
+        for at, (source, target) in enumerate(
+            ((mixed_ref, mixed_hbm), (query_low_ref, query_low_hbm), (inverse_ref, inverse_hbm))
+        )
+    ]
+    for copy in attention_copies:
+        copy.start()
+    loads[4].wait()
+    scatters, gathers = [], []
+    for half in range(2):
+        pair, flow, *rest = transfers[9 * half : 9 * half + 9]
+        scatters.append(
+            Scatter(chain, lambda z, c, half=half: attn_parts.at[z, c, half], pair, flow, *rest[:4])
+        )
+        gathers.append(
+            Gather(chain, ffn_ref.at[half], lambda z, c, half=half: rows_all.at[2 * z + c, half], *rest[4:])
+        )
+
+    def plain_rows(step):
+        z = chain.nearest(step)
+        pl.when(step == 0)(cot_gather.wait_placed)
+        pl.when(step > 0)(lambda: cot_gather.wait_sibling(z))
+        cot_rows = cots[pl.ds(2 * z, 2)].reshape(4 * rows, width)
+        hidden = plain.shape[3]
+        plain[pl.ds(2 * z, 2)] = dot_last(cot_rows, down_w[...]).reshape(2, 2, rows, hidden)
+
+    @pl.loop(0, n)
+    def project(step):
+        z = chain.nearest(n - 1 - step)
+        tokens = pl.ds(pl.multiple_of(z * 4 * rows, 4 * rows), 4 * rows)
+        attn_parts[z] = dot(mixed_ref[tokens], weight_ref[...]).astype(low).reshape(2, 2, rows, width)
+        for scatter in scatters:
+            scatter.start_pair(z)
+        pl.when(step < n - 1)(lambda: scatters[0].step(n - 1 - step))
+        pl.when(step == 0)(lambda: loads[5].wait())
+        pl.when(step == 1)(lambda: cot_gather.service(2))
+        pl.when(step < n - 1)(lambda: plain_rows(step))
+
+    def own_rows(half):
+        span = pl.ds(half * rows, rows)
+        scatters[half].total(resid_ref.at[span])
+        resid_ref[span] += tokens_ref[span].astype(high)
+        ffn_ref[half] = norm_rows(resid_ref[span], gain_ref[...]).astype(low)
+        gathers[half].begin()
+
+    scatters[1].step(n - 1)
+    own_rows(0)
+    cot_gather.service(3)
+    plain_rows(jnp.int32(3))
+    lanes = lax.broadcasted_iota(jnp.int32, (block_rows, 128), 1)
+    expert = lax.axis_index("expert") * gate_hbm.shape[0]
     tile = tile_stage.shape[2]
-    for load in loads:
-        load.wait()
-
-    def mix_copy(z):
-        block = pl.ds(pl.multiple_of(z * pair_rows, pair_rows), pair_rows)
-        return pltpu.make_async_copy(mixture.at[block], mixture_hbm.at[block], mix_sems.at[z])
-
-    @pl.loop(0, n)
-    def each(step):
-        z = chain.nearest(n - 1 - step)
-        block = pl.ds(pl.multiple_of(z * pair_rows, pair_rows), pair_rows)
-        gate_col = jnp.sum(jnp.where(lanes == expert, gates_ref[block], 0.0), axis=-1, keepdims=True)
+    wait_all(loads[6:])
+
+    def mix_copy(z, half, slot):
+        return pltpu.make_async_copy(mix_stage.at[slot], mixture_hbm.at[pl.ds(2 * z, 2), half], mix_sems.at[slot])
+
+    def part_copy(z, half, slot):
+        return pltpu.make_async_copy(part_stage.at[slot], parts_hbm.at[pl.ds(2 * z, 2), half], part_sems.at[slot])
+
+    @pl.loop(0, 2 * n)
+    def each(turn):
+        for step in range(1, n - 1):
+
+            @pl.when(turn == step)
+            def early():
+                scatters[1].step(n - 1 - step)
+                gathers[0].service(step)
+
+        @pl.when(turn == n - 1)
+        def middle():
+            own_rows(1)
+            gathers[0].service(n - 1)
+
+        pl.when((turn >= n) & (turn < 2 * n - 1))(lambda: gathers[1].service(turn - n + 1))
+        half, step = turn // n, turn % n
+        z = chain.nearest(step)
+
+        def arrived(gather):
+            pl.when(step == 0)(lambda: gather.keep().wait())
+            gather.wait_sibling(z)
+
+        pl.when(half == 0)(lambda: arrived(gathers[0]))
+        pl.when(half == 1)(lambda: arrived(gathers[1]))
+        logits = dot_last(Split.take(rows_all, z, half), router_ref[...])
+        named = Split.take(named_ref, z, half).astype(high) > 0.5
+        top = jnp.max(jnp.where(named, logits, -1e30), axis=-1, keepdims=True)
+        terms = jnp.where(named, jnp.exp(jnp.where(named, logits - top, 0.0)), 0.0)
+        gates = terms / jnp.sum(terms, axis=-1, keepdims=True)
+        Split.put(gates_ref, z, half, gates)
+
+        @pl.when(step == 0)
+        def own_gates():
+            own_gates_ref[half] = jnp.where(chain.c == 0, gates[:rows], gates[rows:])
+
+        gate_col = jnp.sum(jnp.where(lanes == expert, gates, 0.0), axis=-1, keepdims=True)
         gate_grad = expert_block(
-            rows_all.at[block], cots.at[block], gate_w, up_w, down_w, gate_col, gated, grad_gate, grad_up, block
+            rows_all, lambda units: Split.take(plain, z, half, units), gate_w, up_w, gate_col, gated, grad_gate,
+            grad_up, z, half,
         )
+        slot = turn % 2
+
+        @pl.when(turn >= 2)
+        def free():
+            mix_copy(z, half, slot).wait()
+            part_copy(z, half, slot).wait()
 
         @pl.loop(0, width // tile)
         def columns(at):
             span = pl.ds(pl.multiple_of(at * tile, tile), tile)
-            grad_rows = dot_last(grad_gate[block], gate_w[span, :]) + dot_last(grad_up[block], up_w[span, :])
-            parts[z, :, span] = (parts[z, :, span].astype(high) + grad_rows).astype(low)
-
-        columns_sent = gate_columns(lanes, expert, gate_grad)
-        parts[z, :, width:] = (parts[z, :, width:].astype(high) + columns_sent).astype(low)
-        scatter.start_pair(z)
-
-        @pl.loop(0, width // tile)
-        def mixture_columns(at):
-            span = pl.ds(pl.multiple_of(at * tile, tile), tile)
-            added = dot(gated[block], down_w[:, span])
-            mixture[block, span] = (mixture[block, span].astype(high) + added).astype(low)
-
-        mix_copy(z).start()
-        pl.when(step < n - 1)(lambda: scatter.step(n - 1 - step))
-
+            mixture = dot(Split.take(gated, z, half), down_w[:, span])
+            mix_stage[slot, :, :, span] = mixture.astype(low).reshape(2, rows, tile)
+            grad_rows = dot_last(Split.take(grad_gate, z, half), gate_w[span, :])
+            grad_rows = grad_rows + dot_last(Split.take(grad_up, z, half), up_w[span, :])
+            part_stage[slot, :, :, span] = grad_rows.astype(low).reshape(2, rows, tile)
+
+        sent = gate_columns(lanes, expert, gate_grad).astype(low)
+        part_stage[slot, :, :, width:] = sent.reshape(2, rows, 128)
+        mix_copy(z, half, slot).start()
+        part_copy(z, half, slot).start()
+
+    whole_copies = [
+        pltpu.make_async_copy(rows_all, rows_hbm, rows_sems.at[0]),
+        pltpu.make_async_copy(cots, cots_hbm, rows_sems.at[1]),
+    ]
+    for copy in whole_copies:
+        copy.start()
     tiles = Tiles(grads_hbm, tile_stage, tile_sems, gated, grad_gate, grad_up, rows_all, cots)
     for kind in range(3):
         tiles.run(kind)
-    scatter.total(sum_ref)
+    for half in range(2):
+        gathers[half].finish()
+        scatters[half].finish()
     tiles.finish()
-    for z in range(n):
-        mix_copy(jnp.int32(z)).wait()
-    scatter.finish()
-
-
-def run_experts(ffn, named, router, cotangents, gate_weight, up_weight, down_weight, peers, groups):
-    length, width = ffn.shape
-    n = peers // 2
-    full = length * peers
-    _, _, hidden = gate_weight.shape
-    tile = width // groups
-    sent = width + 128
-    dma = pltpu.SemaphoreType.DMA
-    rows = pltpu.VMEM((full, width), low)
-    weights = [
+    for slot in range(2):
+        mix_copy(jnp.int32(0), 0, slot).wait()
+        part_copy(jnp.int32(0), 0, slot).wait()
+    wait_all(whole_copies + attention_copies)
+    cot_gather.finish()
+
+
+def second_kernel(
+    gates_ref, rows_hbm, cot_hbm, gate_hbm, up_hbm, down_hbm, mixture_in, parts_in, own_gates_ref, ffn_ref,
+    resid_ref, cot_ref, gain_ref, router_in, weight_ref,
+    mixture_hbm, grads_hbm, grad_resid_ref, attn_hbm, mixed_ref, router_grad_ref, gain_grad_ref,
+    rows_all, cots, gate_w, up_w, down_w, gated, grad_gate, grad_up, mixture, parts, tile_stage, attn_all, own,
+    sums, router_ref, load_sems, chip_sems, mix_sems, tile_sems, attn_sem, *transfers,
+):
+    chain = Chain()
+    n = chain.n
+    _, _, rows, width = rows_all.shape
+    block_rows = 2 * rows
+    loads = [
+        pltpu.make_async_copy(source, target, load_sems.at[at])
+        for at, (source, target) in enumerate(
+            (
+                (gate_hbm.at[1], gate_w), (up_hbm.at[1], up_w), (down_hbm.at[1], down_w), (parts_in, parts),
+                (mixture_in, mixture),
+            )
+        )
+    ]
+
+    def chip_loads(z):
+        block = pl.ds(2 * z, 2)
+        return [
+            pltpu.make_async_copy(rows_hbm.at[block], rows_all.at[block], chip_sems.at[0, z]),
+            pltpu.make_async_copy(cot_hbm.at[block], cots.at[block], chip_sems.at[1, z]),
+        ]
+
+    for load in loads[:3]:
+        load.start()
+    for step in range(n):
+        for load in chip_loads(chain.nearest(n - 1 - step)):
+            load.start()
+    for load in loads[3:]:
+        load.start()
+    chain.greet()
+    scatters, gathers = [], []
+    for half in range(2):
+        pair, flow, *rest = transfers[9 * half : 9 * half + 9]
+        scatters.append(Scatter(chain, lambda z, c, half=half: parts.at[2 * z + c, half], pair, flow, *rest[:4]))
+        gathers.append(
+            Gather(chain, own.at[half], lambda z, c, half=half: attn_all.at[2 * z + c, half], *rest[4:])
+        )
+    lanes = lax.broadcasted_iota(jnp.int32, (block_rows, 128), 1)
+    expert = lax.axis_index("expert") * gate_hbm.shape[0] + 1
+    tile = tile_stage.shape[2]
+    router_ref[...] = jnp.zeros_like(router_ref)
+    router_ref[: router_in.shape[0]] = router_in[...]
+    wait_all(loads[:3])
+
+    def mix_copy(z, half):
+        block = pl.ds(2 * z, 2)
+        return pltpu.make_async_copy(mixture.at[block, half], mixture_hbm.at[block, half], mix_sems.at[half, z])
+
+    def own_rows(half):
+        scatters[half].total(sums)
+        span = pl.ds(half * rows, rows)
+        sent = sums[:, width:]
+        left = lax.broadcasted_iota(jnp.int32, sent.shape, 1) < 64
+        grad_gates = jnp.where(left, sent + pltpu.roll(sent, 64, 1), 0.0)
+        gates = own_gates_ref[half]
+        inner = jnp.sum(gates * grad_gates, axis=-1, keepdims=True)
+        grad_logits = (gates * (grad_gates - inner)).astype(low)
+        router_grad = dot_first(grad_logits, ffn_ref[half])[: router_grad_ref.shape[0]]
+        grad_hidden = sums[:, :width] + dot(grad_logits, router_ref[...])
+        grad_rows, gain_rows = norm_back(resid_ref[span], gain_ref[...], grad_hidden)
+        gain_grad = jnp.broadcast_to(jnp.sum(gain_rows, axis=0, keepdims=True), gain_grad_ref.shape)
+        grad_resid = cot_ref[span].astype(high) + grad_rows
+        grad_resid_ref[span] = grad_resid
+        own[half] = grad_resid.astype(low)
+        gathers[half].begin()
+        if half == 0:
+            router_grad_ref[...] = router_grad
+            gain_grad_ref[...] = gain_grad
+        else:
+            router_grad_ref[...] += router_grad
+            gain_grad_ref[...] += gain_grad
+
+    @pl.loop(0, 2 * n)
+    def each(turn):
+        half, step = turn // n, turn % n
+        z = chain.nearest(n - 1 - step)
+        pl.when(half == 0)(lambda: wait_all(chip_loads(z)))
+        gates = Split.take(gates_ref, z, half)
+        gate_col = jnp.sum(jnp.where(lanes == expert, gates, 0.0), axis=-1, keepdims=True)
+        gate_grad = expert_block(
+            rows_all, lambda units: dot_last(Split.take(cots, z, half), down_w[units, :]), gate_w, up_w, gate_col,
+            gated, grad_gate, grad_up, z, half,
+        )
+
+        pl.when(turn == 0)(lambda: loads[3].wait())
+
+        @pl.loop(0, width // tile)
+        def columns(at):
+            span = pl.ds(pl.multiple_of(at * tile, tile), tile)
+            grad_rows = dot_last(Split.take(grad_gate, z, half), gate_w[span, :])
+            grad_rows = grad_rows + dot_last(Split.take(grad_up, z, half), up_w[span, :])
+            Split.put(parts, z, half, (Split.take(parts, z, half, span).astype(high) + grad_rows).astype(low), span)
+
+        last = pl.ds(width, 128)
+        sent = Split.take(parts, z, half, last).astype(high) + gate_columns(lanes, expert, gate_grad)
+        Split.put(parts, z, half, sent.astype(low), last)
+        pl.when(half == 0)(lambda: scatters[0].start_pair(z))
+        pl.when(half == 1)(lambda: scatters[1].start_pair(z))
+
+        pl.when(turn < n - 1)(lambda: scatters[0].step(n - 1 - step))
+        pl.when((turn >= n) & (turn < 2 * n - 1))(lambda: scatters[1].step(n - 1 - step))
+        pl.when(turn == n)(lambda: own_rows(0))
+        pl.when(turn > n)(lambda: gathers[0].service(turn - n))
+
+    tiles = Tiles(grads_hbm, tile_stage, tile_sems, gated, grad_gate, grad_up, rows_all, cots)
+    own_rows(1)
+    for step in range(1, n):
+        if step <= 3:
+            tiles.run(step - 1)
+        gathers[1].service(step)
+    for kind in range(n - 1, 3):
+        tiles.run(kind)
+    loads[4].wait()
+
+    @pl.loop(0, 2 * n)
+    def mixture_rows(turn):
+        half, z = turn // n, turn % n
+
+        @pl.loop(0, width // tile)
+        def columns(at):
+            span = pl.ds(pl.multiple_of(at * tile, tile), tile)
+            added = dot(Split.take(gated, z, half), down_w[:, span])
+            Split.put(mixture, z, half, (Split.take(mixture, z, half, span).astype(high) + added).astype(low), span)
+
+        mix_copy(z, half).start()
+
+    @pl.loop(0, 2 * n)
+    def mixed_rows(turn):
+        half, z = turn // n, turn % n
+        pl.when(half == 0)(lambda: gathers[0].wait_sibling(z))
+        pl.when(half == 1)(lambda: gathers[1].wait_sibling(z))
+
+        @pl.when(z == chain.z)
+        def mine():
+            pl.when(half == 0)(lambda: gathers[0].keep().wait())
+            pl.when(half == 1)(lambda: gathers[1].keep().wait())
+
+        result = dot_last(Split.take(attn_all, z, half), weight_ref[...])
+        Split.put(mixed_ref, z, half, result.astype(low))
+
+    attn_copy = pltpu.make_async_copy(attn_all, attn_hbm, attn_sem)
+    attn_copy.start()
+    for half in range(2):
+        gathers[half].finish()
+        scatters[half].finish()
+        for z in range(n):
+            mix_copy(jnp.int32(z), half).wait()
+    tiles.finish()
+    attn_copy.wait()
+
+
+def split_rows(array, peers):
+    return array.reshape(peers, 2, array.shape[0] // (2 * peers), array.shape[1])
+
+
+def expert_scratch(gate_weight, up_weight, down_weight, peers, rows, width):
+    hidden = gate_weight.shape[2]
+    whole = pltpu.VMEM((peers, 2, rows, width), low)
+    acts = pltpu.VMEM((peers, 2, rows, hidden), low)
+    return [
+        whole, whole,
         pltpu.VMEM(gate_weight.shape[1:], low),
         pltpu.VMEM(up_weight.shape[1:], low),
         pltpu.VMEM(down_weight.shape[1:], low),
+        acts, acts, acts,
     ]
-    acts = [pltpu.VMEM((full, hidden), low)] * 3
-    grads_shape = jax.ShapeDtypeStruct((groups, 3 * hidden, tile), low)
-    mixture_shape = jax.ShapeDtypeStruct((full, width), low)
-    stage = pltpu.VMEM((2, hidden, tile), low)
-    gates, own_gates, rows_all, mixture, parts, grads = pl.pallas_call(
-        first_expert_kernel,
+
+
+def run_first(
+    raw, query_gain, key_gain, cosines, sines, seg_col, seg_row, weight, tokens, gain, named, router, cotangent, near, gate_weight, up_weight, down_weight,
+    peers, groups,
+):
+    length, width = tokens.shape
+    n, rows = peers // 2, length // 2
+    hidden = gate_weight.shape[2]
+    tile, sent = width // groups, width + 128
+    full, local_width, head_size = length * peers, weight.shape[0], cosines.shape[1]
+    dma = pltpu.SemaphoreType.DMA
+
+    def split(columns, dtype):
+        return jax.ShapeDtypeStruct((peers, 2, rows, columns), dtype)
+
+    return pl.pallas_call(
+        first_kernel,
         out_shape=[
-            jax.ShapeDtypeStruct((full, 128), high),
-            jax.ShapeDtypeStruct((length, 128), high),
-            jax.ShapeDtypeStruct((full, width), low),
-            mixture_shape,
-            jax.ShapeDtypeStruct((n, 2 * length, sent), low),
-            grads_shape,
+            jax.ShapeDtypeStruct((full, head_size), low),
+            jax.ShapeDtypeStruct((full, head_size), low),
+            jax.ShapeDtypeStruct((length, width), high),
+            jax.ShapeDtypeStruct((2, rows, width), low),
+            split(128, high),
+            jax.ShapeDtypeStruct((2, rows, 128), high),
+            jax.ShapeDtypeStruct((full, local_width), low),
+            jax.ShapeDtypeStruct((full, local_width), low),
+            jax.ShapeDtypeStruct((full, local_width), high),
+            split(width, low),
+            split(width, low),
+            split(width, low),
+            split(sent, low),
+            jax.ShapeDtypeStruct((groups, 3 * hidden, tile), low),
         ],
-        in_specs=[VMEM, VMEM, VMEM, ANY, ANY, ANY, ANY],
-        out_specs=[VMEM, VMEM, ANY, ANY, ANY, ANY],
+        in_specs=[VMEM] * 9 + [ANY] * 8,
+        out_specs=[VMEM] * 6 + [ANY] * 8,
         scratch_shapes=[
-            rows, rows, *weights, *acts,
-            pltpu.VMEM((2, 2 * length, width), low),
-            pltpu.VMEM((2, 2 * length, sent), low),
-            stage,
-            dma((4,)), dma(()), dma((2,)), dma((2,)), dma((2, groups)),
-            *Gather.semaphores(n),
+            pltpu.VMEM(raw.shape, high),
+            pltpu.VMEM(cosines.shape, high),
+            pltpu.VMEM(sines.shape, high),
+            pltpu.VMEM(seg_col.shape, jnp.int32),
+            pltpu.VMEM(weight.shape, low),
+            pltpu.VMEM((full, local_width), low),
+            pltpu.VMEM((full, local_width), low),
+            pltpu.VMEM((full, local_width), high),
+            pltpu.VMEM((full, 2 * head_size), low),
+            pltpu.VMEM((128, width), low),
+            pltpu.VMEM((peers, 2, rows, hidden), high),
+            pltpu.VMEM((n, 2, 2, rows, width), low),
+            *expert_scratch(gate_weight, up_weight, down_weight, peers, rows, width),
+            pltpu.VMEM((2, 2, rows, width), low),
+            pltpu.VMEM((2, 2, rows, sent), low),
+            pltpu.VMEM((2, hidden, tile), low),
+            dma((8,)), dma((5,)), dma((2,)), dma((2,)), dma((2, groups)),
+            *NearGather.semaphores(n),
+            *(Scatter.buffers(n, rows, width) + Gather.semaphores(n)) * 2,
         ],
         compiler_params=communicating(3),
         cost_estimate=pl.CostEstimate(flops=0, bytes_accessed=120 << 20, transcendentals=0),
-        name="first_expert",
-    )(ffn, named, router, cotangents, gate_weight, up_weight, down_weight)
-    sums, mixture, more_grads = pl.pallas_call(
-        second_expert_kernel,
-        out_shape=[jax.ShapeDtypeStruct((length, sent), high), mixture_shape, grads_shape],
-        in_specs=[VMEM] + [ANY] * 7,
-        out_specs=[VMEM, ANY, ANY],
+        name="attention_and_first_expert",
+    )(
+        query_gain, key_gain, seg_row, tokens, gain, split_rows(named.reshape(-1, 128), peers), router,
+        cotangent.reshape(2, rows, width), near.reshape(3, 2, rows, width), raw, cosines, sines, seg_col, weight,
+        gate_weight, up_weight, down_weight,
+    )
+
+
+def run_second(
+    gates, rows_all, cotangents, gate_weight, up_weight, down_weight, mixture, parts, own_gates, ffn, resid,
+    cotangent, gain, router, weight, experts, peers, groups,
+):
+    length, width = resid.shape
+    n, rows = peers // 2, length // 2
+    full = length * peers
+    hidden = gate_weight.shape[2]
+    tile, sent = width // groups, width + 128
+    mixed_width = weight.shape[0]
+    dma = pltpu.SemaphoreType.DMA
+
+    def split(columns, dtype):
+        return jax.ShapeDtypeStruct((peers, 2, rows, columns), dtype)
+
+    mixture, grads, grad_resid, grad_attn, grad_mixed, grad_router, gain_grad = pl.pallas_call(
+        second_kernel,
+        out_shape=[
+            split(width, low),
+            jax.ShapeDtypeStruct((groups, 3 * hidden, tile), low),
+            jax.ShapeDtypeStruct((length, width), high),
+            split(width, low),
+            split(mixed_width, low),
+            jax.ShapeDtypeStruct((experts, width), high),
+            jax.ShapeDtypeStruct((8, width), high),
+        ],
+        in_specs=[VMEM] + [ANY] * 7 + [VMEM] * 7,
+        out_specs=[ANY, ANY, VMEM, ANY, VMEM, VMEM, VMEM],
         scratch_shapes=[
-            rows, rows, *weights, *acts,
-            rows,
-            pltpu.VMEM((n, 2 * length, sent), low),
-            stage,
-            dma((7,)), dma((n,)), dma((2, groups)),
-            *Scatter.buffers(n, length, sent),
+            *expert_scratch(gate_weight, up_weight, down_weight, peers, rows, width),
+            pltpu.VMEM((peers, 2, rows, width), low),
+            pltpu.VMEM((peers, 2, rows, sent), low),
+            pltpu.VMEM((2, hidden, tile), low),
+            pltpu.VMEM((peers, 2, rows, width), low),
+            pltpu.VMEM((2, rows, width), low),
+            pltpu.VMEM((rows, sent), high),
+            pltpu.VMEM((128, width), low),
+            dma((5,)), dma((2, n)), dma((2, n)), dma((2, groups)), dma(()),
+            *(Scatter.buffers(n, rows, sent) + Gather.semaphores(n)) * 2,
         ],
         compiler_params=communicating(7),
         cost_estimate=pl.CostEstimate(flops=0, bytes_accessed=120 << 20, transcendentals=0),
-        name="second_expert",
-    )(gates, rows_all, cotangents, gate_weight, up_weight, down_weight, mixture, parts)
-    return sums, own_gates, mixture, grads, more_grads
-
-
-def turn_kernel(
-    sum_ref, gates_ref, ffn_ref, resid_ref, cot_ref, gain_ref, router_ref, weight_ref,
-    grad_resid_ref, attn_ref, mixed_ref, router_grad_ref, gain_grad_ref,
-    own, gather_send, gather_recv, gather_local,
+        name="second_expert_and_turn",
+    )(
+        gates, rows_all, cotangents, gate_weight, up_weight, down_weight, mixture, parts,
+        own_gates, ffn, resid, cotangent, gain, router, weight,
+    )
+    return (
+        mixture.reshape(full, width), grads, grad_resid, grad_attn.reshape(full, width),
+        grad_mixed.reshape(full, mixed_width), grad_router, gain_grad,
+    )
+
+
+def attention_heads_backward(
+    raw_ref, query_low_ref, key_low_ref, value_low_ref, inverse_ref, mixed_ref, grad_mixed_ref, query_gain_ref,
+    cos_ref, sin_ref, col_ref, row_ref, grad_query_ref, grad_key_ref, grad_value_ref, grad_gain_ref,
+):
+    length, head_size = key_low_ref.shape
+    heads = query_low_ref.shape[1] // head_size
+    grad_key_ref[...] = jnp.zeros_like(grad_key_ref)
+    grad_value_ref[...] = jnp.zeros_like(grad_value_ref)
+    grad_gain_ref[...] = jnp.zeros_like(grad_gain_ref)
+
+    @pl.loop(0, heads)
+    def each(head):
+        columns = pl.ds(pl.multiple_of(head * head_size, head_size), head_size)
+        for begin, rows, first, keys in key_spans(length):
+            block, span = pl.ds(begin, rows), pl.ds(first, keys)
+            query_low = query_low_ref[block, columns]
+            key_low = key_low_ref[span]
+            scaled = grad_mixed_ref[block, columns].astype(high) * inverse_ref[block, columns]
+            row_term = jnp.sum(scaled * mixed_ref[block, columns].astype(high), axis=-1, keepdims=True)
+            scaled = scaled.astype(low)
+            scores = dot_last(query_low, key_low)
+            allowed = tile_mask(col_ref, row_ref, begin, rows, first, keys)
+            terms = jnp.where(allowed, jnp.exp2(scores), 0.0)
+            grad_probs = dot_last(scaled, value_low_ref[span])
+            grad_scores = (terms * (grad_probs - row_term)).astype(low)
+            grad_value_ref[span] += dot_first(terms.astype(low), scaled)
+            grad_key_ref[span] += dot_first(grad_scores, query_low) * (1.0 / log2e)
+            grad_rotated = dot(grad_scores, key_low) * head_size**-0.5
+            grad_normed = unrotate(grad_rotated, cos_ref[block], sin_ref[block])
+            grad_raw, gain_rows = norm_back(raw_ref[block, columns], query_gain_ref[...], grad_normed)
+            grad_query_ref[block, columns] = grad_raw.astype(low)
+            grad_gain_ref[...] += jnp.broadcast_to(
+                jnp.sum(gain_rows, axis=0, keepdims=True), grad_gain_ref.shape
+            )
+
+
+def input_kernel(
+    query_gain_ref, key_gain_ref, row_ref, tokens_ref, gain_ref,
+    raw_hbm, query_low_hbm, key_low_hbm, value_low_hbm, inverse_hbm, mixed_hbm, grad_mixed_hbm, cos_hbm, sin_hbm,
+    col_hbm, projection_hbm, attn_hbm, hidden_hbm, resid_hbm,
+    input_grad_ref, gain_grad_ref, query_gain_grad_ref, key_gain_grad_ref, projection_grad_hbm, out_grad_hbm,
+    raw_ref, query_low_ref, key_low_ref, value_low_ref, inverse_ref, mixed_ref, grad_mixed_ref, cos_ref, sin_ref,
+    col_ref, projection_ref, attn_ref, hidden_ref, resid_ref,
+    own_pair, their_pair, key_part, value_part, columns, weight, total, parts, projection_grad, out_grad,
+    load_sems, store_sems, swap_send, swap_recv, pair, flow, *scatter_sems,
 ):
     chain = Chain()
     n = chain.n
-    length, width = ffn_ref.shape
-    sent = sum_ref[:, width:]
-    grad_gates = jnp.where(
-        lax.broadcasted_iota(jnp.int32, sent.shape, 1) < 64, sent + pltpu.roll(sent, 64, 1), 0.0
-    )
-    gates = gates_ref[...]
-    inner = jnp.sum(gates * grad_gates, axis=-1, keepdims=True)
-    grad_logits = (gates * (grad_gates - inner)).astype(low)
-    router_grad_ref[...] = dot_first(grad_logits, ffn_ref[...])[: router_grad_ref.shape[0]]
-    grad_hidden = sum_ref[:, :width] + dot(grad_logits, router_ref[...])
-    grad_rows, gain_rows = norm_back(resid_ref[...], gain_ref[...], grad_hidden)
-    gain_grad_ref[...] = jnp.broadcast_to(jnp.sum(gain_rows, axis=0, keepdims=True), gain_grad_ref.shape)
-    grad_resid = cot_ref[...].astype(high) + grad_rows
-    grad_resid_ref[...] = grad_resid
-    own[...] = grad_resid.astype(low)
-    chain.greet()
-    gather = Gather(chain, own, attn_ref, gather_send, gather_recv, gather_local)
-    gather.begin()
-    gather.keep().wait()
-    pair_rows = 2 * length
-
-    @pl.loop(0, n)
-    def each(step):
-        pl.when(step > 0)(lambda: gather.service(step))
-        z = chain.nearest(step)
-        gather.wait_sibling(z)
-        block = pl.ds(pl.multiple_of(z * pair_rows, pair_rows), pair_rows)
-        mixed_ref[block] = dot_last(attn_ref[block], weight_ref[...]).astype(low)
-
-    gather.finish()
-
-
-def run_turn(sums, gates, ffn, resid, cotangent, gain, router, weight, experts, peers):
-    length, width = ffn.shape
-    n = peers // 2
-    full = length * peers
-    return pl.pallas_call(
-        turn_kernel,
-        out_shape=[
-            jax.ShapeDtypeStruct((length, width), high),
-            jax.ShapeDtypeStruct((full, width), low),
-            jax.ShapeDtypeStruct((full, weight.shape[0]), low),
-            jax.ShapeDtypeStruct((experts, width), high),
-            jax.ShapeDtypeStruct((8, width), high),
-        ],
-        in_specs=[VMEM] * 8,
-        out_specs=[VMEM] * 5,
-        scratch_shapes=[pltpu.VMEM((length, width), low), *Gather.semaphores(n)],
-        compiler_params=communicating(4),
-        cost_estimate=pl.CostEstimate(flops=0, bytes_accessed=64 << 20, transcendentals=0),
-        name="turn_to_attention",
-    )(sums, gates, ffn, resid, cotangent, gain, router, weight)
-
-
-def input_kernel(
-    key_part_ref, value_part_ref, raw_ref, key_gain_ref, cos_ref, sin_ref, grad_query_ref, projection_ref,
-    hidden_ref, mixed_ref, attn_ref, grad_resid_ref, tokens_ref, gain_ref,
-    input_grad_ref, projection_grad_ref, out_grad_ref, gain_grad_ref, key_gain_grad_ref,
-    own_pair, their_pair, columns, weight, total, parts, hidden_all, mixed_all, attn_all, load_sems,
-    swap_send, swap_recv, pair, flow, *scatter_sems,
-):
-    chain = Chain()
-    n = chain.n
+    full, head_size = key_part.shape
+    sources = (
+        raw_hbm, query_low_hbm, key_low_hbm, value_low_hbm, inverse_hbm, mixed_hbm, grad_mixed_hbm, cos_hbm,
+        sin_hbm, col_hbm, projection_hbm, attn_hbm, hidden_hbm, resid_hbm,
+    )
+    targets = (
+        raw_ref, query_low_ref, key_low_ref, value_low_ref, inverse_ref, mixed_ref, grad_mixed_ref, cos_ref,
+        sin_ref, col_ref, projection_ref, attn_ref, hidden_ref, resid_ref,
+    )
     loads = [
         pltpu.make_async_copy(source, target, load_sems.at[at])
-        for at, (source, target) in enumerate(
-            ((mixed_ref, mixed_all), (attn_ref, attn_all), (hidden_ref, hidden_all))
-        )
+        for at, (source, target) in enumerate(zip(sources, targets))
     ]
     for load in loads:
         load.start()
-    full, head_size = key_part_ref.shape
-    query_width = grad_query_ref.shape[1]
-    own_pair[:, :head_size] = key_part_ref[...].astype(low)
-    own_pair[:, head_size:] = value_part_ref[...].astype(low)
+    query_width = query_low_ref.shape[1]
+    wait_all(loads[:10])
+    attention_heads_backward(
+        raw_ref, query_low_ref, key_low_ref, value_low_ref, inverse_ref, mixed_ref, grad_mixed_ref, query_gain_ref,
+        cos_ref, sin_ref, col_ref, row_ref, columns, key_part, value_part, query_gain_grad_ref,
+    )
+    own_pair[:, :head_size] = key_part[...].astype(low)
+    own_pair[:, head_size:] = value_part[...].astype(low)
     chain.greet()
     swap = pltpu.make_async_remote_copy(
         src_ref=own_pair,
@@ -1024,29 +1387,28 @@
     )
     swap.start()
     first = chain.c == 0
+    loads[10].wait()
     weight[:, :query_width] = projection_ref[:, :query_width]
     weight[:, query_width:] = jnp.where(
         first,
         projection_ref[:, query_width : query_width + head_size],
         projection_ref[:, query_width + head_size :],
     )
-    columns[:, :query_width] = grad_query_ref[...]
     swap.wait_recv()
-    grad_key = key_part_ref[...] + their_pair[:, :head_size].astype(high)
-    grad_value = value_part_ref[...] + their_pair[:, head_size:].astype(high)
+    grad_key = key_part[...] + their_pair[:, :head_size].astype(high)
+    grad_value = value_part[...] + their_pair[:, head_size:].astype(high)
+    key_raw = raw_ref[:, query_width : query_width + head_size]
     grad_key, gain_rows = norm_back(
-        raw_ref[...], key_gain_ref[...], unrotate(grad_key, cos_ref[...], sin_ref[...])
+        key_raw, key_gain_ref[...], unrotate(grad_key, cos_ref[...], sin_ref[...])
     )
     columns[:, query_width:] = jnp.where(first, grad_key, grad_value).astype(low)
     key_gain = jnp.where(first, jnp.sum(gain_rows, axis=0, keepdims=True), 0.0)
     key_gain_grad_ref[...] = jnp.broadcast_to(key_gain, key_gain_grad_ref.shape)
-    scatter = Scatter(chain, parts, pair, flow, *scatter_sems)
     pair_rows = parts.shape[1]
-
-    for load in loads:
-        load.wait()
-    projection_tile = projection_grad_ref.shape[0] // n
-    out_tile = out_grad_ref.shape[1] // n
+    scatter = Scatter(chain, chip_block(parts, pair_rows // 2), pair, flow, *scatter_sems)
+    wait_all(loads[11:])
+    projection_tile = projection_grad.shape[0] // n
+    out_tile = out_grad.shape[1] // n
 
     @pl.loop(0, n)
     def each(step):
@@ -1056,59 +1418,70 @@
         scatter.start_pair(z)
         pl.when(step < n - 1)(lambda: scatter.step(n - 1 - step))
         span = pl.ds(pl.multiple_of(step * projection_tile, projection_tile), projection_tile)
-        projection_grad_ref[span] = dot_first(hidden_all[:, span], columns[...]).astype(low)
+        projection_grad[span] = dot_first(hidden_ref[:, span], columns[...]).astype(low)
         span = pl.ds(pl.multiple_of(step * out_tile, out_tile), out_tile)
-        out_grad_ref[:, span] = dot_first(mixed_all[...], attn_all[:, span]).astype(low)
-
+        out_grad[:, span] = dot_first(mixed_ref[...], attn_ref[:, span]).astype(low)
+
+    stores = [
+        pltpu.make_async_copy(projection_grad, projection_grad_hbm, store_sems.at[0]),
+        pltpu.make_async_copy(out_grad, out_grad_hbm, store_sems.at[1]),
+    ]
+    for store in stores:
+        store.start()
     scatter.total(total)
     grad_rows, gain_rows = norm_back(tokens_ref[...].astype(high), gain_ref[...], total[...])
-    input_grad_ref[...] = grad_resid_ref[...] + grad_rows
+    input_grad_ref[...] = resid_ref[...] + grad_rows
     gain_grad_ref[...] = jnp.broadcast_to(jnp.sum(gain_rows, axis=0, keepdims=True), gain_grad_ref.shape)
     swap.wait_send()
     scatter.finish()
+    wait_all(stores)
 
 
 def run_input(
-    key_part, value_part, key_raw, key_gain, cosines, sines, grad_query, projection, hidden, mixed, grad_attn,
-    grad_resid, tokens, gain, peers,
+    raw, query_low, key_low, value_low, inverse, mixed, grad_mixed, query_gain, key_gain, cosines, sines, seg_col,
+    seg_row, projection, hidden, grad_attn, grad_resid, tokens, gain, peers,
 ):
     length, width = tokens.shape
     n = peers // 2
-    full, head_size = key_part.shape
-    query_width = grad_query.shape[1]
-    return pl.pallas_call(
+    full, head_size = key_low.shape
+    query_width = query_low.shape[1]
+    loaded = [
+        raw, query_low, key_low, value_low, inverse, mixed, grad_mixed, cosines, sines, seg_col, projection,
+        grad_attn, hidden, grad_resid,
+    ]
+    dma = pltpu.SemaphoreType.DMA
+    input_grad, gain_grad, query_gain_grad, key_gain_grad, projection_grad, out_grad = pl.pallas_call(
         input_kernel,
         out_shape=[
             jax.ShapeDtypeStruct((length, width), high),
+            jax.ShapeDtypeStruct((8, width), high),
+            jax.ShapeDtypeStruct((8, head_size), high),
+            jax.ShapeDtypeStruct((8, head_size), high),
             jax.ShapeDtypeStruct((width, query_width + head_size), low),
             jax.ShapeDtypeStruct((query_width, width), low),
-            jax.ShapeDtypeStruct((8, width), high),
-            jax.ShapeDtypeStruct((8, head_size), high),
         ],
-        in_specs=[VMEM] * 8 + [ANY] * 3 + [VMEM] * 3,
-        out_specs=[VMEM] * 5,
+        in_specs=[VMEM] * 5 + [ANY] * len(loaded),
+        out_specs=[VMEM] * 4 + [ANY] * 2,
         scratch_shapes=[
+            *[pltpu.VMEM(array.shape, array.dtype) for array in loaded],
             pltpu.VMEM((full, 2 * head_size), low),
             pltpu.VMEM((full, 2 * head_size), low),
+            pltpu.VMEM((full, head_size), high),
+            pltpu.VMEM((full, head_size), high),
             pltpu.VMEM((full, query_width + head_size), low),
             pltpu.VMEM((width, query_width + head_size), low),
             pltpu.VMEM((length, width), high),
             pltpu.VMEM((n, 2 * length, width), low),
-            pltpu.VMEM(hidden.shape, low),
-            pltpu.VMEM(mixed.shape, low),
-            pltpu.VMEM(grad_attn.shape, low),
-            pltpu.SemaphoreType.DMA((3,)),
-            pltpu.SemaphoreType.DMA(()),
-            pltpu.SemaphoreType.DMA(()),
+            pltpu.VMEM((width, query_width + head_size), low),
+            pltpu.VMEM((query_width, width), low),
+            dma((len(loaded),)), dma((2,)), dma(()), dma(()),
             *Scatter.buffers(n, length, width),
         ],
         compiler_params=communicating(5),
         cost_estimate=pl.CostEstimate(flops=0, bytes_accessed=64 << 20, transcendentals=0),
-        name="input_gradient",
-    )(
-        key_part, value_part, key_raw, key_gain, cosines, sines, grad_query, projection, hidden, mixed,
-        grad_attn, grad_resid, tokens, gain,
-    )
+        name="attention_backward_and_input",
+    )(query_gain, key_gain, seg_row, tokens, gain, *loaded)
+    return input_grad, projection_grad, out_grad, gain_grad, query_gain_grad, key_gain_grad
 def weights_kernel(
     proj_ref, out_ref, attn_gain_ref, ffn_gain_ref, query_gain_ref, key_gain_ref, router_ref, resid_ref,
     mixture_ref,
@@ -1123,7 +1496,7 @@
     group, y, x, from_x, from_y = square()
     beside, across = {"dp": from_x}, {"dp": from_y}
     chain = Chain()
-    scatter = Scatter(chain, mixture_ref, pair, flow, *scatter_sems)
+    scatter = Scatter(chain, chip_block(mixture_ref, resid_ref.shape[0]), pair, flow, *scatter_sems)
     width = out_ref.shape[1]
     head_size = query_gain_ref.shape[1]
     small[...] = jnp.zeros_like(small)
@@ -1393,8 +1766,9 @@
 
         @pl.when(pl.program_id(0) == expert)
         def place():
-            gate_ref[0] = wide[0, 0].astype(high)
-            up_ref[0] = wide[0, 1].astype(high)
+            piece = gate_ref.shape[1]
+            gate_ref[0] = wide[:piece].astype(high)
+            up_ref[0] = wide[piece:].astype(high)
             down_ref[0] = down[...].astype(high)
 
     for source, target in ((query_in, query_ref), (key_in, key_ref), (value_in, value_ref), (out_in, out_ref)):
@@ -1410,10 +1784,10 @@
 
     for expert, rows in enumerate(grads):
         turn = of_expert(expert)
-        operands += [rows[: 2 * hidden_units].reshape(groups, 2, piece, tile), rows[2 * hidden_units :]]
+        operands += [rows, rows]
         specs += [
-            pl.BlockSpec((1, 2, piece, tile), lambda x, j, turn=turn: (turn(x, j), 0, 0, 0)),
-            pl.BlockSpec((piece, tile), lambda x, j, turn=turn: (turn(x, j), 0)),
+            pl.BlockSpec((2 * piece, tile), lambda x, j, turn=turn: (turn(x, j), 0)),
+            pl.BlockSpec((piece, tile), lambda x, j, turn=turn: (2 * groups + turn(x, j), 0)),
         ]
     steps = 2 * groups
 
@@ -1436,7 +1810,7 @@
             pl.BlockSpec((1, piece, tile), lambda x, j: (x, j, 0)),
             *[rows_of(array) for array in weight_grads],
         ],
-        compiler_params=pltpu.CompilerParams(vmem_limit_bytes=40 << 20),
+        compiler_params=pltpu.CompilerParams(vmem_limit_bytes=60 << 20),
         name="widen",
     )(*operands, *weight_grads)
 
@@ -1487,7 +1861,7 @@
 
 
 def fits_kernels(peers, groups, sharers, experts, full_length, width):
-    return groups == 4 and peers % 2 == 0 and peers <= 8 and sharers == 2 and experts == 2 * peers and full_length * width <= 1 << 21
+    return groups == 4 and peers == 8 and sharers == 2 and experts == 2 * peers and full_length * width <= 1 << 21
 
 
 def fused_layer(
@@ -1507,37 +1881,33 @@
     gain_ffn_row = norm_gain_ffn.reshape(1, model_width)
 
     named = jnp.any(routes[:, :, None] == jnp.arange(128, dtype=jnp.int32)[None, None, :], axis=1).astype(low)
-    hidden, all_named, projection, raw = run_gather(
-        tokens, gain_attn_row, named, query_weight, key_matrix, value_matrix, peers, groups
-    )
-    cotangent_ready, hidden = lax.optimization_barrier((cotangent, hidden))
-    cotangents = lax.all_gather(cotangent_ready, "expert", axis=0, tiled=True)
+    hidden, all_named, near, projection, raw = run_gather(
+        tokens, gain_attn_row, named, cotangent, query_weight, key_matrix, value_matrix, peers, groups
+    )
     cosines, sines = constant_tables(full_length, head_size)
     seg_col = jnp.broadcast_to(segments.reshape(full_length, 1), (full_length, head_size))
     seg_row = jnp.broadcast_to(segments.reshape(1, full_length), (8, full_length))
     query_gain_row = query_gain.reshape(1, head_size)
     key_gain_row = key_gain.reshape(1, head_size)
-    mixed, query_low, key_low, value_low, inverse = run_attention_forward(
-        raw, heads, head_size, query_gain_row, key_gain_row, cosines, sines, seg_col, seg_row
-    )
-    resid, ffn_local = run_project(mixed, out_weight, tokens, gain_ffn_row, peers)
-    router = jnp.concatenate([router_weight.T, jnp.zeros((128 - experts, model_width), low)], axis=0)
-    sums, gates, mixture, *grads = run_experts(
-        ffn_local, all_named, router, cotangents, gate_weight, up_weight, down_weight, peers, groups
-    )
+    router = router_weight.T
+    (
+        key_low, value_low, resid, ffn_local, gates, own_gates, mixed, query_low, inverse, rows_all, cotangents,
+        mixture, parts, first_grads,
+    ) = run_first(
+        raw, query_gain_row, key_gain_row, cosines, sines, seg_col, seg_row, out_weight, tokens, gain_ffn_row,
+        all_named, router, cotangent, near, gate_weight, up_weight, down_weight, peers, groups,
+    )
+    mixture, second_grads, grad_resid, grad_attn, grad_mixed, grad_router, gain_ffn_part = run_second(
+        gates, rows_all, cotangents, gate_weight, up_weight, down_weight, mixture, parts, own_gates, ffn_local,
+        resid, cotangent, gain_ffn_row, router, out_weight, experts, peers, groups,
+    )
+    grads = (first_grads, second_grads)
     grads = [
         lax.psum_scatter(each.reshape(-1, each.shape[2]), "dp", scatter_dimension=0, tiled=True) for each in grads
     ]
-    grad_resid, grad_attn, grad_mixed, grad_router, gain_ffn_part = run_turn(
-        sums, gates, ffn_local, resid, cotangent, gain_ffn_row, router, out_weight, experts, peers
-    )
-    grad_query_low, grad_key_part, grad_value_part, query_gain_part = run_attention_backward(
-        raw, query_low, key_low, value_low, inverse, mixed, grad_mixed, heads, head_size,
-        query_gain_row, cosines, sines, seg_col, seg_row,
-    )
-    input_grad, grad_projection, grad_out, gain_attn_part, key_gain_part = run_input(
-        grad_key_part, grad_value_part, raw[:, local_width : local_width + head_size], key_gain_row, cosines,
-        sines, grad_query_low, projection, hidden, mixed, grad_attn, grad_resid, tokens, gain_attn_row, peers,
+    input_grad, grad_projection, grad_out, gain_attn_part, query_gain_part, key_gain_part = run_input(
+        raw, query_low, key_low, value_low, inverse, mixed, grad_mixed, query_gain_row, key_gain_row, cosines, sines,
+        seg_col, seg_row, projection, hidden, grad_attn, grad_resid, tokens, gain_attn_row, peers,
     )
     *weight_grads, small, output = run_weights(
         grad_projection, grad_out, gain_attn_part, gain_ffn_part, query_gain_part, key_gain_part, grad_router,

time: 535 us -> 514 us (0.961)
  Pallas kernels: 495 us -> 484 us
  local copies, waits for them, and re-layouts: 18.8 us -> 8.54 us
    pallas_call x6 -> x2, Pallas kernels: 268 us -> 221 us  [the longest x1 111 us: run_first(): pl.pallas_call(first_kernel, out_shape=[jax.ShapeDtypeStruct((full, head_...]
    pallas_call x1, Pallas kernels: 90.9 us -> 111 us  [run_weights(): pl.pallas_call(weights_kernel, out_shape=[jax.ShapeDtypeStruct((shard_row...]
    pallas_call x1, Pallas kernels: 51 us -> 63.9 us  [run_input(): pl.pallas_call(input_kernel, out_shape=[jax.ShapeDtypeStruct((length, wid...]
    slice x5 -> x0, local copies, waits for them, and re-layouts: 7.54 us -> none  [the longest x2 3.17 us: run_widen(): rows[:2 * hidden_units].reshape(groups, 2, piece, tile)]
  transfers between devices with their start and end apart: 3 -> 2, of which waited for: 0 -> 0; matrix products, arithmetic and copies ran while one was open for 2% -> 1% of each run, Pallas kernels for 66% -> 56%
where the time goes in v3:
time: 514 us; the launch traced here: 508 us
  Pallas kernels  484 us (94%)
  between operations  14.1 us (3%)
  local copies, waits for them, and re-layouts  8.54 us (2%)
    pallas_call x1, Pallas kernels, run_weights(): pl.pallas_call(weights_kernel, out_shape=[jax.ShapeDtypeStruct((shard_row...  111 us
    pallas_call x1, Pallas kernels, run_first(): pl.pallas_call(first_kernel, out_shape=[jax.ShapeDtypeStruct((full, head_...  111 us
    pallas_call x1, Pallas kernels, run_second(): pl.pallas_call(second_kernel, out_shape=[split(width, low), jax.ShapeDtyp...  111 us
    pallas_call x1, Pallas kernels, run_gather(): pl.pallas_call(gather_kernel, out_shape=[jax.ShapeDtypeStruct((length * p...  76.6 us
    pallas_call x1, Pallas kernels, run_input(): pl.pallas_call(input_kernel, out_shape=[jax.ShapeDtypeStruct((length, wid...  63.9 us
    pallas_call x1, Pallas kernels, run_widen(): pl.pallas_call(widen_kernel, grid=(2, groups), out_shape=[jax.ShapeDtypeS...  11.7 us
  transfers between devices with their start and end apart: 2, of which 0 were waited for; matrix products, arithmetic and copies ran while one was open for 1% of the time, Pallas kernels for 56%

profile of v3, /device:TPU:0, one launch (start us, length us, event | category | flops | bytes accessed | tf_op | source)
XLA Modules:
  0.0 508.0 jit_solution(4011566195514173831)
XLA Ops:
  7.2 0.0 copy-start.2
  7.2 0.0 reduce-scatter.3.cloned.1.call-start
  7.2 0.8 copy.33
  8.0 0.3 fusion
  8.3 0.6 convert_element_type.3.named_ref
  8.9 76.6 %gather_hidden.1 = (bf16[1024,2048]{1,0:T(8,128)(2,1)}, bf16[8,128,128]{2,1,0:T(8,128)(2,1)}, bf16[3,128,2048]{2,1,0:T(8,128)(2,1)}, bf16[8,4,64,768]{3,2,1,0:T(8,128)(2,1)}, f32[1024,768]{1,0:T(8,128)}) custom-call(bf16[128,2048]{1,0:T(8,128)(2,1)} %tokens_ref.5, f32[1,2048]{1,0:T(1,128)} %bitcast.38, bf16[128,128]{1,0:T(8,128)(2,1)} %convert_element_type.3.named_ref, ...), custom_call_target="tpu_custom_call" | custom-call | bytes 67108864 | tf_op jit(solution)/shard_map/gather_hidden/pallas_call | solution.py:689
  85.5 0.0 copy-done.2
  85.6 0.6 broadcast_in_dim.7.row_ref
  86.2 1.0 broadcast_in_dim.16.col_hbm
  87.2 110.7 %attention_and_first_expert.1 = (bf16[1024,128]{1,0:T(8,128)(2,1)}, bf16[1024,128]{1,0:T(8,128)(2,1)}, f32[128,2048]{1,0:T(8,128)}, bf16[2,64,2048]{2,1,0:T(8,12...) custom-call(f32[1,128]{1,0:T(1,128)} %bitcast.46, ...), custom_call_target="tpu_custom_call" | custom-call | bytes 125829120 | tf_op jit(solution)/shard_map/attention_and_first_expert/pallas_call | solution.py:1204
  197.9 0.0 reduce-scatter.3.cloned.1.call-update
  197.9 0.0 reduce-scatter.5.cloned.1.call-start
  198.0 110.6 %second_expert_and_turn.1 = (bf16[8,2,64,2048]{3,2,1,0:T(8,128)(2,1)}, bf16[4,2304,512]{2,1,0:T(8,128)(2,1)}, f32[128,2048]{1,0:T(8,128)}, bf16[8,2,64,2048]{3,2...) custom-call(f32[8,2,64,128]{3,2,1,0:T(8,128)} %get-tuple-element.67.gates_ref, ...), custom_call_target="tpu_custom_call" | custom-call | bytes 125829120 | tf_op jit(solution)/shard_map/second_expert_and_turn/pallas_call | solution.py:1270
  308.6 0.0 reduce-scatter.5.cloned.1.call-update
  308.7 63.9 %attention_backward_and_input.1 = (f32[128,2048]{1,0:T(8,128)}, f32[8,2048]{1,0:T(8,128)}, f32[8,128]{1,0:T(8,128)}, f32[8,128]{1,0:T(8,128)}, bf16[2048,640]{1,0:T(8,128)(2,1)}, /*index=5*/bf16[512,2048]{1,0:T(8,128)(2,1)}) custom-call(f32[1,128]{1,0:T(1,128)} %bitcast.47, f32[1,128]{1,0:T(1,128)} %bitcast.49, s32[8,1024]{1,0:T(8,128)} %broadcast_in_dim.7.row_ref, ...), custom_call_target="tpu_custom_call" | custom-call | bytes 67108864 | tf_op jit(solution)/shard_map/attention_backward_and_input/pallas_call | solution.py:1453
  372.5 110.8 %sum_weight_gradients.1 = (bf16[256,4096]{1,0:T(8,128)(2,1)}, bf16[256,512]{1,0:T(8,128)(2,1)}, bf16[256,512]{1,0:T(8,128)(2,1)}, bf16[512,2048]{1,0:T(8,128)(2,...) custom-call(bf16[8,256,640]{2,1,0:T(8,128)(2,1)} %bitcast.32, bf16[512,2048]{1,0:T(8,128)(2,1)} %get-tuple-element.81.out_ref, ...), custom_call_target="tpu_custom_call" | custom-call | bytes 67108864 | tf_op jit(solution)/shard_map/sum_weight_gradients/pallas_call | solution.py:1713
  483.3 1.3 slice_bitcast_fusion.1
  484.6 1.5 fusion.1
  486.1 1.6 slice_bitcast_fusion
  487.7 11.7 %widen.1 = (f32[2,192,2048]{2,1,0:T(8,128)}, f32[2,192,2048]{2,1,0:T(8,128)}, f32[2,768,512]{2,1,0:T(8,128)}, f32[256,4096]{1,0:T(8,128)}, f32[256,512]{1,0:T(8,...) custom-call(bf16[2304,512]{1,0:T(8,128)(2,1)} %reduce-scatter.3.cloned.1.call-done.wide_0.down_0, ...), custom_call_target="tpu_custom_call" | custom-call | tf_op jit(solution)/shard_map/widen/pallas_call | solution.py:1797
  499.4 0.0 copy-done.1
  499.4 0.8 copy.36
  500.2 0.0 copy-done
  500.2 1.0 copy.37
  (4 shorter events, 0.0 us)
Async XLA Ops:
  7.2 78.4 %copy-start.2 = (s32[1,1024]{1,0:T(1,128)S(1)}, s32[1,1024]{1,0:T(1,128)}, u32[]{:S(2)}) copy-start(s32[1,1024]{1,0:T(1,128)} %param.19) | copy-start | bytes 12292
  7.2 480.5 %reduce-scatter.3.cloned.1.call-start = ((), (), s32[]{:S(2)}) async-start(), calls=%async_computation.2 | async-start | bytes 11796480 | tf_op jit(solution)/shard_map/reduce_scatter | solution.py:1906
  197.9 289.7 %reduce-scatter.5.cloned.1.call-start = ((), (), s32[]{:S(2)}) async-start(), calls=%async_computation.3 | async-start | bytes 11796480 | tf_op jit(solution)/shard_map/reduce_scatter | solution.py:1906
  487.7 11.8 %copy-start.1 = (bf16[128,2048]{1,0:T(8,128)(2,1)S(1)}, bf16[128,2048]{1,0:T(8,128)(2,1)}, u32[]{:S(2)}) copy-start(bf16[128,2048]{1,0:T(8,128)(2,1)} %get-tuple-element.122) | copy-start | bytes 1572868
  487.7 12.6 %copy-start = (f32[128,2048]{1,0:T(8,128)S(1)}, f32[128,2048]{1,0:T(8,128)}, u32[]{:S(2)}) copy-start(f32[128,2048]{1,0:T(8,128)} %get-tuple-element.123) | copy-start | bytes 3145732
Sparse Core Ops, SparseCore 0:
  198.1 92.4 reduce-scatter.2
  308.8 112.8 reduce-scatter.4

commit v4 on v3

--- a/solution.py
+++ b/solution.py
@@ -219,7 +219,7 @@
         self.sibling, self.up, self.down = me + 1 - 2 * self.c, me + 2, me - 2
         self.has_up, self.has_down = self.z < self.n - 1, self.z > 0
 
-    def greet(self):
+    def greet(self, others=()):
         barrier = pltpu.get_barrier_semaphore()
 
         def signal(peer):
@@ -228,7 +228,9 @@
         signal(self.sibling)
         pl.when(self.has_up)(lambda: signal(self.up))
         pl.when(self.has_down)(lambda: signal(self.down))
-        peers = 1 + self.has_up.astype(jnp.int32) + self.has_down.astype(jnp.int32)
+        for device in others:
+            pl.semaphore_signal(barrier, inc=1, device_id=device, device_id_type=MESH)
+        peers = 1 + len(others) + self.has_up.astype(jnp.int32) + self.has_down.astype(jnp.int32)
         pl.semaphore_wait(barrier, peers)
 
     def nearest(self, step):
@@ -491,25 +493,107 @@
             copy.wait_send()
 
 
-def row_block(ref, rows):
-    return lambda z, c: ref.at[pl.ds(pl.multiple_of((2 * z + c) * rows, rows), rows)]
-
-
-def chip_block(ref, rows):
-    return lambda z, c: ref.at[z, pl.ds(pl.multiple_of(c * rows, rows), rows)]
-
-
-def communicating(collective_id):
-    return pltpu.CompilerParams(
-        collective_id=collective_id, has_side_effects=True, vmem_limit_bytes=60 << 20
-    )
-
-
 def square():
     group = lax.axis_index("dp")
     y, x = group // 2, group % 2
     from_x, from_y = 2 * y + 1 - x, 2 * (1 - y) + x
     return group, y, x, from_x, from_y
+
+
+class SquareSum:
+    def __init__(self, source, result, first_a, first_b, second_a, second_b, send_a, send_b, ports):
+        self.source, self.result = source, result
+        self.own, self.y, self.x, self.from_x, self.from_y = square()
+        self.first_a, self.first_b, self.second_a, self.second_b = first_a, first_b, second_a, second_b
+        self.send_a, self.send_b = send_a, send_b
+        self.rows, self.middle = source.shape[0] // 4, source.shape[1] // 2
+        beside, across = {"dp": self.from_x}, {"dp": self.from_y}
+        self.first = []
+        for k in range(2):
+            self.first.append(ports.copy(self.part(source, 0, 2 * k + 1 - self.x), first_a.at[k], beside))
+            self.first.append(ports.copy(self.part(source, 1, 2 * (1 - self.y) + k), first_b.at[k], across))
+        self.second = [ports.copy(send_a, second_a, across), ports.copy(send_b, second_b, beside)]
+
+    @staticmethod
+    def buffers(rows, columns):
+        quarter = (rows // 4, columns // 2)
+        return [pltpu.VMEM((2, *quarter), low)] * 2 + [pltpu.VMEM(quarter, low)] * 4
+
+    def part(self, ref, side, quarter):
+        rows = pl.ds(pl.multiple_of(quarter * self.rows, self.rows), self.rows)
+        return ref.at[rows, pl.ds(side * self.middle, self.middle)]
+
+    @staticmethod
+    def start(copies):
+        for copy in copies:
+            copy.start()
+
+    @staticmethod
+    def arrive(copies):
+        for copy in copies:
+            copy.wait_recv()
+
+    def begin(self):
+        self.start(self.first)
+
+    def exchange(self):
+        self.arrive(self.first)
+        along_y = self.part(self.source, 0, self.from_y)[...].astype(high)
+        self.send_a[...] = (along_y + self.first_a[1 - self.y].astype(high)).astype(low)
+        along_x = self.part(self.source, 1, self.from_x)[...].astype(high)
+        self.send_b[...] = (along_x + self.first_b[1 - self.x].astype(high)).astype(low)
+        self.start(self.second)
+
+    def settle(self):
+        self.arrive(self.second)
+        for side, first, second in (
+            (0, self.first_a[self.y], self.second_a), (1, self.first_b[self.x], self.second_b)
+        ):
+            total = self.part(self.source, side, self.own)[...].astype(high) + first.astype(high)
+            columns = pl.ds(side * self.middle, self.middle)
+            self.result[:, columns] = (total + second[...].astype(high)).astype(low)
+
+
+class SquareCopy:
+    def __init__(self, mine, result, ports):
+        own, _, _, from_x, from_y = square()
+        rows, middle = mine.shape[0], mine.shape[1] // 2
+        beside, across = {"dp": from_x}, {"dp": from_y}
+
+        def quarter(at):
+            return pl.ds(pl.multiple_of(at * rows, rows), rows)
+
+        target = result.at[quarter(own)]
+        self.mine, self.target = mine, target
+        self.near = [ports.copy(mine, target, beside), ports.copy(mine, target, across)]
+        left = result.at[quarter(from_x), pl.ds(0, middle)]
+        right = result.at[quarter(from_y), pl.ds(middle, middle)]
+        self.far = [ports.copy(left, left, across), ports.copy(right, right, beside)]
+
+    def begin(self):
+        SquareSum.start(self.near)
+        self.target[...] = self.mine[...]
+
+    def hand_on(self):
+        SquareSum.arrive(self.near)
+        SquareSum.start(self.far)
+
+    def finish(self):
+        SquareSum.arrive(self.far)
+
+
+def row_block(ref, rows):
+    return lambda z, c: ref.at[pl.ds(pl.multiple_of((2 * z + c) * rows, rows), rows)]
+
+
+def chip_block(ref, rows):
+    return lambda z, c: ref.at[z, pl.ds(pl.multiple_of(c * rows, rows), rows)]
+
+
+def communicating(collective_id):
+    return pltpu.CompilerParams(
+        collective_id=collective_id, has_side_effects=True, vmem_limit_bytes=60 << 20
+    )
 
 
 def gather_kernel(
@@ -615,19 +699,22 @@
             wait_swap(source)
         to_x(at, source, group).start()
         to_y(at, source, group).start()
-        if step > 0 and core == 1:
-            for gather in wide:
-                gather.service(step)
-    def near(slot, peer):
-        return remote(cot_ref, near_ref.at[slot], near_send.at[slot], near_recv.at[slot], {"expert": peer})
-
-    pl.when(chain.has_up)(lambda: near(0, chain.up).start())
-    pl.when(chain.has_down)(lambda: near(1, chain.down).start())
-    near(2, chain.sibling).start()
+    for gather in wide:
+        gather.service(1)
     for at, (source, core, _) in enumerate(sources):
         to_x(at, source, from_x).wait_recv()
         to_y(at, source, from_y).wait_recv()
         to_far(at, core, source, from_x if core == 0 else from_y).start()
+    for step in range(2, n):
+        for gather in wide:
+            gather.service(step)
+
+    def near(slot, peer):
+        return remote(cot_ref, near_ref.at[slot], near_send.at[slot], near_recv.at[slot], {"expert": peer})
+
+    pl.when(chain.has_up)(lambda: near(0, chain.up).start())
+    pl.when(chain.has_down)(lambda: near(1, chain.down).start())
+    near(2, chain.sibling).start()
     for gather in wide:
         for z in range(n):
             gather.wait_sibling(jnp.int32(z))
@@ -750,14 +837,17 @@
 
 
 class Split:
+    both = slice(None)
+
     @staticmethod
     def take(ref, z, half, columns=slice(None)):
         block = ref[pl.ds(2 * z, 2), half, :, columns]
-        return block.reshape(block.shape[0] * block.shape[1], block.shape[2])
+        return block.reshape(-1, block.shape[-1])
 
     @staticmethod
     def put(ref, z, half, value, columns=slice(None)):
-        ref[pl.ds(2 * z, 2), half, :, columns] = value.reshape(2, value.shape[0] // 2, value.shape[1])
+        halves = (2, 2) if half is Split.both else (2,)
+        ref[pl.ds(2 * z, 2), half, :, columns] = value.reshape(*halves, ref.shape[2], value.shape[1])
 
     @staticmethod
     def every(ref, columns=slice(None)):
@@ -839,9 +929,9 @@
     query_gain_ref, key_gain_ref, row_ref, tokens_ref, gain_ref, named_ref, router_in, cot_ref, near_ref,
     raw_hbm, cos_hbm, sin_hbm, col_hbm, weight_hbm, gate_hbm, up_hbm, down_hbm,
     key_low_ref, value_low_ref, resid_ref, ffn_ref, gates_ref, own_gates_ref,
-    mixed_hbm, query_low_hbm, inverse_hbm, rows_hbm, cots_hbm, mixture_hbm, parts_hbm, grads_hbm,
+    mixed_hbm, query_low_hbm, inverse_hbm, rows_hbm, cots_hbm, gated_hbm, parts_hbm, grads_hbm,
     raw_ref, cos_ref, sin_ref, col_ref, weight_ref, mixed_ref, query_low_ref, inverse_ref, value_wide, router_ref, plain, attn_parts, rows_all, cots, gate_w, up_w, down_w, gated, grad_gate, grad_up,
-    mix_stage, part_stage, tile_stage, load_sems, rows_sems, mix_sems, part_sems, tile_sems, cot_send, cot_recv, cot_local, *transfers,
+    part_stage, tile_stage, load_sems, rows_sems, part_sems, tile_sems, cot_send, cot_recv, cot_local, *transfers,
 ):
     chain = Chain()
     n = chain.n
@@ -919,6 +1009,7 @@
 
     scatters[1].step(n - 1)
     own_rows(0)
+    scatters[1].step(n - 2)
     cot_gather.service(3)
     plain_rows(jnp.int32(3))
     lanes = lax.broadcasted_iota(jnp.int32, (block_rows, 128), 1)
@@ -926,20 +1017,13 @@
     tile = tile_stage.shape[2]
     wait_all(loads[6:])
 
-    def mix_copy(z, half, slot):
-        return pltpu.make_async_copy(mix_stage.at[slot], mixture_hbm.at[pl.ds(2 * z, 2), half], mix_sems.at[slot])
-
     def part_copy(z, half, slot):
         return pltpu.make_async_copy(part_stage.at[slot], parts_hbm.at[pl.ds(2 * z, 2), half], part_sems.at[slot])
 
     @pl.loop(0, 2 * n)
     def each(turn):
-        for step in range(1, n - 1):
-
-            @pl.when(turn == step)
-            def early():
-                scatters[1].step(n - 1 - step)
-                gathers[0].service(step)
+        pl.when((turn >= 1) & (turn < n - 1))(lambda: gathers[0].service(turn))
+        pl.when((turn >= 1) & (turn < n - 2))(lambda: scatters[1].step(n - 2 - turn))
 
         @pl.when(turn == n - 1)
         def middle():
@@ -974,28 +1058,23 @@
         )
         slot = turn % 2
 
-        @pl.when(turn >= 2)
-        def free():
-            mix_copy(z, half, slot).wait()
-            part_copy(z, half, slot).wait()
+        pl.when(turn >= 2)(lambda: part_copy(z, half, slot).wait())
 
         @pl.loop(0, width // tile)
         def columns(at):
             span = pl.ds(pl.multiple_of(at * tile, tile), tile)
-            mixture = dot(Split.take(gated, z, half), down_w[:, span])
-            mix_stage[slot, :, :, span] = mixture.astype(low).reshape(2, rows, tile)
             grad_rows = dot_last(Split.take(grad_gate, z, half), gate_w[span, :])
             grad_rows = grad_rows + dot_last(Split.take(grad_up, z, half), up_w[span, :])
             part_stage[slot, :, :, span] = grad_rows.astype(low).reshape(2, rows, tile)
 
         sent = gate_columns(lanes, expert, gate_grad).astype(low)
         part_stage[slot, :, :, width:] = sent.reshape(2, rows, 128)
-        mix_copy(z, half, slot).start()
         part_copy(z, half, slot).start()
 
     whole_copies = [
         pltpu.make_async_copy(rows_all, rows_hbm, rows_sems.at[0]),
         pltpu.make_async_copy(cots, cots_hbm, rows_sems.at[1]),
+        pltpu.make_async_copy(gated, gated_hbm, rows_sems.at[5]),
     ]
     for copy in whole_copies:
         copy.start()
@@ -1007,29 +1086,26 @@
         scatters[half].finish()
     tiles.finish()
     for slot in range(2):
-        mix_copy(jnp.int32(0), 0, slot).wait()
         part_copy(jnp.int32(0), 0, slot).wait()
     wait_all(whole_copies + attention_copies)
     cot_gather.finish()
 
 
 def second_kernel(
-    gates_ref, rows_hbm, cot_hbm, gate_hbm, up_hbm, down_hbm, mixture_in, parts_in, own_gates_ref, ffn_ref,
-    resid_ref, cot_ref, gain_ref, router_in, weight_ref,
-    mixture_hbm, grads_hbm, grad_resid_ref, attn_hbm, mixed_ref, router_grad_ref, gain_grad_ref,
-    rows_all, cots, gate_w, up_w, down_w, gated, grad_gate, grad_up, mixture, parts, tile_stage, attn_all, own,
-    sums, router_ref, load_sems, chip_sems, mix_sems, tile_sems, attn_sem, *transfers,
+    gates_ref, rows_hbm, cot_hbm, gate_hbm, up_hbm, down_hbm, parts_in,
+    sum_ref, gated_hbm, grads_hbm,
+    rows_all, cots, gate_w, up_w, down_w, gated, grad_gate, grad_up, parts, tile_stage, load_sems, chip_sems,
+    tile_sems, out_sem, pair, flow, *scatter_sems,
 ):
     chain = Chain()
     n = chain.n
-    _, _, rows, width = rows_all.shape
-    block_rows = 2 * rows
+    width = rows_all.shape[3]
+    block_rows = parts.shape[1]
     loads = [
         pltpu.make_async_copy(source, target, load_sems.at[at])
         for at, (source, target) in enumerate(
             (
                 (gate_hbm.at[1], gate_w), (up_hbm.at[1], up_w), (down_hbm.at[1], down_w), (parts_in, parts),
-                (mixture_in, mixture),
             )
         )
     ]
@@ -1046,128 +1122,47 @@
     for step in range(n):
         for load in chip_loads(chain.nearest(n - 1 - step)):
             load.start()
-    for load in loads[3:]:
-        load.start()
+    loads[3].start()
     chain.greet()
-    scatters, gathers = [], []
-    for half in range(2):
-        pair, flow, *rest = transfers[9 * half : 9 * half + 9]
-        scatters.append(Scatter(chain, lambda z, c, half=half: parts.at[2 * z + c, half], pair, flow, *rest[:4]))
-        gathers.append(
-            Gather(chain, own.at[half], lambda z, c, half=half: attn_all.at[2 * z + c, half], *rest[4:])
-        )
+    scatter = Scatter(chain, chip_block(parts, block_rows // 2), pair, flow, *scatter_sems)
     lanes = lax.broadcasted_iota(jnp.int32, (block_rows, 128), 1)
     expert = lax.axis_index("expert") * gate_hbm.shape[0] + 1
     tile = tile_stage.shape[2]
-    router_ref[...] = jnp.zeros_like(router_ref)
-    router_ref[: router_in.shape[0]] = router_in[...]
     wait_all(loads[:3])
 
-    def mix_copy(z, half):
-        block = pl.ds(2 * z, 2)
-        return pltpu.make_async_copy(mixture.at[block, half], mixture_hbm.at[block, half], mix_sems.at[half, z])
-
-    def own_rows(half):
-        scatters[half].total(sums)
-        span = pl.ds(half * rows, rows)
-        sent = sums[:, width:]
-        left = lax.broadcasted_iota(jnp.int32, sent.shape, 1) < 64
-        grad_gates = jnp.where(left, sent + pltpu.roll(sent, 64, 1), 0.0)
-        gates = own_gates_ref[half]
-        inner = jnp.sum(gates * grad_gates, axis=-1, keepdims=True)
-        grad_logits = (gates * (grad_gates - inner)).astype(low)
-        router_grad = dot_first(grad_logits, ffn_ref[half])[: router_grad_ref.shape[0]]
-        grad_hidden = sums[:, :width] + dot(grad_logits, router_ref[...])
-        grad_rows, gain_rows = norm_back(resid_ref[span], gain_ref[...], grad_hidden)
-        gain_grad = jnp.broadcast_to(jnp.sum(gain_rows, axis=0, keepdims=True), gain_grad_ref.shape)
-        grad_resid = cot_ref[span].astype(high) + grad_rows
-        grad_resid_ref[span] = grad_resid
-        own[half] = grad_resid.astype(low)
-        gathers[half].begin()
-        if half == 0:
-            router_grad_ref[...] = router_grad
-            gain_grad_ref[...] = gain_grad
-        else:
-            router_grad_ref[...] += router_grad
-            gain_grad_ref[...] += gain_grad
-
-    @pl.loop(0, 2 * n)
-    def each(turn):
-        half, step = turn // n, turn % n
+    @pl.loop(0, n)
+    def each(step):
         z = chain.nearest(n - 1 - step)
-        pl.when(half == 0)(lambda: wait_all(chip_loads(z)))
-        gates = Split.take(gates_ref, z, half)
+        wait_all(chip_loads(z))
+        gates = Split.take(gates_ref, z, Split.both)
         gate_col = jnp.sum(jnp.where(lanes == expert, gates, 0.0), axis=-1, keepdims=True)
         gate_grad = expert_block(
-            rows_all, lambda units: dot_last(Split.take(cots, z, half), down_w[units, :]), gate_w, up_w, gate_col,
-            gated, grad_gate, grad_up, z, half,
+            rows_all, lambda units: dot_last(Split.take(cots, z, Split.both), down_w[units, :]), gate_w, up_w,
+            gate_col, gated, grad_gate, grad_up, z, Split.both,
         )
-
-        pl.when(turn == 0)(lambda: loads[3].wait())
+        pl.when(step == 0)(lambda: loads[3].wait())
 
         @pl.loop(0, width // tile)
         def columns(at):
             span = pl.ds(pl.multiple_of(at * tile, tile), tile)
-            grad_rows = dot_last(Split.take(grad_gate, z, half), gate_w[span, :])
-            grad_rows = grad_rows + dot_last(Split.take(grad_up, z, half), up_w[span, :])
-            Split.put(parts, z, half, (Split.take(parts, z, half, span).astype(high) + grad_rows).astype(low), span)
-
-        last = pl.ds(width, 128)
-        sent = Split.take(parts, z, half, last).astype(high) + gate_columns(lanes, expert, gate_grad)
-        Split.put(parts, z, half, sent.astype(low), last)
-        pl.when(half == 0)(lambda: scatters[0].start_pair(z))
-        pl.when(half == 1)(lambda: scatters[1].start_pair(z))
-
-        pl.when(turn < n - 1)(lambda: scatters[0].step(n - 1 - step))
-        pl.when((turn >= n) & (turn < 2 * n - 1))(lambda: scatters[1].step(n - 1 - step))
-        pl.when(turn == n)(lambda: own_rows(0))
-        pl.when(turn > n)(lambda: gathers[0].service(turn - n))
-
+            grad_rows = dot_last(Split.take(grad_gate, z, Split.both), gate_w[span, :])
+            grad_rows = grad_rows + dot_last(Split.take(grad_up, z, Split.both), up_w[span, :])
+            parts[z, :, span] = (parts[z, :, span].astype(high) + grad_rows).astype(low)
+
+        sent = parts[z, :, width:].astype(high) + gate_columns(lanes, expert, gate_grad)
+        parts[z, :, width:] = sent.astype(low)
+        scatter.start_pair(z)
+        pl.when(step < n - 1)(lambda: scatter.step(n - 1 - step))
+
+    gated_copy = pltpu.make_async_copy(gated, gated_hbm, out_sem)
+    gated_copy.start()
     tiles = Tiles(grads_hbm, tile_stage, tile_sems, gated, grad_gate, grad_up, rows_all, cots)
-    own_rows(1)
-    for step in range(1, n):
-        if step <= 3:
-            tiles.run(step - 1)
-        gathers[1].service(step)
-    for kind in range(n - 1, 3):
+    for kind in range(3):
         tiles.run(kind)
-    loads[4].wait()
-
-    @pl.loop(0, 2 * n)
-    def mixture_rows(turn):
-        half, z = turn // n, turn % n
-
-        @pl.loop(0, width // tile)
-        def columns(at):
-            span = pl.ds(pl.multiple_of(at * tile, tile), tile)
-            added = dot(Split.take(gated, z, half), down_w[:, span])
-            Split.put(mixture, z, half, (Split.take(mixture, z, half, span).astype(high) + added).astype(low), span)
-
-        mix_copy(z, half).start()
-
-    @pl.loop(0, 2 * n)
-    def mixed_rows(turn):
-        half, z = turn // n, turn % n
-        pl.when(half == 0)(lambda: gathers[0].wait_sibling(z))
-        pl.when(half == 1)(lambda: gathers[1].wait_sibling(z))
-
-        @pl.when(z == chain.z)
-        def mine():
-            pl.when(half == 0)(lambda: gathers[0].keep().wait())
-            pl.when(half == 1)(lambda: gathers[1].keep().wait())
-
-        result = dot_last(Split.take(attn_all, z, half), weight_ref[...])
-        Split.put(mixed_ref, z, half, result.astype(low))
-
-    attn_copy = pltpu.make_async_copy(attn_all, attn_hbm, attn_sem)
-    attn_copy.start()
-    for half in range(2):
-        gathers[half].finish()
-        scatters[half].finish()
-        for z in range(n):
-            mix_copy(jnp.int32(z), half).wait()
+    scatter.total(sum_ref)
+    scatter.finish()
     tiles.finish()
-    attn_copy.wait()
+    gated_copy.wait()
 
 
 def split_rows(array, peers):
@@ -1215,7 +1210,7 @@
             jax.ShapeDtypeStruct((full, local_width), high),
             split(width, low),
             split(width, low),
-            split(width, low),
+            split(hidden, low),
             split(sent, low),
             jax.ShapeDtypeStruct((groups, 3 * hidden, tile), low),
         ],
@@ -1235,10 +1230,9 @@
             pltpu.VMEM((peers, 2, rows, hidden), high),
             pltpu.VMEM((n, 2, 2, rows, width), low),
             *expert_scratch(gate_weight, up_weight, down_weight, peers, rows, width),
-            pltpu.VMEM((2, 2, rows, width), low),
             pltpu.VMEM((2, 2, rows, sent), low),
             pltpu.VMEM((2, hidden, tile), low),
-            dma((8,)), dma((5,)), dma((2,)), dma((2,)), dma((2, groups)),
+            dma((8,)), dma((6,)), dma((2,)), dma((2, groups)),
             *NearGather.semaphores(n),
             *(Scatter.buffers(n, rows, width) + Gather.semaphores(n)) * 2,
         ],
@@ -1252,115 +1246,91 @@
     )
 
 
-def run_second(
-    gates, rows_all, cotangents, gate_weight, up_weight, down_weight, mixture, parts, own_gates, ffn, resid,
-    cotangent, gain, router, weight, experts, peers, groups,
-):
-    length, width = resid.shape
-    n, rows = peers // 2, length // 2
-    full = length * peers
+def run_second(gates, rows_all, cotangents, gate_weight, up_weight, down_weight, parts, peers, groups):
+    _, _, rows, width = rows_all.shape
+    n, length = peers // 2, 2 * rows
     hidden = gate_weight.shape[2]
     tile, sent = width // groups, width + 128
-    mixed_width = weight.shape[0]
     dma = pltpu.SemaphoreType.DMA
-
-    def split(columns, dtype):
-        return jax.ShapeDtypeStruct((peers, 2, rows, columns), dtype)
-
-    mixture, grads, grad_resid, grad_attn, grad_mixed, grad_router, gain_grad = pl.pallas_call(
+    return pl.pallas_call(
         second_kernel,
         out_shape=[
-            split(width, low),
+            jax.ShapeDtypeStruct((length, sent), high),
+            jax.ShapeDtypeStruct((peers, 2, rows, hidden), low),
             jax.ShapeDtypeStruct((groups, 3 * hidden, tile), low),
-            jax.ShapeDtypeStruct((length, width), high),
-            split(width, low),
-            split(mixed_width, low),
-            jax.ShapeDtypeStruct((experts, width), high),
-            jax.ShapeDtypeStruct((8, width), high),
         ],
-        in_specs=[VMEM] + [ANY] * 7 + [VMEM] * 7,
-        out_specs=[ANY, ANY, VMEM, ANY, VMEM, VMEM, VMEM],
+        in_specs=[VMEM] + [ANY] * 6,
+        out_specs=[VMEM, ANY, ANY],
         scratch_shapes=[
             *expert_scratch(gate_weight, up_weight, down_weight, peers, rows, width),
-            pltpu.VMEM((peers, 2, rows, width), low),
-            pltpu.VMEM((peers, 2, rows, sent), low),
+            pltpu.VMEM((n, 2 * length, sent), low),
             pltpu.VMEM((2, hidden, tile), low),
-            pltpu.VMEM((peers, 2, rows, width), low),
-            pltpu.VMEM((2, rows, width), low),
-            pltpu.VMEM((rows, sent), high),
-            pltpu.VMEM((128, width), low),
-            dma((5,)), dma((2, n)), dma((2, n)), dma((2, groups)), dma(()),
-            *(Scatter.buffers(n, rows, sent) + Gather.semaphores(n)) * 2,
+            dma((4,)), dma((2, n)), dma((2, groups)), dma(()),
+            *Scatter.buffers(n, length, sent),
         ],
         compiler_params=communicating(7),
         cost_estimate=pl.CostEstimate(flops=0, bytes_accessed=120 << 20, transcendentals=0),
-        name="second_expert_and_turn",
-    )(
-        gates, rows_all, cotangents, gate_weight, up_weight, down_weight, mixture, parts,
-        own_gates, ffn, resid, cotangent, gain, router, weight,
-    )
-    return (
-        mixture.reshape(full, width), grads, grad_resid, grad_attn.reshape(full, width),
-        grad_mixed.reshape(full, mixed_width), grad_router, gain_grad,
-    )
-
-
-def attention_heads_backward(
-    raw_ref, query_low_ref, key_low_ref, value_low_ref, inverse_ref, mixed_ref, grad_mixed_ref, query_gain_ref,
-    cos_ref, sin_ref, col_ref, row_ref, grad_query_ref, grad_key_ref, grad_value_ref, grad_gain_ref,
+        name="second_expert",
+    )(gates, rows_all, cotangents, gate_weight, up_weight, down_weight, parts.reshape(n, 2 * length, sent))
+
+
+def attention_block_backward(
+    span_of, raw_ref, query_low_ref, key_low_ref, value_low_ref, inverse_ref, mixed_ref, grad_mixed_ref,
+    query_gain_ref, cos_ref, sin_ref, col_ref, row_ref, grad_query_ref, grad_key_ref, grad_value_ref, grad_gain_ref,
 ):
-    length, head_size = key_low_ref.shape
+    begin, rows, first, keys = span_of
+    head_size = key_low_ref.shape[1]
     heads = query_low_ref.shape[1] // head_size
-    grad_key_ref[...] = jnp.zeros_like(grad_key_ref)
-    grad_value_ref[...] = jnp.zeros_like(grad_value_ref)
-    grad_gain_ref[...] = jnp.zeros_like(grad_gain_ref)
+    block, span = pl.ds(begin, rows), pl.ds(first, keys)
 
     @pl.loop(0, heads)
     def each(head):
         columns = pl.ds(pl.multiple_of(head * head_size, head_size), head_size)
-        for begin, rows, first, keys in key_spans(length):
-            block, span = pl.ds(begin, rows), pl.ds(first, keys)
-            query_low = query_low_ref[block, columns]
-            key_low = key_low_ref[span]
-            scaled = grad_mixed_ref[block, columns].astype(high) * inverse_ref[block, columns]
-            row_term = jnp.sum(scaled * mixed_ref[block, columns].astype(high), axis=-1, keepdims=True)
-            scaled = scaled.astype(low)
-            scores = dot_last(query_low, key_low)
-            allowed = tile_mask(col_ref, row_ref, begin, rows, first, keys)
-            terms = jnp.where(allowed, jnp.exp2(scores), 0.0)
-            grad_probs = dot_last(scaled, value_low_ref[span])
-            grad_scores = (terms * (grad_probs - row_term)).astype(low)
-            grad_value_ref[span] += dot_first(terms.astype(low), scaled)
-            grad_key_ref[span] += dot_first(grad_scores, query_low) * (1.0 / log2e)
-            grad_rotated = dot(grad_scores, key_low) * head_size**-0.5
-            grad_normed = unrotate(grad_rotated, cos_ref[block], sin_ref[block])
-            grad_raw, gain_rows = norm_back(raw_ref[block, columns], query_gain_ref[...], grad_normed)
-            grad_query_ref[block, columns] = grad_raw.astype(low)
-            grad_gain_ref[...] += jnp.broadcast_to(
-                jnp.sum(gain_rows, axis=0, keepdims=True), grad_gain_ref.shape
-            )
+        query_low = query_low_ref[block, columns]
+        key_low = key_low_ref[span]
+        scaled = grad_mixed_ref[block, columns].astype(high) * inverse_ref[block, columns]
+        row_term = jnp.sum(scaled * mixed_ref[block, columns].astype(high), axis=-1, keepdims=True)
+        scaled = scaled.astype(low)
+        scores = dot_last(query_low, key_low)
+        allowed = tile_mask(col_ref, row_ref, begin, rows, first, keys)
+        terms = jnp.where(allowed, jnp.exp2(scores), 0.0)
+        grad_probs = dot_last(scaled, value_low_ref[span])
+        grad_scores = (terms * (grad_probs - row_term)).astype(low)
+        grad_value_ref[span] += dot_first(terms.astype(low), scaled)
+        grad_key_ref[span] += dot_first(grad_scores, query_low) * (1.0 / log2e)
+        grad_rotated = dot(grad_scores, key_low) * head_size**-0.5
+        grad_normed = unrotate(grad_rotated, cos_ref[block], sin_ref[block])
+        grad_raw, gain_rows = norm_back(raw_ref[block, columns], query_gain_ref[...], grad_normed)
+        grad_query_ref[block, columns] = grad_raw.astype(low)
+        grad_gain_ref[...] += jnp.broadcast_to(jnp.sum(gain_rows, axis=0, keepdims=True), grad_gain_ref.shape)
 
 
 def input_kernel(
+    sums_ref, own_gates_ref, ffn_ref, resid_ref, cot_ref, gain_ffn_ref, router_in, weight_ref,
     query_gain_ref, key_gain_ref, row_ref, tokens_ref, gain_ref,
-    raw_hbm, query_low_hbm, key_low_hbm, value_low_hbm, inverse_hbm, mixed_hbm, grad_mixed_hbm, cos_hbm, sin_hbm,
-    col_hbm, projection_hbm, attn_hbm, hidden_hbm, resid_hbm,
-    input_grad_ref, gain_grad_ref, query_gain_grad_ref, key_gain_grad_ref, projection_grad_hbm, out_grad_hbm,
-    raw_ref, query_low_ref, key_low_ref, value_low_ref, inverse_ref, mixed_ref, grad_mixed_ref, cos_ref, sin_ref,
-    col_ref, projection_ref, attn_ref, hidden_ref, resid_ref,
-    own_pair, their_pair, key_part, value_part, columns, weight, total, parts, projection_grad, out_grad,
-    load_sems, store_sems, swap_send, swap_recv, pair, flow, *scatter_sems,
+    raw_hbm, query_low_hbm, key_low_hbm, value_low_hbm, inverse_hbm, mixed_hbm, cos_hbm, sin_hbm, col_hbm,
+    projection_hbm, hidden_hbm,
+    input_grad_ref, out_own_ref, gain_grad_ref, ffn_gain_grad_ref, query_gain_grad_ref, key_gain_grad_ref,
+    router_grad_ref, projection_grad_hbm,
+    raw_ref, query_low_ref, key_low_ref, value_low_ref, inverse_ref, mixed_ref, cos_ref, sin_ref, col_ref,
+    projection_ref, hidden_ref,
+    router_ref, own, attn_ref, grad_mixed, grad_resid, own_pair, their_pair, key_part, value_part, columns, weight,
+    total, parts, projection_grad, out_grad, load_sems, store_sem, swap_send, swap_recv, port_send, port_recv,
+    send_a, recv_a, local_a, send_b, recv_b, local_b, pair, flow, *rest,
 ):
     chain = Chain()
     n = chain.n
+    scatter_sems, square_buffers = rest[:4], rest[4:]
     full, head_size = key_part.shape
+    _, _, rows, width = attn_ref.shape
+    query_width = query_low_ref.shape[1]
     sources = (
-        raw_hbm, query_low_hbm, key_low_hbm, value_low_hbm, inverse_hbm, mixed_hbm, grad_mixed_hbm, cos_hbm,
-        sin_hbm, col_hbm, projection_hbm, attn_hbm, hidden_hbm, resid_hbm,
+        raw_hbm, query_low_hbm, key_low_hbm, value_low_hbm, inverse_hbm, mixed_hbm, cos_hbm, sin_hbm, col_hbm,
+        projection_hbm, hidden_hbm,
     )
     targets = (
-        raw_ref, query_low_ref, key_low_ref, value_low_ref, inverse_ref, mixed_ref, grad_mixed_ref, cos_ref,
-        sin_ref, col_ref, projection_ref, attn_ref, hidden_ref, resid_ref,
+        raw_ref, query_low_ref, key_low_ref, value_low_ref, inverse_ref, mixed_ref, cos_ref, sin_ref, col_ref,
+        projection_ref, hidden_ref,
     )
     loads = [
         pltpu.make_async_copy(source, target, load_sems.at[at])
@@ -1368,15 +1338,58 @@
     ]
     for load in loads:
         load.start()
-    query_width = query_low_ref.shape[1]
-    wait_all(loads[:10])
-    attention_heads_backward(
-        raw_ref, query_low_ref, key_low_ref, value_low_ref, inverse_ref, mixed_ref, grad_mixed_ref, query_gain_ref,
-        cos_ref, sin_ref, col_ref, row_ref, columns, key_part, value_part, query_gain_grad_ref,
-    )
+    _, _, _, from_x, from_y = square()
+    router_ref[...] = jnp.zeros_like(router_ref)
+    router_ref[: router_in.shape[0]] = router_in[...]
+    sent = sums_ref[:, width:]
+    left = lax.broadcasted_iota(jnp.int32, sent.shape, 1) < 64
+    grad_gates = jnp.where(left, sent + pltpu.roll(sent, 64, 1), 0.0)
+    gates = own_gates_ref[...]
+    inner = jnp.sum(gates * grad_gates, axis=-1, keepdims=True)
+    grad_logits = (gates * (grad_gates - inner)).astype(low)
+    grad_hidden = sums_ref[:, :width] + dot(grad_logits, router_ref[...])
+    grad_rows, gain_rows = norm_back(resid_ref[...], gain_ffn_ref[...], grad_hidden)
+    grad_resid[...] = cot_ref[...].astype(high) + grad_rows
+    own[...] = grad_resid[...].astype(low).reshape(2, rows, width)
+    chain.greet([{"dp": from_x}, {"dp": from_y}])
+    gathers = [
+        Gather(chain, own.at[half], lambda z, c, half=half: attn_ref.at[2 * z + c, half], *sems)
+        for half, sems in enumerate(((send_a, recv_a, local_a), (send_b, recv_b, local_b)))
+    ]
+    for gather in gathers:
+        gather.begin()
+    router_grad_ref[...] = dot_first(grad_logits, ffn_ref[...])[: router_grad_ref.shape[0]]
+    ffn_gain_grad_ref[...] = jnp.broadcast_to(
+        jnp.sum(gain_rows, axis=0, keepdims=True), ffn_gain_grad_ref.shape
+    )
+    key_part[...] = jnp.zeros_like(key_part)
+    value_part[...] = jnp.zeros_like(value_part)
+    query_gain_grad_ref[...] = jnp.zeros_like(query_gain_grad_ref)
+    wait_all(loads[:9])
+    spans = key_spans(full)
+
+    @pl.loop(0, n)
+    def blocks(step):
+        z = chain.nearest(step)
+        for gather in gathers:
+            pl.when(step > 0)(lambda: gather.service(step))
+        for gather in gathers:
+            pl.when(step == 0)(lambda: gather.keep().wait())
+            gather.wait_sibling(z)
+        tokens = pl.ds(pl.multiple_of(z * 4 * rows, 4 * rows), 4 * rows)
+        grad_mixed[tokens] = dot_last(Split.take(attn_ref, z, Split.both), weight_ref[...]).astype(low)
+        for at, span_of in enumerate(spans):
+
+            @pl.when(z == at)
+            def backward():
+                attention_block_backward(
+                    span_of, raw_ref, query_low_ref, key_low_ref, value_low_ref, inverse_ref, mixed_ref, grad_mixed,
+                    query_gain_ref, cos_ref, sin_ref, col_ref, row_ref, columns, key_part, value_part,
+                    query_gain_grad_ref,
+                )
+
     own_pair[:, :head_size] = key_part[...].astype(low)
     own_pair[:, head_size:] = value_part[...].astype(low)
-    chain.greet()
     swap = pltpu.make_async_remote_copy(
         src_ref=own_pair,
         dst_ref=their_pair,
@@ -1387,7 +1400,7 @@
     )
     swap.start()
     first = chain.c == 0
-    loads[10].wait()
+    wait_all(loads[9:])
     weight[:, :query_width] = projection_ref[:, :query_width]
     weight[:, query_width:] = jnp.where(
         first,
@@ -1406,88 +1419,114 @@
     key_gain_grad_ref[...] = jnp.broadcast_to(key_gain, key_gain_grad_ref.shape)
     pair_rows = parts.shape[1]
     scatter = Scatter(chain, chip_block(parts, pair_rows // 2), pair, flow, *scatter_sems)
-    wait_all(loads[11:])
+    ports = Ports(port_send, port_recv)
+    out_total = SquareSum(out_grad, out_own_ref, *square_buffers, ports)
     projection_tile = projection_grad.shape[0] // n
-    out_tile = out_grad.shape[1] // n
+    out_tile = width // n
 
     @pl.loop(0, n)
     def each(step):
         z = chain.nearest(n - 1 - step)
-        rows = pl.ds(pl.multiple_of(z * pair_rows, pair_rows), pair_rows)
-        parts[z] = dot_last(columns[rows], weight[...]).astype(low)
+        tokens = pl.ds(pl.multiple_of(z * pair_rows, pair_rows), pair_rows)
+        parts[z] = dot_last(columns[tokens], weight[...]).astype(low)
         scatter.start_pair(z)
         pl.when(step < n - 1)(lambda: scatter.step(n - 1 - step))
+
+        @pl.when(step == 0)
+        def out_gradient():
+            @pl.loop(0, n)
+            def tiles(at):
+                span = pl.ds(pl.multiple_of(at * out_tile, out_tile), out_tile)
+                out_grad[:, span] = dot_first(mixed_ref[...], Split.every(attn_ref, span)).astype(low)
+
+            out_total.begin()
+
         span = pl.ds(pl.multiple_of(step * projection_tile, projection_tile), projection_tile)
         projection_grad[span] = dot_first(hidden_ref[:, span], columns[...]).astype(low)
-        span = pl.ds(pl.multiple_of(step * out_tile, out_tile), out_tile)
-        out_grad[:, span] = dot_first(mixed_ref[...], attn_ref[:, span]).astype(low)
-
-    stores = [
-        pltpu.make_async_copy(projection_grad, projection_grad_hbm, store_sems.at[0]),
-        pltpu.make_async_copy(out_grad, out_grad_hbm, store_sems.at[1]),
-    ]
-    for store in stores:
-        store.start()
+
+    projection_store = pltpu.make_async_copy(projection_grad, projection_grad_hbm, store_sem)
+    projection_store.start()
+    out_total.exchange()
     scatter.total(total)
     grad_rows, gain_rows = norm_back(tokens_ref[...].astype(high), gain_ref[...], total[...])
-    input_grad_ref[...] = resid_ref[...] + grad_rows
+    input_grad_ref[...] = grad_resid[...] + grad_rows
     gain_grad_ref[...] = jnp.broadcast_to(jnp.sum(gain_rows, axis=0, keepdims=True), gain_grad_ref.shape)
+    out_total.settle()
     swap.wait_send()
+    for gather in gathers:
+        gather.finish()
     scatter.finish()
-    wait_all(stores)
+    ports.finish()
+    projection_store.wait()
 
 
 def run_input(
-    raw, query_low, key_low, value_low, inverse, mixed, grad_mixed, query_gain, key_gain, cosines, sines, seg_col,
-    seg_row, projection, hidden, grad_attn, grad_resid, tokens, gain, peers,
+    sums, own_gates, ffn, resid, cotangent, gain_ffn, router, out_weight, raw, query_low, key_low, value_low,
+    inverse, mixed, query_gain, key_gain, cosines, sines, seg_col, seg_row, projection, hidden, tokens, gain,
+    experts, peers,
 ):
     length, width = tokens.shape
-    n = peers // 2
+    n, rows = peers // 2, length // 2
     full, head_size = key_low.shape
     query_width = query_low.shape[1]
     loaded = [
-        raw, query_low, key_low, value_low, inverse, mixed, grad_mixed, cosines, sines, seg_col, projection,
-        grad_attn, hidden, grad_resid,
+        raw, query_low, key_low, value_low, inverse, mixed, cosines, sines, seg_col, projection, hidden,
     ]
     dma = pltpu.SemaphoreType.DMA
-    input_grad, gain_grad, query_gain_grad, key_gain_grad, projection_grad, out_grad = pl.pallas_call(
-        input_kernel,
-        out_shape=[
-            jax.ShapeDtypeStruct((length, width), high),
-            jax.ShapeDtypeStruct((8, width), high),
-            jax.ShapeDtypeStruct((8, head_size), high),
-            jax.ShapeDtypeStruct((8, head_size), high),
-            jax.ShapeDtypeStruct((width, query_width + head_size), low),
-            jax.ShapeDtypeStruct((query_width, width), low),
-        ],
-        in_specs=[VMEM] * 5 + [ANY] * len(loaded),
-        out_specs=[VMEM] * 4 + [ANY] * 2,
-        scratch_shapes=[
-            *[pltpu.VMEM(array.shape, array.dtype) for array in loaded],
-            pltpu.VMEM((full, 2 * head_size), low),
-            pltpu.VMEM((full, 2 * head_size), low),
-            pltpu.VMEM((full, head_size), high),
-            pltpu.VMEM((full, head_size), high),
-            pltpu.VMEM((full, query_width + head_size), low),
-            pltpu.VMEM((width, query_width + head_size), low),
-            pltpu.VMEM((length, width), high),
-            pltpu.VMEM((n, 2 * length, width), low),
-            pltpu.VMEM((width, query_width + head_size), low),
-            pltpu.VMEM((query_width, width), low),
-            dma((len(loaded),)), dma((2,)), dma(()), dma(()),
-            *Scatter.buffers(n, length, width),
-        ],
-        compiler_params=communicating(5),
-        cost_estimate=pl.CostEstimate(flops=0, bytes_accessed=64 << 20, transcendentals=0),
-        name="attention_backward_and_input",
-    )(query_gain, key_gain, seg_row, tokens, gain, *loaded)
-    return input_grad, projection_grad, out_grad, gain_grad, query_gain_grad, key_gain_grad
+    input_grad, out_own, gain_grad, ffn_gain_grad, query_gain_grad, key_gain_grad, router_grad, projection_grad = (
+        pl.pallas_call(
+            input_kernel,
+            out_shape=[
+                jax.ShapeDtypeStruct((length, width), high),
+                jax.ShapeDtypeStruct((query_width // 4, width), low),
+                jax.ShapeDtypeStruct((8, width), high),
+                jax.ShapeDtypeStruct((8, width), high),
+                jax.ShapeDtypeStruct((8, head_size), high),
+                jax.ShapeDtypeStruct((8, head_size), high),
+                jax.ShapeDtypeStruct((experts, width), high),
+                jax.ShapeDtypeStruct((width, query_width + head_size), low),
+            ],
+            in_specs=[VMEM] * 13 + [ANY] * len(loaded),
+            out_specs=[VMEM] * 7 + [ANY],
+            scratch_shapes=[
+                *[pltpu.VMEM(array.shape, array.dtype) for array in loaded],
+                pltpu.VMEM((128, width), low),
+                pltpu.VMEM((2, rows, width), low),
+                pltpu.VMEM((peers, 2, rows, width), low),
+                pltpu.VMEM((full, query_width), low),
+                pltpu.VMEM((length, width), high),
+                pltpu.VMEM((full, 2 * head_size), low),
+                pltpu.VMEM((full, 2 * head_size), low),
+                pltpu.VMEM((full, head_size), high),
+                pltpu.VMEM((full, head_size), high),
+                pltpu.VMEM((full, query_width + head_size), low),
+                pltpu.VMEM((width, query_width + head_size), low),
+                pltpu.VMEM((length, width), high),
+                pltpu.VMEM((n, 2 * length, width), low),
+                pltpu.VMEM((width, query_width + head_size), low),
+                pltpu.VMEM((query_width, width), low),
+                dma((len(loaded),)), dma(()), dma(()), dma(()), dma((6,)), dma((6,)),
+                *Gather.semaphores(n) * 2,
+                *Scatter.buffers(n, length, width),
+                *SquareSum.buffers(query_width, width),
+            ],
+            compiler_params=communicating(5),
+            cost_estimate=pl.CostEstimate(flops=0, bytes_accessed=64 << 20, transcendentals=0),
+            name="attention_backward_and_input",
+        )(
+            sums, own_gates.reshape(length, 128), ffn.reshape(length, width), resid, cotangent, gain_ffn, router,
+            out_weight, query_gain, key_gain, seg_row, tokens, gain, *loaded,
+        )
+    )
+    return (
+        input_grad, projection_grad, out_own, gain_grad, ffn_gain_grad, query_gain_grad, key_gain_grad, router_grad,
+    )
 def weights_kernel(
-    proj_ref, out_ref, attn_gain_ref, ffn_gain_ref, query_gain_ref, key_gain_ref, router_ref, resid_ref,
-    mixture_ref,
+    attn_gain_ref, ffn_gain_ref, query_gain_ref, key_gain_ref, router_ref, out_own_ref, proj_hbm, resid_hbm,
+    gated_0, gated_1, down_hbm,
     query_grad_ref, key_grad_ref, value_grad_ref, out_grad_ref, small_out_ref, output_ref,
-    all_proj, first_a, first_b, out_first_a, out_first_b, second_a, second_b, out_second_a, out_second_b,
-    send_a, send_b, out_send_a, out_send_b, quarter, small, got, part, small_sum, total_mixture,
+    proj_ref, resid_ref, gated, down_w, mixture, load_sems, all_proj, first_a, first_b, second_a, second_b,
+    send_a, send_b, quarter, small, got, part, small_sum, total_mixture,
     port_send, port_recv, swap_send, swap_recv, send_1, recv_1, send_2, recv_2, send_3, recv_3,
     pair, flow, *scatter_sems,
 ):
@@ -1496,8 +1535,19 @@
     group, y, x, from_x, from_y = square()
     beside, across = {"dp": from_x}, {"dp": from_y}
     chain = Chain()
-    scatter = Scatter(chain, chip_block(mixture_ref, resid_ref.shape[0]), pair, flow, *scatter_sems)
-    width = out_ref.shape[1]
+    scatter = Scatter(chain, chip_block(mixture, resid_ref.shape[0]), pair, flow, *scatter_sems)
+    loads = [
+        pltpu.make_async_copy(source, target, load_sems.at[at])
+        for at, (source, target) in enumerate(
+            (
+                (proj_hbm, proj_ref), (gated_0, gated.at[0]), (gated_1, gated.at[1]),
+                (down_hbm, down_w), (resid_hbm, resid_ref),
+            )
+        )
+    ]
+    for load in loads:
+        load.start()
+    width = resid_ref.shape[1]
     head_size = query_gain_ref.shape[1]
     small[...] = jnp.zeros_like(small)
     small[0:1] = attn_gain_ref[0:1]
@@ -1521,15 +1571,10 @@
 
     shard_rows, columns = proj_ref.shape[1:]
     rows, half = shard_rows // 4, peers // 2
-    out_rows = out_ref.shape[0] // 4
-    middle = width // 2
     ports = Ports(port_send, port_recv)
 
-    def proj_part(side, q):
-        return proj_ref.at[pl.ds(side * half, half), pl.ds(pl.multiple_of(q * rows, rows), rows)]
-
-    def out_part(ref, side, q):
-        return ref.at[pl.ds(pl.multiple_of(q * out_rows, out_rows), out_rows), pl.ds(side * middle, middle)]
+    def proj_part(side, q, ref=proj_ref):
+        return ref.at[pl.ds(side * half, half), pl.ds(pl.multiple_of(q * rows, rows), rows)]
 
     def remote(source, target, send, recv, device):
         return pltpu.make_async_remote_copy(
@@ -1538,12 +1583,12 @@
 
     along_x = [2 * other + 1 - x for other in range(2)]
     along_y = [2 * (1 - y) + other for other in range(2)]
-    out_1a = [ports.copy(out_part(out_ref, 0, along_x[k]), out_first_a.at[k], beside) for k in range(2)]
-    out_1b = [ports.copy(out_part(out_ref, 1, along_y[k]), out_first_b.at[k], across) for k in range(2)]
-    proj_1a = [ports.copy(proj_part(0, along_x[k]), first_a.at[k], beside) for k in range(2)]
-    proj_1b = [ports.copy(proj_part(1, along_y[k]), first_b.at[k], across) for k in range(2)]
-    for copy in out_1a + out_1b + proj_1a + proj_1b:
+    proj_1a = [ports.copy(proj_part(0, along_x[k], proj_hbm), first_a.at[k], beside) for k in range(2)]
+    proj_1b = [ports.copy(proj_part(1, along_y[k], proj_hbm), first_b.at[k], across) for k in range(2)]
+    for copy in proj_1a + proj_1b:
         copy.start()
+    out_copy = SquareCopy(out_own_ref, out_grad_ref, ports)
+    out_copy.begin()
 
     small_1 = [
         remote(small_piece(small, peer), got.at[me], send_1.at[at], recv_1.at[me], {"expert": peer})
@@ -1552,23 +1597,25 @@
     for copy in small_1:
         copy.start()
     got[me] = small_piece(small, me)[...]
-    for z in range(chain.n):
-        scatter.start_pair(jnp.int32(z))
+    wait_all(loads)
+
+    def mixture_rows(step):
+        z = chain.nearest(chain.n - 1 - step)
+
+        @pl.loop(0, 4)
+        def columns(at):
+            span = pl.ds(pl.multiple_of(at * (width // 4), width // 4), width // 4)
+            mixture[z, :, span] = (dot(gated[0, z], down_w[0, :, span]) + dot(gated[1, z], down_w[1, :, span])).astype(low)
+
+        scatter.start_pair(z)
+
+    @pl.loop(0, chain.n)
+    def each_chip(step):
+        mixture_rows(step)
+
 
     own = group
-    for copy in out_1a + out_1b:
-        copy.wait_recv()
     for_y, for_x = 2 * (1 - y) + x, 2 * y + 1 - x
-    out_send_a[...] = (
-        out_part(out_ref, 0, for_y)[...].astype(high) + out_first_a[1 - y].astype(high)
-    ).astype(low)
-    out_send_b[...] = (
-        out_part(out_ref, 1, for_x)[...].astype(high) + out_first_b[1 - x].astype(high)
-    ).astype(low)
-    out_2a = ports.copy(out_send_a, out_second_a, across)
-    out_2b = ports.copy(out_send_b, out_second_b, beside)
-    out_2a.start()
-    out_2b.start()
     scatter.step(3) if chain.n > 3 else None
     for copy in proj_1a + proj_1b:
         copy.wait_recv()
@@ -1579,6 +1626,7 @@
     proj_2a.start()
     proj_2b.start()
     scatter.step(2) if chain.n > 2 else None
+    out_copy.hand_on()
 
     for at, peer in enumerate(others):
         remote(got.at[peer], got.at[peer], send_1.at[at], recv_1.at[peer], {"expert": peer}).wait_recv()
@@ -1593,19 +1641,6 @@
     for copy in small_2:
         copy.start()
 
-    out_2a.wait_recv()
-    out_2b.wait_recv()
-    for side, first, second, at in ((0, out_first_a, out_second_a, y), (1, out_first_b, out_second_b, x)):
-        out_part(out_grad_ref, side, own)[...] = (
-            out_part(out_ref, side, own)[...].astype(high) + first[at].astype(high) + second[...].astype(high)
-        ).astype(low)
-
-    def out_quarter(q):
-        return out_grad_ref.at[pl.ds(pl.multiple_of(q * out_rows, out_rows), out_rows)]
-
-    out_gx = ports.copy(out_quarter(own), out_quarter(own), beside)
-    out_gy = ports.copy(out_quarter(own), out_quarter(own), across)
-
     proj_2a.wait_recv()
     proj_2b.wait_recv()
     for side, first, second, at in ((0, first_a, second_a, y), (1, first_b, second_b, x)):
@@ -1618,8 +1653,6 @@
     ]
     for copy in swaps:
         copy.start()
-    out_gx.start()
-    out_gy.start()
     all_proj[own, me] = quarter[me]
 
     for at, other in enumerate(groups):
@@ -1642,13 +1675,7 @@
     proj_gy = ports.copy(all_proj.at[own], all_proj.at[own], across)
     proj_gx.start()
     proj_gy.start()
-    out_gx.wait_recv()
-    out_gy.wait_recv()
     far = 3 - group
-    out_fa = ports.copy(out_part(out_grad_ref, 0, from_x), out_part(out_grad_ref, 0, from_x), across)
-    out_fb = ports.copy(out_part(out_grad_ref, 1, from_y), out_part(out_grad_ref, 1, from_y), beside)
-    out_fa.start()
-    out_fb.start()
     scatter.step(1) if chain.n > 1 else None
 
     def proj_half(q, side):
@@ -1680,8 +1707,7 @@
         small_out_ref[:, peer * piece : (peer + 1) * piece] = small_sum[peer]
     scatter.total(total_mixture)
     output_ref[...] = (resid_ref[...] + total_mixture[...]).astype(low)
-    out_fa.wait_recv()
-    out_fb.wait_recv()
+    out_copy.finish()
     proj_fa.wait_recv()
     proj_fb.wait_recv()
     spread(far)
@@ -1692,7 +1718,8 @@
 
 
 def run_weights(
-    grad_projection, grad_out, attn_gain, ffn_gain, query_gain, key_gain, router, resid, mixture, peers, kv_heads
+    grad_projection, out_own, attn_gain, ffn_gain, query_gain, key_gain, router, resid, first_gated, second_gated,
+    down_weight, peers, kv_heads,
 ):
     width, columns = grad_projection.shape
     head_size = query_gain.shape[1]
@@ -1700,9 +1727,9 @@
     n = peers // 2
     shard_rows = width // peers
     rows, half = shard_rows // 4, peers // 2
-    out_rows, middle = grad_out.shape[0] // 4, grad_out.shape[1] // 2
     small_rows = 8 + router.shape[0]
     piece = (small_rows, width // peers)
+    hidden = down_weight.shape[1]
     dma = pltpu.SemaphoreType.DMA
     kv_width = kv_heads * head_size
     query_width = columns - head_size
@@ -1716,33 +1743,33 @@
             jax.ShapeDtypeStruct((shard_rows, peers * query_width), low),
             jax.ShapeDtypeStruct((shard_rows, kv_width), low),
             jax.ShapeDtypeStruct((shard_rows, kv_width), low),
-            jax.ShapeDtypeStruct(grad_out.shape, low),
+            jax.ShapeDtypeStruct((4 * out_own.shape[0], width), low),
             jax.ShapeDtypeStruct((small_rows, width), high),
             jax.ShapeDtypeStruct((length, width), low),
         ],
-        in_specs=[VMEM] * 9,
+        in_specs=[VMEM] * 6 + [ANY] * 5,
         out_specs=[VMEM] * 6,
         scratch_shapes=[
+            low_buffer(peers, shard_rows, columns),
+            pltpu.VMEM(resid.shape, high),
+            low_buffer(2, n, 2 * length, hidden),
+            low_buffer(*down_weight.shape),
+            low_buffer(n, 2 * length, width),
+            dma((5,)),
             low_buffer(4, peers, rows, columns),
             low_buffer(2, half, rows, columns),
             low_buffer(2, half, rows, columns),
-            low_buffer(2, out_rows, middle),
-            low_buffer(2, out_rows, middle),
             low_buffer(half, rows, columns),
             low_buffer(half, rows, columns),
-            low_buffer(out_rows, middle),
-            low_buffer(out_rows, middle),
             low_buffer(half, rows, columns),
             low_buffer(half, rows, columns),
-            low_buffer(out_rows, middle),
-            low_buffer(out_rows, middle),
             low_buffer(peers, rows, columns),
             pltpu.VMEM((small_rows, width), high),
             pltpu.VMEM((peers, *piece), high),
             pltpu.VMEM((4, *piece), high),
             pltpu.VMEM((peers, *piece), high),
             pltpu.VMEM((length, width), high),
-            dma((20,)), dma((20,)),
+            dma((14,)), dma((14,)),
             dma((peers - 1,)), dma((peers,)),
             dma((peers - 1,)), dma((peers,)),
             dma((3,)), dma((4,)),
@@ -1753,14 +1780,16 @@
         cost_estimate=pl.CostEstimate(flops=0, bytes_accessed=64 << 20, transcendentals=0),
         name="sum_weight_gradients",
     )(
-        grad_projection.reshape(peers, shard_rows, columns), grad_out, attn_gain, ffn_gain, query_gain, key_gain,
-        router, resid, mixture.reshape(n, 2 * length, width),
+        attn_gain, ffn_gain, query_gain, key_gain, router, out_own, grad_projection.reshape(peers, shard_rows, columns),
+        resid, first_gated.reshape(n, 2 * length, hidden), second_gated.reshape(n, 2 * length, hidden),
+        down_weight,
     )
 
 
 def widen_kernel(
-    wide_0, down_0, wide_1, down_1, query_in, key_in, value_in, out_in,
+    wide_0, down_0, wide_1, down_1, query_in, key_in, value_in, out_in, small_ref,
     gate_ref, up_ref, down_ref, query_ref, key_ref, value_ref, out_ref,
+    attn_gain_ref, ffn_gain_ref, query_gain_ref, key_gain_ref, router_ref,
 ):
     for expert, (wide, down) in enumerate(((wide_0, down_0), (wide_1, down_1))):
 
@@ -1774,8 +1803,16 @@
     for source, target in ((query_in, query_ref), (key_in, key_ref), (value_in, value_ref), (out_in, out_ref)):
         target[...] = source[...].astype(high)
 
-
-def run_widen(grads, weight_grads, hidden_units, model_width, groups):
+    @pl.when((pl.program_id(0) == 0) & (pl.program_id(1) == 0))
+    def small():
+        attn_gain_ref[...] = small_ref[0]
+        ffn_gain_ref[...] = small_ref[1]
+        query_gain_ref[...] = small_ref[2, : query_gain_ref.shape[0]]
+        key_gain_ref[...] = small_ref[3, : key_gain_ref.shape[0]]
+        router_ref[...] = small_ref[8:]
+
+
+def run_widen(grads, weight_grads, small, head_size, hidden_units, model_width, groups):
     piece, tile = hidden_units // groups, model_width // groups
     operands, specs = [], []
 
@@ -1790,6 +1827,9 @@
             pl.BlockSpec((piece, tile), lambda x, j, turn=turn: (2 * groups + turn(x, j), 0)),
         ]
     steps = 2 * groups
+    small_shapes = [
+        (model_width,), (model_width,), (head_size,), (head_size,), (small.shape[0] - 8, model_width),
+    ]
 
     def rows_of(array):
         return pl.BlockSpec((array.shape[0] // steps, array.shape[1]), lambda x, j: (x * groups + j, 0))
@@ -1802,17 +1842,19 @@
             jax.ShapeDtypeStruct((2, piece, model_width), high),
             jax.ShapeDtypeStruct((2, hidden_units, tile), high),
             *[jax.ShapeDtypeStruct(array.shape, high) for array in weight_grads],
+            *[jax.ShapeDtypeStruct(shape, high) for shape in small_shapes],
         ],
-        in_specs=specs + [rows_of(array) for array in weight_grads],
+        in_specs=specs + [rows_of(array) for array in weight_grads] + [pl.BlockSpec(small.shape, lambda x, j: (0, 0))],
         out_specs=[
             pl.BlockSpec((1, piece, tile), lambda x, j: (x, 0, j)),
             pl.BlockSpec((1, piece, tile), lambda x, j: (x, 0, j)),
             pl.BlockSpec((1, piece, tile), lambda x, j: (x, j, 0)),
             *[rows_of(array) for array in weight_grads],
+            *[pl.BlockSpec(shape, lambda x, j, rank=len(shape): (0,) * rank) for shape in small_shapes],
         ],
         compiler_params=pltpu.CompilerParams(vmem_limit_bytes=60 << 20),
         name="widen",
-    )(*operands, *weight_grads)
+    )(*operands, *weight_grads, small)
 
 
 def gather_tokens(rows):
@@ -1892,42 +1934,46 @@
     router = router_weight.T
     (
         key_low, value_low, resid, ffn_local, gates, own_gates, mixed, query_low, inverse, rows_all, cotangents,
-        mixture, parts, first_grads,
+        first_gated, parts, first_grads,
     ) = run_first(
         raw, query_gain_row, key_gain_row, cosines, sines, seg_col, seg_row, out_weight, tokens, gain_ffn_row,
         all_named, router, cotangent, near, gate_weight, up_weight, down_weight, peers, groups,
     )
-    mixture, second_grads, grad_resid, grad_attn, grad_mixed, grad_router, gain_ffn_part = run_second(
-        gates, rows_all, cotangents, gate_weight, up_weight, down_weight, mixture, parts, own_gates, ffn_local,
-        resid, cotangent, gain_ffn_row, router, out_weight, experts, peers, groups,
-    )
-    grads = (first_grads, second_grads)
+    sums, second_gated, second_grads = run_second(
+        gates, rows_all, cotangents, gate_weight, up_weight, down_weight, parts, peers, groups
+    )
     grads = [
-        lax.psum_scatter(each.reshape(-1, each.shape[2]), "dp", scatter_dimension=0, tiled=True) for each in grads
+        lax.psum_scatter(each.reshape(-1, each.shape[2]), "dp", scatter_dimension=0, tiled=True)
+        for each in (first_grads, second_grads)
     ]
-    input_grad, grad_projection, grad_out, gain_attn_part, query_gain_part, key_gain_part = run_input(
-        raw, query_low, key_low, value_low, inverse, mixed, grad_mixed, query_gain_row, key_gain_row, cosines, sines,
-        seg_col, seg_row, projection, hidden, grad_attn, grad_resid, tokens, gain_attn_row, peers,
-    )
+    input_grad, grad_projection, out_own, gain_attn_part, gain_ffn_part, query_gain_part, key_gain_part, grad_router = (
+        run_input(
+            sums, own_gates, ffn_local, resid, cotangent, gain_ffn_row, router, out_weight, raw, query_low, key_low,
+            value_low, inverse, mixed, query_gain_row, key_gain_row, cosines, sines, seg_col, seg_row, projection,
+            hidden, tokens, gain_attn_row, experts, peers,
+        )
+    )
+    grads[0], grad_projection = lax.optimization_barrier((grads[0], grad_projection))
     *weight_grads, small, output = run_weights(
-        grad_projection, grad_out, gain_attn_part, gain_ffn_part, query_gain_part, key_gain_part, grad_router,
-        resid, mixture, peers, kv_heads,
-    )
-    gate_w, up_w, down_w, query_w, key_w, value_w, out_w = run_widen(
-        grads, weight_grads, hidden_units, model_width, groups
-    )
+        grad_projection, out_own, gain_attn_part, gain_ffn_part, query_gain_part, key_gain_part, grad_router,
+        resid, first_gated, second_gated, down_weight, peers, kv_heads,
+    )
+    gate_w, up_w, down_w, query_w, key_w, value_w, out_w, *sums = run_widen(
+        grads, weight_grads, small, head_size, hidden_units, model_width, groups
+    )
+    gain_attn_grad, gain_ffn_grad, query_gain_grad, key_gain_grad, router_grad = sums
     return (
         output,
         input_grad,
-        small[0],
+        gain_attn_grad,
         query_w,
         key_w,
         value_w,
-        small[2, :head_size],
-        small[3, :head_size],
+        query_gain_grad,
+        key_gain_grad,
         out_w,
-        small[1],
-        small[8:].T,
+        gain_ffn_grad,
+        router_grad.T,
         gate_w.transpose(0, 2, 1),
         up_w.transpose(0, 2, 1),
         down_w,

time: 514 us -> 479 us (0.932); the launches traced: 508 us -> 478 us
  Pallas kernels: 484 us -> 459 us
    pallas_call x1, Pallas kernels: 111 us -> 57.6 us  [run_second(): pl.pallas_call(second_kernel, out_shape=[jax.ShapeDtypeStruct((length, se...]
    pallas_call x1, Pallas kernels: 63.9 us -> 98.6 us  [run_input(): pl.pallas_call(input_kernel, out_shape=[jax.ShapeDtypeStruct((length, wid...]
  transfers between devices with their start and end apart: 2 -> 2, of which waited for: 0 -> 0; matrix products, arithmetic and copies ran while one was open for 1% -> 0% of each run, Pallas kernels for 56% -> 55%
where the time goes in v4:
time: 479 us; the launch traced here: 478 us
  Pallas kernels  459 us (96%)
  between operations  14.2 us (3%)
    pallas_call x1, Pallas kernels, run_first(): pl.pallas_call(first_kernel, out_shape=[jax.ShapeDtypeStruct((full, head_...  109 us
    pallas_call x1, Pallas kernels, run_weights(): pl.pallas_call(weights_kernel, out_shape=[jax.ShapeDtypeStruct((shard_row...  108 us
    pallas_call x1, Pallas kernels, run_input(): pl.pallas_call(input_kernel, out_shape=[jax.ShapeDtypeStruct((length, wid...  98.6 us
    pallas_call x1, Pallas kernels, run_gather(): pl.pallas_call(gather_kernel, out_shape=[jax.ShapeDtypeStruct((length * p...  73.2 us
    pallas_call x1, Pallas kernels, run_second(): pl.pallas_call(second_kernel, out_shape=[jax.ShapeDtypeStruct((length, se...  57.6 us
    pallas_call x1, Pallas kernels, run_widen(): pl.pallas_call(widen_kernel, grid=(2, groups), out_shape=[jax.ShapeDtypeS...  12.3 us
  transfers between devices with their start and end apart: 2, of which 0 were waited for; matrix products, arithmetic and copies ran while one was open for 0% of the time, Pallas kernels for 55%

profile of v4, /device:TPU:0, one launch (start us, length us, event | category | flops | bytes accessed | tf_op | source)
XLA Modules:
  0.0 478.3 jit_solution(4692580577221099991)
XLA Ops:
  7.2 0.0 copy-start.2
  7.2 0.0 reduce-scatter.3.cloned.1.call-start
  7.2 0.8 copy.33
  8.0 0.3 fusion
  8.3 0.6 convert_element_type.3.named_ref
  8.9 73.2 %gather_hidden.1 = (bf16[1024,2048]{1,0:T(8,128)(2,1)}, bf16[8,128,128]{2,1,0:T(8,128)(2,1)}, bf16[3,128,2048]{2,1,0:T(8,128)(2,1)}, bf16[8,4,64,768]{3,2,1,0:T(8,128)(2,1)}, f32[1024,768]{1,0:T(8,128)}) custom-call(bf16[128,2048]{1,0:T(8,128)(2,1)} %tokens_ref.5, f32[1,2048]{1,0:T(1,128)} %bitcast.35, bf16[128,128]{1,0:T(8,128)(2,1)} %convert_element_type.3.named_ref, ...), custom_call_target="tpu_custom_call" | custom-call | bytes 67108864 | tf_op jit(solution)/shard_map/gather_hidden/pallas_call | solution.py:776
  82.1 0.0 copy-done.2
  82.1 0.6 broadcast_in_dim.7.row_ref
  82.8 1.0 broadcast_in_dim.16.col_hbm
  83.8 108.7 %attention_and_first_expert.1 = (bf16[1024,128]{1,0:T(8,128)(2,1)}, bf16[1024,128]{1,0:T(8,128)(2,1)}, f32[128,2048]{1,0:T(8,128)}, bf16[2,64,2048]{2,1,0:T(8,12...) custom-call(f32[1,128]{1,0:T(1,128)} %bitcast.41, ...), custom_call_target="tpu_custom_call" | custom-call | bytes 125829120 | tf_op jit(solution)/shard_map/attention_and_first_expert/pallas_call | solution.py:1199
  192.5 0.0 reduce-scatter.3.cloned.1.call-update
  192.5 0.0 reduce-scatter.5.cloned.1.call-start
  192.6 57.6 %second_expert.1 = (f32[128,2176]{1,0:T(8,128)}, bf16[8,2,64,768]{3,2,1,0:T(8,128)(2,1)}, bf16[4,2304,512]{2,1,0:T(8,128)(2,1)}) custom-call(f32[8,2,64,128]{3,2,1,0:T(8,128)} %get-tuple-element.67.gates_ref, bf16[8,2,64,2048]{3,2,1,0:T(8,128)(2,1)} %get-tuple-element.68.rows_hbm, bf16[8,2,64,2048]{3,2,1,0:T(8,128)(2,1)} %get-tuple-element.69.cot_hbm, ...), custom_call_target="tpu_custom_call" | custom-call | bytes 125829120 | tf_op jit(solution)/shard_map/second_expert/pallas_call | solution.py:1255
  250.2 0.0 reduce-scatter.5.cloned.1.call-update
  250.2 98.6 %attention_backward_and_input.1 = (f32[128,2048]{1,0:T(8,128)}, bf16[128,2048]{1,0:T(8,128)(2,1)}, f32[8,2048]{1,0:T(8,128)}, f32[8,2048]{1,0:T(8,128)}, f32[8,1...) custom-call(f32[128,2176]{1,0:T(8,128)} %get-tuple-element.71.sums_ref, ...), custom_call_target="tpu_custom_call" | custom-call | bytes 67108864 | tf_op jit(solution)/shard_map/attention_backward_and_input/pallas_call | solution.py:1477
  348.9 0.0 reduce-scatter.3.cloned.1.call-done.wide_0.down_0
  348.9 108.5 %sum_weight_gradients.1 = (bf16[256,4096]{1,0:T(8,128)(2,1)}, bf16[256,512]{1,0:T(8,128)(2,1)}, bf16[256,512]{1,0:T(8,128)(2,1)}, bf16[512,2048]{1,0:T(8,128)(2,...) custom-call(f32[8,2048]{1,0:T(8,128)} %get-tuple-element.82.attn_gain_ref, f32[8,2048]{1,0:T(8,128)} %get-tuple-element.83.ffn_gain_ref, ...), custom_call_target="tpu_custom_call" | custom-call | bytes 67108864 | tf_op jit(solution)/shard_map/sum_weight_gradients/pallas_call | solution.py:1740
  457.4 0.0 reduce-scatter.5.cloned.1.call-done.wide_1.down_1
  457.4 0.0 copy-start.1
  457.4 0.0 copy-start
  457.4 12.3 %widen.1 = (f32[2,192,2048]{2,1,0:T(8,128)}, f32[2,192,2048]{2,1,0:T(8,128)}, f32[2,768,512]{2,1,0:T(8,128)}, f32[256,4096]{1,0:T(8,128)}, f32[256,512]{1,0:T(8,...) custom-call(bf16[2304,512]{1,0:T(8,128)(2,1)} %reduce-scatter.3.clon, ...), custom_call_target="tpu_custom_call" | custom-call | tf_op jit(solution)/shard_map/widen/pallas_call | solution.py:1837
  469.7 0.0 copy-done.1
  469.7 0.8 copy.36
  470.5 1.0 copy.37
  (1 shorter events, 0.0 us)
Async XLA Ops:
  7.2 75.0 %copy-start.2 = (s32[1,1024]{1,0:T(1,128)S(1)}, s32[1,1024]{1,0:T(1,128)}, u32[]{:S(2)}) copy-start(s32[1,1024]{1,0:T(1,128)} %param.19) | copy-start | bytes 12292
  7.2 341.7 %reduce-scatter.3.cloned.1.call-start = ((), (), s32[]{:S(2)}) async-start(), calls=%async_computation.2 | async-start | bytes 11796480 | tf_op jit(solution)/shard_map/reduce_scatter | solution.py:1946
  192.5 264.9 %reduce-scatter.5.cloned.1.call-start = ((), (), s32[]{:S(2)}) async-start(), calls=%async_computation.3 | async-start | bytes 11796480 | tf_op jit(solution)/shard_map/reduce_scatter | solution.py:1946
  457.4 12.3 %copy-start.1 = (bf16[128,2048]{1,0:T(8,128)(2,1)S(1)}, bf16[128,2048]{1,0:T(8,128)(2,1)}, u32[]{:S(2)}) copy-start(bf16[128,2048]{1,0:T(8,128)(2,1)} %get-tuple-element.128) | copy-start | bytes 1572868
  457.4 13.1 %copy-start = (f32[128,2048]{1,0:T(8,128)S(1)}, f32[128,2048]{1,0:T(8,128)}, u32[]{:S(2)}) copy-start(f32[128,2048]{1,0:T(8,128)} %get-tuple-element.129) | copy-start | bytes 3145732
Sparse Core Ops, SparseCore 0:
  192.6 94.5 reduce-scatter.2
  290.3 146.5 reduce-scatter.4

commit v5 on v4

--- a/solution.py
+++ b/solution.py
@@ -554,6 +554,46 @@
             self.result[:, columns] = (total + second[...].astype(high)).astype(low)
 
 
+class WideSum:
+    def __init__(self, grads):
+        self.grads = grads
+        self.own, self.y, self.x, self.from_x, self.from_y = square()
+        self.middle = grads.shape[2] // 2
+        self.beside, self.across = {"dp": self.from_x}, {"dp": self.from_y}
+
+    def part(self, side, quarter):
+        return self.grads.at[quarter, :, pl.ds(side * self.middle, self.middle)]
+
+    def first(self, first_a, first_b, ports):
+        copies = []
+        for k in range(2):
+            copies.append(ports.copy(self.part(0, 2 * k + 1 - self.x), first_a.at[k], self.beside))
+            copies.append(ports.copy(self.part(1, 2 * (1 - self.y) + k), first_b.at[k], self.across))
+        return copies
+
+    def load(self, first_a, first_b, left, right, sems):
+        pairs = (
+            (self.part(0, self.from_y), left.at[0]), (first_a.at[1 - self.y], left.at[1]),
+            (self.part(1, self.from_x), right.at[0]), (first_b.at[1 - self.x], right.at[1]),
+        )
+        return [pltpu.make_async_copy(source, target, sems.at[at]) for at, (source, target) in enumerate(pairs)]
+
+    def second(self, left, right, second_a, second_b, ports):
+        for both in (left, right):
+            both[0] = (both[0].astype(high) + both[1].astype(high)).astype(low)
+        return [
+            ports.copy(left.at[0], second_a, self.across),
+            ports.copy(right.at[0], second_b, self.beside),
+        ]
+
+
+def wide_shapes(grads):
+    _, rows, columns = grads.shape
+    first = jax.ShapeDtypeStruct((2, rows, columns // 2), low)
+    second = jax.ShapeDtypeStruct((rows, columns // 2), low)
+    return [first, first], [second, second]
+
+
 class SquareCopy:
     def __init__(self, mine, result, ports):
         own, _, _, from_x, from_y = square()
@@ -590,16 +630,16 @@
     return lambda z, c: ref.at[z, pl.ds(pl.multiple_of(c * rows, rows), rows)]
 
 
-def communicating(collective_id):
+def communicating(collective_id, mebibytes=60):
     return pltpu.CompilerParams(
-        collective_id=collective_id, has_side_effects=True, vmem_limit_bytes=60 << 20
+        collective_id=collective_id, has_side_effects=True, vmem_limit_bytes=mebibytes << 20
     )
 
 
 def gather_kernel(
-    tokens_ref, gain_ref, named_ref, cot_ref, query_hbm, key_hbm, value_hbm,
-    hidden_hbm, all_named_ref, near_ref, projection_hbm, raw_hbm,
-    own, stage, hidden_ref, projection_ref, raw_ref, query_ref, key_ref, value_ref,
+    tokens_ref, gain_ref, routes_ref, segments_ref, cot_ref, query_hbm, key_hbm, value_hbm,
+    hidden_hbm, all_named_ref, near_ref, col_ref, projection_hbm, raw_hbm,
+    named_ref, own, stage, hidden_ref, projection_ref, raw_ref, query_ref, key_ref, value_ref,
     send_a, recv_a, local_a, send_b, recv_b, local_b, name_send, name_recv,
     swap_send, swap_recv, x_send, x_recv, y_send, y_recv, far_send, far_recv, out_sems, load_sems,
     near_send, near_recv,
@@ -629,6 +669,12 @@
     query_width = query_ref.shape[1] // peers
     head_size = key_ref.shape[1] // n
     own[...] = norm_rows(tokens_ref[...].astype(high), gain_ref[...]).astype(low)
+    lanes = lax.broadcasted_iota(jnp.int32, named_ref.shape, 1)
+    named = jnp.zeros(named_ref.shape, high)
+    routes = routes_ref[...].astype(high).T.astype(jnp.int32)
+    for at in range(routes.shape[1]):
+        named = jnp.where(routes[:, at : at + 1] == lanes, 1.0, named)
+    named_ref[...] = named.astype(low)
     for load in loads:
         load.wait()
     for peer in range(peers):
@@ -674,6 +720,8 @@
     for copy in names:
         copy.start()
     all_named_ref[me] = named_ref[...]
+    row = jnp.broadcast_to(segments_ref[...].astype(high), (col_ref.shape[1], col_ref.shape[0]))
+    col_ref[...] = row.T.astype(jnp.int32)
     projection_ref[me, group] = stage[me]
 
     def to_x(at, source, place):
@@ -766,25 +814,27 @@
         raw_out(step).wait()
 
 
-def run_gather(tokens, gain, named, cotangent, query_weight, key_matrix, value_matrix, peers, groups):
+def run_gather(tokens, gain, routes, segments, cotangent, query_weight, key_matrix, value_matrix, peers, groups):
     length, width = tokens.shape
     n = peers // 2
     shard_rows, query_columns = query_weight.shape
     columns = query_columns // peers + 2 * key_matrix.shape[1] // n
     rows = shard_rows // groups
     dma = pltpu.SemaphoreType.DMA
-    hidden, all_named, near, projection, raw = pl.pallas_call(
+    hidden, all_named, near, seg_col, projection, raw = pl.pallas_call(
         gather_kernel,
         out_shape=[
             jax.ShapeDtypeStruct((length * peers, width), low),
-            jax.ShapeDtypeStruct((peers, *named.shape), named.dtype),
+            jax.ShapeDtypeStruct((peers, length, 128), low),
             jax.ShapeDtypeStruct((3, length, width), low),
+            jax.ShapeDtypeStruct((length * peers, 128), jnp.int32),
             jax.ShapeDtypeStruct((peers, groups, rows, columns), low),
             jax.ShapeDtypeStruct((length * peers, columns), high),
         ],
-        in_specs=[VMEM] * 4 + [ANY] * 3,
-        out_specs=[ANY, VMEM, VMEM, ANY, ANY],
+        in_specs=[VMEM] * 5 + [ANY] * 3,
+        out_specs=[ANY, VMEM, VMEM, VMEM, ANY, ANY],
         scratch_shapes=[
+            pltpu.VMEM((length, 128), low),
             pltpu.VMEM((length, width), low),
             pltpu.VMEM((peers, rows, columns), low),
             pltpu.VMEM((length * peers, width), low),
@@ -804,8 +854,8 @@
         compiler_params=communicating(1),
         cost_estimate=pl.CostEstimate(flops=0, bytes_accessed=64 << 20, transcendentals=0),
         name="gather_hidden",
-    )(tokens, gain, named, cotangent, query_weight, key_matrix, value_matrix)
-    return hidden, all_named, near, projection.reshape(width, columns), raw
+    )(tokens, gain, routes, segments, cotangent, query_weight, key_matrix, value_matrix)
+    return hidden, all_named, near, seg_col, projection.reshape(width, columns), raw
 
 
 def attention_heads(
@@ -897,10 +947,11 @@
         made = []
         for part in range(self.groups):
             if kind < 2:
-                target = self.grads.at[part, pl.ds(pl.multiple_of((2 * at + kind) * piece, 16), piece)]
+                columns = pl.ds(pl.multiple_of(at * self.tile, self.tile), self.tile)
+                target = self.grads.at[part, pl.ds(kind * piece, piece), columns]
             else:
-                begin = 2 * self.hidden + part * piece
-                target = self.grads.at[at, pl.ds(begin, piece)]
+                columns = pl.ds(part * self.tile, self.tile)
+                target = self.grads.at[at, pl.ds(2 * piece, piece), columns]
             source = self.stage.at[slot, pl.ds(part * piece, piece)]
             made.append(pltpu.make_async_copy(source, target, self.sems.at[slot, part]))
         return made
@@ -928,8 +979,9 @@
 def first_kernel(
     query_gain_ref, key_gain_ref, row_ref, tokens_ref, gain_ref, named_ref, router_in, cot_ref, near_ref,
     raw_hbm, cos_hbm, sin_hbm, col_hbm, weight_hbm, gate_hbm, up_hbm, down_hbm,
-    key_low_ref, value_low_ref, resid_ref, ffn_ref, gates_ref, own_gates_ref,
+    key_low_ref, value_low_ref, own_gates_ref, resid_hbm, ffn_hbm, gates_hbm,
     mixed_hbm, query_low_hbm, inverse_hbm, rows_hbm, cots_hbm, gated_hbm, parts_hbm, grads_hbm,
+    resid_ref, ffn_ref, gates_ref,
     raw_ref, cos_ref, sin_ref, col_ref, weight_ref, mixed_ref, query_low_ref, inverse_ref, value_wide, router_ref, plain, attn_parts, rows_all, cots, gate_w, up_w, down_w, gated, grad_gate, grad_up,
     part_stage, tile_stage, load_sems, rows_sems, part_sems, tile_sems, cot_send, cot_recv, cot_local, *transfers,
 ):
@@ -1075,6 +1127,9 @@
         pltpu.make_async_copy(rows_all, rows_hbm, rows_sems.at[0]),
         pltpu.make_async_copy(cots, cots_hbm, rows_sems.at[1]),
         pltpu.make_async_copy(gated, gated_hbm, rows_sems.at[5]),
+        pltpu.make_async_copy(resid_ref, resid_hbm, rows_sems.at[6]),
+        pltpu.make_async_copy(ffn_ref, ffn_hbm, rows_sems.at[7]),
+        pltpu.make_async_copy(gates_ref, gates_hbm, rows_sems.at[8]),
     ]
     for copy in whole_copies:
         copy.start()
@@ -1092,10 +1147,10 @@
 
 
 def second_kernel(
-    gates_ref, rows_hbm, cot_hbm, gate_hbm, up_hbm, down_hbm, parts_in,
-    sum_ref, gated_hbm, grads_hbm,
+    gates_ref, rows_hbm, cot_hbm, gate_hbm, up_hbm, down_hbm, parts_in, wide_hbm,
+    sum_ref, gated_hbm, grads_hbm, first_a, first_b,
     rows_all, cots, gate_w, up_w, down_w, gated, grad_gate, grad_up, parts, tile_stage, load_sems, chip_sems,
-    tile_sems, out_sem, pair, flow, *scatter_sems,
+    tile_sems, out_sem, port_send, port_recv, pair, flow, *scatter_sems,
 ):
     chain = Chain()
     n = chain.n
@@ -1123,7 +1178,11 @@
         for load in chip_loads(chain.nearest(n - 1 - step)):
             load.start()
     loads[3].start()
-    chain.greet()
+    wide = WideSum(wide_hbm)
+    chain.greet([wide.beside, wide.across])
+    ports = Ports(port_send, port_recv)
+    wide_sent = wide.first(first_a, first_b, ports)
+    SquareSum.start(wide_sent)
     scatter = Scatter(chain, chip_block(parts, block_rows // 2), pair, flow, *scatter_sems)
     lanes = lax.broadcasted_iota(jnp.int32, (block_rows, 128), 1)
     expert = lax.axis_index("expert") * gate_hbm.shape[0] + 1
@@ -1163,6 +1222,8 @@
     scatter.finish()
     tiles.finish()
     gated_copy.wait()
+    SquareSum.arrive(wide_sent)
+    ports.finish()
 
 
 def split_rows(array, peers):
@@ -1201,10 +1262,10 @@
         out_shape=[
             jax.ShapeDtypeStruct((full, head_size), low),
             jax.ShapeDtypeStruct((full, head_size), low),
+            jax.ShapeDtypeStruct((2, rows, 128), high),
             jax.ShapeDtypeStruct((length, width), high),
             jax.ShapeDtypeStruct((2, rows, width), low),
             split(128, high),
-            jax.ShapeDtypeStruct((2, rows, 128), high),
             jax.ShapeDtypeStruct((full, local_width), low),
             jax.ShapeDtypeStruct((full, local_width), low),
             jax.ShapeDtypeStruct((full, local_width), high),
@@ -1212,11 +1273,14 @@
             split(width, low),
             split(hidden, low),
             split(sent, low),
-            jax.ShapeDtypeStruct((groups, 3 * hidden, tile), low),
+            jax.ShapeDtypeStruct((groups, 3 * hidden // groups, width), low),
         ],
         in_specs=[VMEM] * 9 + [ANY] * 8,
-        out_specs=[VMEM] * 6 + [ANY] * 8,
+        out_specs=[VMEM] * 3 + [ANY] * 11,
         scratch_shapes=[
+            pltpu.VMEM((length, width), high),
+            pltpu.VMEM((2, rows, width), low),
+            pltpu.VMEM((peers, 2, rows, 128), high),
             pltpu.VMEM(raw.shape, high),
             pltpu.VMEM(cosines.shape, high),
             pltpu.VMEM(sines.shape, high),
@@ -1232,7 +1296,7 @@
             *expert_scratch(gate_weight, up_weight, down_weight, peers, rows, width),
             pltpu.VMEM((2, 2, rows, sent), low),
             pltpu.VMEM((2, hidden, tile), low),
-            dma((8,)), dma((6,)), dma((2,)), dma((2, groups)),
+            dma((8,)), dma((9,)), dma((2,)), dma((2, groups)),
             *NearGather.semaphores(n),
             *(Scatter.buffers(n, rows, width) + Gather.semaphores(n)) * 2,
         ],
@@ -1246,7 +1310,7 @@
     )
 
 
-def run_second(gates, rows_all, cotangents, gate_weight, up_weight, down_weight, parts, peers, groups):
+def run_second(gates, rows_all, cotangents, gate_weight, up_weight, down_weight, parts, first_grads, peers, groups):
     _, _, rows, width = rows_all.shape
     n, length = peers // 2, 2 * rows
     hidden = gate_weight.shape[2]
@@ -1257,21 +1321,25 @@
         out_shape=[
             jax.ShapeDtypeStruct((length, sent), high),
             jax.ShapeDtypeStruct((peers, 2, rows, hidden), low),
-            jax.ShapeDtypeStruct((groups, 3 * hidden, tile), low),
+            jax.ShapeDtypeStruct((groups, 3 * hidden // groups, width), low),
+            *wide_shapes(first_grads)[0],
         ],
-        in_specs=[VMEM] + [ANY] * 6,
-        out_specs=[VMEM, ANY, ANY],
+        in_specs=[VMEM] + [ANY] * 7,
+        out_specs=[VMEM, ANY, ANY, ANY, ANY],
         scratch_shapes=[
             *expert_scratch(gate_weight, up_weight, down_weight, peers, rows, width),
             pltpu.VMEM((n, 2 * length, sent), low),
             pltpu.VMEM((2, hidden, tile), low),
-            dma((4,)), dma((2, n)), dma((2, groups)), dma(()),
+            dma((4,)), dma((2, n)), dma((2, groups)), dma(()), dma((4,)), dma((4,)),
             *Scatter.buffers(n, length, sent),
         ],
         compiler_params=communicating(7),
         cost_estimate=pl.CostEstimate(flops=0, bytes_accessed=120 << 20, transcendentals=0),
         name="second_expert",
-    )(gates, rows_all, cotangents, gate_weight, up_weight, down_weight, parts.reshape(n, 2 * length, sent))
+    )(
+        gates, rows_all, cotangents, gate_weight, up_weight, down_weight, parts.reshape(n, 2 * length, sent),
+        first_grads,
+    )
 
 
 def attention_block_backward(
@@ -1309,13 +1377,14 @@
     sums_ref, own_gates_ref, ffn_ref, resid_ref, cot_ref, gain_ffn_ref, router_in, weight_ref,
     query_gain_ref, key_gain_ref, row_ref, tokens_ref, gain_ref,
     raw_hbm, query_low_hbm, key_low_hbm, value_low_hbm, inverse_hbm, mixed_hbm, cos_hbm, sin_hbm, col_hbm,
-    projection_hbm, hidden_hbm,
+    projection_hbm, hidden_hbm, wide_0, wide_0a, wide_0b, wide_1,
     input_grad_ref, out_own_ref, gain_grad_ref, ffn_gain_grad_ref, query_gain_grad_ref, key_gain_grad_ref,
-    router_grad_ref, projection_grad_hbm,
+    router_grad_ref, projection_grad_hbm, second_a, second_b, first_a, first_b,
     raw_ref, query_low_ref, key_low_ref, value_low_ref, inverse_ref, mixed_ref, cos_ref, sin_ref, col_ref,
     projection_ref, hidden_ref,
-    router_ref, own, attn_ref, grad_mixed, grad_resid, own_pair, their_pair, key_part, value_part, columns, weight,
-    total, parts, projection_grad, out_grad, load_sems, store_sem, swap_send, swap_recv, port_send, port_recv,
+    router_ref, own, attn_ref, grad_mixed, grad_resid, own_pair, their_pair, key_part, value_part, columns,
+    parts, projection_grad, out_grad, load_sems, store_sem, swap_send, swap_recv, port_send, port_recv,
+    wide_left, wide_right, wide_sems,
     send_a, recv_a, local_a, send_b, recv_b, local_b, pair, flow, *rest,
 ):
     chain = Chain()
@@ -1325,7 +1394,7 @@
     _, _, rows, width = attn_ref.shape
     query_width = query_low_ref.shape[1]
     sources = (
-        raw_hbm, query_low_hbm, key_low_hbm, value_low_hbm, inverse_hbm, mixed_hbm, cos_hbm, sin_hbm, col_hbm,
+        raw_hbm.at[:, pl.ds(0, query_width + head_size)], query_low_hbm, key_low_hbm, value_low_hbm, inverse_hbm, mixed_hbm, cos_hbm, sin_hbm, col_hbm,
         projection_hbm, hidden_hbm,
     )
     targets = (
@@ -1336,9 +1405,14 @@
         pltpu.make_async_copy(source, target, load_sems.at[at])
         for at, (source, target) in enumerate(zip(sources, targets))
     ]
-    for load in loads:
+    wide = WideSum(wide_0)
+    wide_loads = wide.load(wide_0a, wide_0b, wide_left, wide_right, wide_sems)
+    for load in wide_loads + loads:
         load.start()
-    _, _, _, from_x, from_y = square()
+    chain.greet([wide.beside, wide.across])
+    ports = Ports(port_send, port_recv)
+    wide_first = WideSum(wide_1).first(first_a, first_b, ports)
+    SquareSum.start(wide_first)
     router_ref[...] = jnp.zeros_like(router_ref)
     router_ref[: router_in.shape[0]] = router_in[...]
     sent = sums_ref[:, width:]
@@ -1351,13 +1425,15 @@
     grad_rows, gain_rows = norm_back(resid_ref[...], gain_ffn_ref[...], grad_hidden)
     grad_resid[...] = cot_ref[...].astype(high) + grad_rows
     own[...] = grad_resid[...].astype(low).reshape(2, rows, width)
-    chain.greet([{"dp": from_x}, {"dp": from_y}])
     gathers = [
         Gather(chain, own.at[half], lambda z, c, half=half: attn_ref.at[2 * z + c, half], *sems)
         for half, sems in enumerate(((send_a, recv_a, local_a), (send_b, recv_b, local_b)))
     ]
     for gather in gathers:
         gather.begin()
+    wait_all(wide_loads)
+    wide_second = wide.second(wide_left, wide_right, second_a, second_b, ports)
+    SquareSum.start(wide_second)
     router_grad_ref[...] = dot_first(grad_logits, ffn_ref[...])[: router_grad_ref.shape[0]]
     ffn_gain_grad_ref[...] = jnp.broadcast_to(
         jnp.sum(gain_rows, axis=0, keepdims=True), ffn_gain_grad_ref.shape
@@ -1401,16 +1477,15 @@
     swap.start()
     first = chain.c == 0
     wait_all(loads[9:])
-    weight[:, :query_width] = projection_ref[:, :query_width]
-    weight[:, query_width:] = jnp.where(
-        first,
-        projection_ref[:, query_width : query_width + head_size],
-        projection_ref[:, query_width + head_size :],
-    )
+    shared = pl.ds(query_width, head_size)
+    projection_ref[:, shared] = jnp.where(
+        first, projection_ref[:, shared], projection_ref[:, query_width + head_size :]
+    )
+    own_width = query_width + head_size
     swap.wait_recv()
     grad_key = key_part[...] + their_pair[:, :head_size].astype(high)
     grad_value = value_part[...] + their_pair[:, head_size:].astype(high)
-    key_raw = raw_ref[:, query_width : query_width + head_size]
+    key_raw = raw_ref[:, query_width:]
     grad_key, gain_rows = norm_back(
         key_raw, key_gain_ref[...], unrotate(grad_key, cos_ref[...], sin_ref[...])
     )
@@ -1419,7 +1494,6 @@
     key_gain_grad_ref[...] = jnp.broadcast_to(key_gain, key_gain_grad_ref.shape)
     pair_rows = parts.shape[1]
     scatter = Scatter(chain, chip_block(parts, pair_rows // 2), pair, flow, *scatter_sems)
-    ports = Ports(port_send, port_recv)
     out_total = SquareSum(out_grad, out_own_ref, *square_buffers, ports)
     projection_tile = projection_grad.shape[0] // n
     out_tile = width // n
@@ -1428,7 +1502,7 @@
     def each(step):
         z = chain.nearest(n - 1 - step)
         tokens = pl.ds(pl.multiple_of(z * pair_rows, pair_rows), pair_rows)
-        parts[z] = dot_last(columns[tokens], weight[...]).astype(low)
+        parts[z] = dot_last(columns[tokens], projection_ref[:, :own_width]).astype(low)
         scatter.start_pair(z)
         pl.when(step < n - 1)(lambda: scatter.step(n - 1 - step))
 
@@ -1447,11 +1521,12 @@
     projection_store = pltpu.make_async_copy(projection_grad, projection_grad_hbm, store_sem)
     projection_store.start()
     out_total.exchange()
-    scatter.total(total)
-    grad_rows, gain_rows = norm_back(tokens_ref[...].astype(high), gain_ref[...], total[...])
+    scatter.total(input_grad_ref)
+    grad_rows, gain_rows = norm_back(tokens_ref[...].astype(high), gain_ref[...], input_grad_ref[...])
     input_grad_ref[...] = grad_resid[...] + grad_rows
     gain_grad_ref[...] = jnp.broadcast_to(jnp.sum(gain_rows, axis=0, keepdims=True), gain_grad_ref.shape)
     out_total.settle()
+    SquareSum.arrive(wide_first + wide_second)
     swap.wait_send()
     for gather in gathers:
         gather.finish()
@@ -1463,7 +1538,7 @@
 def run_input(
     sums, own_gates, ffn, resid, cotangent, gain_ffn, router, out_weight, raw, query_low, key_low, value_low,
     inverse, mixed, query_gain, key_gain, cosines, sines, seg_col, seg_row, projection, hidden, tokens, gain,
-    experts, peers,
+    first_wide, second_grads, experts, peers,
 ):
     length, width = tokens.shape
     n, rows = peers // 2, length // 2
@@ -1473,7 +1548,12 @@
         raw, query_low, key_low, value_low, inverse, mixed, cosines, sines, seg_col, projection, hidden,
     ]
     dma = pltpu.SemaphoreType.DMA
-    input_grad, out_own, gain_grad, ffn_gain_grad, query_gain_grad, key_gain_grad, router_grad, projection_grad = (
+    wide_first, wide_second = wide_shapes(second_grads)
+    half = (2, *wide_second[0].shape)
+    (
+        input_grad, out_own, gain_grad, ffn_gain_grad, query_gain_grad, key_gain_grad, router_grad, projection_grad,
+        *wide,
+    ) = (
         pl.pallas_call(
             input_kernel,
             out_shape=[
@@ -1485,11 +1565,14 @@
                 jax.ShapeDtypeStruct((8, head_size), high),
                 jax.ShapeDtypeStruct((experts, width), high),
                 jax.ShapeDtypeStruct((width, query_width + head_size), low),
+                *wide_second,
+                *wide_first,
             ],
-            in_specs=[VMEM] * 13 + [ANY] * len(loaded),
-            out_specs=[VMEM] * 7 + [ANY],
+            in_specs=[VMEM] * 13 + [ANY] * (len(loaded) + 4),
+            out_specs=[VMEM] * 7 + [ANY] * 5,
             scratch_shapes=[
-                *[pltpu.VMEM(array.shape, array.dtype) for array in loaded],
+                pltpu.VMEM((full, query_width + head_size), high),
+                *[pltpu.VMEM(array.shape, array.dtype) for array in loaded[1:]],
                 pltpu.VMEM((128, width), low),
                 pltpu.VMEM((2, rows, width), low),
                 pltpu.VMEM((peers, 2, rows, width), low),
@@ -1500,35 +1583,35 @@
                 pltpu.VMEM((full, head_size), high),
                 pltpu.VMEM((full, head_size), high),
                 pltpu.VMEM((full, query_width + head_size), low),
-                pltpu.VMEM((width, query_width + head_size), low),
-                pltpu.VMEM((length, width), high),
                 pltpu.VMEM((n, 2 * length, width), low),
                 pltpu.VMEM((width, query_width + head_size), low),
                 pltpu.VMEM((query_width, width), low),
-                dma((len(loaded),)), dma(()), dma(()), dma(()), dma((6,)), dma((6,)),
+                dma((len(loaded),)), dma(()), dma(()), dma(()), dma((12,)), dma((12,)),
+                pltpu.VMEM(half, low), pltpu.VMEM(half, low), dma((4,)),
                 *Gather.semaphores(n) * 2,
                 *Scatter.buffers(n, length, width),
                 *SquareSum.buffers(query_width, width),
             ],
-            compiler_params=communicating(5),
+            compiler_params=communicating(5, 62),
             cost_estimate=pl.CostEstimate(flops=0, bytes_accessed=64 << 20, transcendentals=0),
             name="attention_backward_and_input",
         )(
             sums, own_gates.reshape(length, 128), ffn.reshape(length, width), resid, cotangent, gain_ffn, router,
-            out_weight, query_gain, key_gain, seg_row, tokens, gain, *loaded,
+            out_weight, query_gain, key_gain, seg_row, tokens, gain, *loaded, *first_wide, second_grads,
         )
     )
     return (
         input_grad, projection_grad, out_own, gain_grad, ffn_gain_grad, query_gain_grad, key_gain_grad, router_grad,
+        wide[:2], wide[2:],
     )
 def weights_kernel(
     attn_gain_ref, ffn_gain_ref, query_gain_ref, key_gain_ref, router_ref, out_own_ref, proj_hbm, resid_hbm,
-    gated_0, gated_1, down_hbm,
-    query_grad_ref, key_grad_ref, value_grad_ref, out_grad_ref, small_out_ref, output_ref,
+    gated_0, gated_1, down_hbm, wide_hbm, wide_a, wide_b,
+    query_grad_ref, key_grad_ref, value_grad_ref, out_grad_ref, small_out_ref, output_ref, wide_second_a, wide_second_b,
     proj_ref, resid_ref, gated, down_w, mixture, load_sems, all_proj, first_a, first_b, second_a, second_b,
     send_a, send_b, quarter, small, got, part, small_sum, total_mixture,
     port_send, port_recv, swap_send, swap_recv, send_1, recv_1, send_2, recv_2, send_3, recv_3,
-    pair, flow, *scatter_sems,
+    wide_left, wide_right, wide_sems, pair, flow, *scatter_sems,
 ):
     peers = lax.axis_size("expert")
     me = lax.axis_index("expert")
@@ -1545,7 +1628,9 @@
             )
         )
     ]
-    for load in loads:
+    wide = WideSum(wide_hbm)
+    wide_loads = wide.load(wide_a, wide_b, wide_left, wide_right, wide_sems)
+    for load in wide_loads + loads:
         load.start()
     width = resid_ref.shape[1]
     head_size = query_gain_ref.shape[1]
@@ -1587,8 +1672,6 @@
     proj_1b = [ports.copy(proj_part(1, along_y[k], proj_hbm), first_b.at[k], across) for k in range(2)]
     for copy in proj_1a + proj_1b:
         copy.start()
-    out_copy = SquareCopy(out_own_ref, out_grad_ref, ports)
-    out_copy.begin()
 
     small_1 = [
         remote(small_piece(small, peer), got.at[me], send_1.at[at], recv_1.at[me], {"expert": peer})
@@ -1625,8 +1708,12 @@
     proj_2b = ports.copy(send_b, second_b, beside)
     proj_2a.start()
     proj_2b.start()
+    wait_all(wide_loads)
+    wide_sent = wide.second(wide_left, wide_right, wide_second_a, wide_second_b, ports)
+    SquareSum.start(wide_sent)
+    out_copy = SquareCopy(out_own_ref, out_grad_ref, ports)
+    out_copy.begin()
     scatter.step(2) if chain.n > 2 else None
-    out_copy.hand_on()
 
     for at, peer in enumerate(others):
         remote(got.at[peer], got.at[peer], send_1.at[at], recv_1.at[peer], {"expert": peer}).wait_recv()
@@ -1677,6 +1764,7 @@
     proj_gy.start()
     far = 3 - group
     scatter.step(1) if chain.n > 1 else None
+    out_copy.hand_on()
 
     def proj_half(q, side):
         return all_proj.at[q, pl.ds(side * half, half)]
@@ -1708,6 +1796,7 @@
     scatter.total(total_mixture)
     output_ref[...] = (resid_ref[...] + total_mixture[...]).astype(low)
     out_copy.finish()
+    SquareSum.arrive(wide_sent)
     proj_fa.wait_recv()
     proj_fb.wait_recv()
     spread(far)
@@ -1719,7 +1808,7 @@
 
 def run_weights(
     grad_projection, out_own, attn_gain, ffn_gain, query_gain, key_gain, router, resid, first_gated, second_gated,
-    down_weight, peers, kv_heads,
+    down_weight, second_wide, peers, kv_heads,
 ):
     width, columns = grad_projection.shape
     head_size = query_gain.shape[1]
@@ -1734,6 +1823,9 @@
     kv_width = kv_heads * head_size
     query_width = columns - head_size
 
+    _, wide_second = wide_shapes(second_wide[0])
+    wide_half = (2, *wide_second[0].shape)
+
     def low_buffer(*shape):
         return pltpu.VMEM(shape, low)
 
@@ -1746,9 +1838,10 @@
             jax.ShapeDtypeStruct((4 * out_own.shape[0], width), low),
             jax.ShapeDtypeStruct((small_rows, width), high),
             jax.ShapeDtypeStruct((length, width), low),
+            *wide_second,
         ],
-        in_specs=[VMEM] * 6 + [ANY] * 5,
-        out_specs=[VMEM] * 6,
+        in_specs=[VMEM] * 6 + [ANY] * 8,
+        out_specs=[VMEM] * 6 + [ANY] * 2,
         scratch_shapes=[
             low_buffer(peers, shard_rows, columns),
             pltpu.VMEM(resid.shape, high),
@@ -1769,11 +1862,12 @@
             pltpu.VMEM((4, *piece), high),
             pltpu.VMEM((peers, *piece), high),
             pltpu.VMEM((length, width), high),
-            dma((14,)), dma((14,)),
+            dma((16,)), dma((16,)),
             dma((peers - 1,)), dma((peers,)),
             dma((peers - 1,)), dma((peers,)),
             dma((3,)), dma((4,)),
             dma((peers - 1,)), dma((peers,)),
+            low_buffer(*wide_half), low_buffer(*wide_half), dma((4,)),
             *Scatter.buffers(n, length, width),
         ],
         compiler_params=communicating(6),
@@ -1782,25 +1876,34 @@
     )(
         attn_gain, ffn_gain, query_gain, key_gain, router, out_own, grad_projection.reshape(peers, shard_rows, columns),
         resid, first_gated.reshape(n, 2 * length, hidden), second_gated.reshape(n, 2 * length, hidden),
-        down_weight,
-    )
-
-
-def widen_kernel(
-    wide_0, down_0, wide_1, down_1, query_in, key_in, value_in, out_in, small_ref,
-    gate_ref, up_ref, down_ref, query_ref, key_ref, value_ref, out_ref,
-    attn_gain_ref, ffn_gain_ref, query_gain_ref, key_gain_ref, router_ref,
-):
-    for expert, (wide, down) in enumerate(((wide_0, down_0), (wide_1, down_1))):
+        down_weight, *second_wide,
+    )
+
+
+def widen_kernel(*refs):
+    sums, refs = refs[1:31], refs[31:]
+    sources, small_ref, refs = refs[:4], refs[4], refs[5:]
+    gate_ref, up_ref, down_ref, *targets = refs[:7]
+    attn_gain_ref, ffn_gain_ref, query_gain_ref, key_gain_ref, router_ref = refs[7:]
+    tile = down_ref.shape[3]
+    middle = gate_ref.shape[2] // 2
+    for expert in range(2):
 
         @pl.when(pl.program_id(0) == expert)
         def place():
-            piece = gate_ref.shape[1]
-            gate_ref[0] = wide[:piece].astype(high)
-            up_ref[0] = wide[piece:].astype(high)
-            down_ref[0] = down[...].astype(high)
-
-    for source, target in ((query_in, query_ref), (key_in, key_ref), (value_in, value_ref), (out_in, out_ref)):
+            for kind, target in enumerate((gate_ref, up_ref, down_ref)):
+                at = 15 * expert + 5 * kind
+                grads, first_a, first_b, second_a, second_b = sums[at : at + 5]
+                for side, first, second in ((0, first_a, second_a), (1, first_b, second_b)):
+                    columns = pl.ds(side * middle, middle)
+                    total = grads[0, :, columns].astype(high) + first[0].astype(high) + second[...].astype(high)
+                    if kind < 2:
+                        target[0, :, columns] = total
+                    else:
+                        for part in range(middle // tile):
+                            target[0, side * (middle // tile) + part] = total[:, part * tile : (part + 1) * tile]
+
+    for source, target in zip(sources, targets):
         target[...] = source[...].astype(high)
 
     @pl.when((pl.program_id(0) == 0) & (pl.program_id(1) == 0))
@@ -1812,49 +1915,64 @@
         router_ref[...] = small_ref[8:]
 
 
-def run_widen(grads, weight_grads, small, head_size, hidden_units, model_width, groups):
+def run_widen(sums, weight_grads, small, head_size, hidden_units, model_width, groups):
     piece, tile = hidden_units // groups, model_width // groups
     operands, specs = [], []
+    block, middle = piece // groups, model_width // 2
+    group = lax.axis_index("dp").astype(jnp.int32).reshape(1)
 
     def of_expert(expert):
         return lambda x, j: jnp.where(x == expert, j, 0 if expert else groups - 1)
 
-    for expert, rows in enumerate(grads):
+    for expert, (grads, (first_a, first_b), (second_a, second_b)) in enumerate(sums):
         turn = of_expert(expert)
-        operands += [rows, rows]
-        specs += [
-            pl.BlockSpec((2 * piece, tile), lambda x, j, turn=turn: (turn(x, j), 0)),
-            pl.BlockSpec((piece, tile), lambda x, j, turn=turn: (2 * groups + turn(x, j), 0)),
-        ]
+        for at in range(3):
+
+            def row(x, j, turn=turn, at=at):
+                return at * groups + turn(x, j)
+
+            operands += [grads, first_a, first_b, second_a, second_b]
+            specs += [
+                pl.BlockSpec((1, block, model_width), lambda x, j, g, row=row: (g[0], row(x, j), 0)),
+                pl.BlockSpec((1, block, middle), lambda x, j, g, row=row: (g[0] // 2, row(x, j), 0)),
+                pl.BlockSpec((1, block, middle), lambda x, j, g, row=row: (g[0] % 2, row(x, j), 0)),
+                pl.BlockSpec((block, middle), lambda x, j, g, row=row: (row(x, j), 0)),
+                pl.BlockSpec((block, middle), lambda x, j, g, row=row: (row(x, j), 0)),
+            ]
     steps = 2 * groups
     small_shapes = [
         (model_width,), (model_width,), (head_size,), (head_size,), (small.shape[0] - 8, model_width),
     ]
 
     def rows_of(array):
-        return pl.BlockSpec((array.shape[0] // steps, array.shape[1]), lambda x, j: (x * groups + j, 0))
+        return pl.BlockSpec((array.shape[0] // steps, array.shape[1]), lambda x, j, g: (x * groups + j, 0))
 
     return pl.pallas_call(
         widen_kernel,
-        grid=(2, groups),
         out_shape=[
             jax.ShapeDtypeStruct((2, piece, model_width), high),
             jax.ShapeDtypeStruct((2, piece, model_width), high),
-            jax.ShapeDtypeStruct((2, hidden_units, tile), high),
+            jax.ShapeDtypeStruct((2, groups, piece, tile), high),
             *[jax.ShapeDtypeStruct(array.shape, high) for array in weight_grads],
             *[jax.ShapeDtypeStruct(shape, high) for shape in small_shapes],
         ],
-        in_specs=specs + [rows_of(array) for array in weight_grads] + [pl.BlockSpec(small.shape, lambda x, j: (0, 0))],
-        out_specs=[
-            pl.BlockSpec((1, piece, tile), lambda x, j: (x, 0, j)),
-            pl.BlockSpec((1, piece, tile), lambda x, j: (x, 0, j)),
-            pl.BlockSpec((1, piece, tile), lambda x, j: (x, j, 0)),
-            *[rows_of(array) for array in weight_grads],
-            *[pl.BlockSpec(shape, lambda x, j, rank=len(shape): (0,) * rank) for shape in small_shapes],
-        ],
+        grid_spec=pltpu.PrefetchScalarGridSpec(
+            num_scalar_prefetch=1,
+            grid=(2, groups),
+            in_specs=specs
+            + [rows_of(array) for array in weight_grads]
+            + [pl.BlockSpec(small.shape, lambda x, j, g: (0, 0))],
+            out_specs=[
+                pl.BlockSpec((1, block, model_width), lambda x, j, g: (x, j, 0)),
+                pl.BlockSpec((1, block, model_width), lambda x, j, g: (x, j, 0)),
+                pl.BlockSpec((1, groups, block, tile), lambda x, j, g: (x, 0, j, 0)),
+                *[rows_of(array) for array in weight_grads],
+                *[pl.BlockSpec(shape, lambda x, j, g, rank=len(shape): (0,) * rank) for shape in small_shapes],
+            ],
+        ),
         compiler_params=pltpu.CompilerParams(vmem_limit_bytes=60 << 20),
         name="widen",
-    )(*operands, *weight_grads, small)
+    )(group, *operands, *weight_grads, small)
 
 
 def gather_tokens(rows):
@@ -1922,42 +2040,37 @@
     gain_attn_row = norm_gain_attn.reshape(1, model_width)
     gain_ffn_row = norm_gain_ffn.reshape(1, model_width)
 
-    named = jnp.any(routes[:, :, None] == jnp.arange(128, dtype=jnp.int32)[None, None, :], axis=1).astype(low)
-    hidden, all_named, near, projection, raw = run_gather(
-        tokens, gain_attn_row, named, cotangent, query_weight, key_matrix, value_matrix, peers, groups
+    hidden, all_named, near, seg_col, projection, raw = run_gather(
+        tokens, gain_attn_row, routes.T, segments, cotangent, query_weight, key_matrix, value_matrix, peers, groups
     )
     cosines, sines = constant_tables(full_length, head_size)
-    seg_col = jnp.broadcast_to(segments.reshape(full_length, 1), (full_length, head_size))
-    seg_row = jnp.broadcast_to(segments.reshape(1, full_length), (8, full_length))
+    seg_row = segments
     query_gain_row = query_gain.reshape(1, head_size)
     key_gain_row = key_gain.reshape(1, head_size)
     router = router_weight.T
     (
-        key_low, value_low, resid, ffn_local, gates, own_gates, mixed, query_low, inverse, rows_all, cotangents,
+        key_low, value_low, own_gates, resid, ffn_local, gates, mixed, query_low, inverse, rows_all, cotangents,
         first_gated, parts, first_grads,
     ) = run_first(
         raw, query_gain_row, key_gain_row, cosines, sines, seg_col, seg_row, out_weight, tokens, gain_ffn_row,
         all_named, router, cotangent, near, gate_weight, up_weight, down_weight, peers, groups,
     )
-    sums, second_gated, second_grads = run_second(
-        gates, rows_all, cotangents, gate_weight, up_weight, down_weight, parts, peers, groups
-    )
-    grads = [
-        lax.psum_scatter(each.reshape(-1, each.shape[2]), "dp", scatter_dimension=0, tiled=True)
-        for each in (first_grads, second_grads)
-    ]
-    input_grad, grad_projection, out_own, gain_attn_part, gain_ffn_part, query_gain_part, key_gain_part, grad_router = (
-        run_input(
-            sums, own_gates, ffn_local, resid, cotangent, gain_ffn_row, router, out_weight, raw, query_low, key_low,
-            value_low, inverse, mixed, query_gain_row, key_gain_row, cosines, sines, seg_col, seg_row, projection,
-            hidden, tokens, gain_attn_row, experts, peers,
-        )
-    )
-    grads[0], grad_projection = lax.optimization_barrier((grads[0], grad_projection))
-    *weight_grads, small, output = run_weights(
+    sums, second_gated, second_grads, *first_step = run_second(
+        gates, rows_all, cotangents, gate_weight, up_weight, down_weight, parts, first_grads, peers, groups
+    )
+    (
+        input_grad, grad_projection, out_own, gain_attn_part, gain_ffn_part, query_gain_part, key_gain_part,
+        grad_router, first_end, second_step,
+    ) = run_input(
+        sums, own_gates, ffn_local, resid, cotangent, gain_ffn_row, router, out_weight, raw, query_low, key_low,
+        value_low, inverse, mixed, query_gain_row, key_gain_row, cosines, sines, seg_col, seg_row, projection,
+        hidden, tokens, gain_attn_row, (first_grads, *first_step), second_grads, experts, peers,
+    )
+    *weight_grads, small, output, second_a, second_b = run_weights(
         grad_projection, out_own, gain_attn_part, gain_ffn_part, query_gain_part, key_gain_part, grad_router,
-        resid, first_gated, second_gated, down_weight, peers, kv_heads,
-    )
+        resid, first_gated, second_gated, down_weight, (second_grads, *second_step), peers, kv_heads,
+    )
+    grads = ((first_grads, first_step, first_end), (second_grads, second_step, (second_a, second_b)))
     gate_w, up_w, down_w, query_w, key_w, value_w, out_w, *sums = run_widen(
         grads, weight_grads, small, head_size, hidden_units, model_width, groups
     )
@@ -1976,7 +2089,7 @@
         router_grad.T,
         gate_w.transpose(0, 2, 1),
         up_w.transpose(0, 2, 1),
-        down_w,
+        down_w.reshape(local_experts, hidden_units, model_width // groups),
     )
 
 

time: 479 us -> 469 us (0.979); the launches traced: 478 us -> 463 us
  between operations: 14.2 us -> 1.16 us
    pallas_call x1, Pallas kernels: 108 us -> 97.5 us  [run_weights(): pl.pallas_call(weights_kernel, out_shape=[jax.ShapeDtypeStruct((shard_row...]
    pallas_call x1, Pallas kernels: 98.6 us -> 106 us  [run_input(): pl.pallas_call(input_kernel, out_shape=[jax.ShapeDtypeStruct((length, wid...]
  transfers between devices with their start and end apart: 2 -> 0, of which waited for: 0 -> 0; matrix products, arithmetic and copies ran while one was open for 0% -> 0% of each run, Pallas kernels for 55% -> 0%
where the time goes in v5:
time: 469 us; the launch traced here: 463 us
  Pallas kernels  460 us (98%)
    pallas_call x1, Pallas kernels, run_first(): pl.pallas_call(first_kernel, out_shape=[jax.ShapeDtypeStruct((full, head_...  109 us
    pallas_call x1, Pallas kernels, run_input(): pl.pallas_call(input_kernel, out_shape=[jax.ShapeDtypeStruct((length, wid...  106 us
    pallas_call x1, Pallas kernels, run_weights(): pl.pallas_call(weights_kernel, out_shape=[jax.ShapeDtypeStruct((shard_row...  97.5 us
    pallas_call x1, Pallas kernels, run_gather(): pl.pallas_call(gather_kernel, out_shape=[jax.ShapeDtypeStruct((length * p...  73.4 us
    pallas_call x1, Pallas kernels, run_second(): pl.pallas_call(second_kernel, out_shape=[jax.ShapeDtypeStruct((length, se...  57 us
    pallas_call x1, Pallas kernels, run_widen(): pl.pallas_call(widen_kernel, out_shape=[jax.ShapeDtypeStruct((2, piece, m...  16.4 us

profile of v5, /device:TPU:0, one launch (start us, length us, event | category | flops | bytes accessed | tf_op | source)
XLA Modules:
  0.0 463.1 jit_solution(12906444173648318524)
XLA Ops:
  0.6 73.4 %gather_hidden.1 = (bf16[1024,2048]{1,0:T(8,128)(2,1)}, bf16[8,128,128]{2,1,0:T(8,128)(2,1)}, bf16[3,128,2048]{2,1,0:T(8,128)(2,1)}, s32[1024,128]{1,0:T(8,128)}...) custom-call(bf16[128,2048]{1,0:T(8,128)(2,1)} %tokens_ref.5, f32[1,2048]{1,0:T(1,128)} %bitcast.35, ...), custom_call_target="tpu_custom_call" | custom-call | bytes 67108864 | tf_op jit(solution)/shard_map/gather_hidden/pallas_call | solution.py:824
  74.0 109.4 %attention_and_first_expert.1 = (bf16[1024,128]{1,0:T(8,128)(2,1)}, bf16[1024,128]{1,0:T(8,128)(2,1)}, f32[2,64,128]{2,1,0:T(8,128)}, f32[128,2048]{1,0:T(8,128)...) custom-call(f32[1,128]{1,0:T(1,128)} %bitcast.38, ...), custom_call_target="tpu_custom_call" | custom-call | bytes 125829120 | tf_op jit(solution)/shard_map/attention_and_first_expert/pallas_call | solution.py:1260
  183.5 57.0 %second_expert.1 = (f32[128,2176]{1,0:T(8,128)}, bf16[8,2,64,768]{3,2,1,0:T(8,128)(2,1)}, bf16[4,576,2048]{2,1,0:T(8,128)(2,1)}, bf16[2,576,1024]{2,1,0:T(8,128)(2,1)}, bf16[2,576,1024]{2,1,0:T(8,128)(2,1)}) custom-call(f32[8,2,64,128]{3,2,1,0:T(8,128)} %get-tuple-element.75.gates_ref, bf16[8,2,64,2048]{3,2,1,0:T(8,128)(2,1)} %get-tuple-element.76.rows_hbm, ...), custom_call_target="tpu_custom_call" | custom-call | bytes 125829120 | tf_op jit(solution)/shard_map/second_expert/pallas_call | solution.py:1319
  240.5 106.4 %attention_backward_and_input.1 = (f32[128,2048]{1,0:T(8,128)}, bf16[128,2048]{1,0:T(8,128)(2,1)}, f32[8,2048]{1,0:T(8,128)}, f32[8,2048]{1,0:T(8,128)}, f32[8,1...) custom-call(f32[128,2176]{1,0:T(8,128)} %get-tuple-element.80.sums_r, ...), custom_call_target="tpu_custom_call" | custom-call | bytes 67108864 | tf_op jit(solution)/shard_map/attention_backward_and_input/pallas_call | solution.py:1557
  346.9 97.5 %sum_weight_gradients.1 = (bf16[256,4096]{1,0:T(8,128)(2,1)}, bf16[256,512]{1,0:T(8,128)(2,1)}, bf16[256,512]{1,0:T(8,128)(2,1)}, bf16[512,2048]{1,0:T(8,128)(2,...) custom-call(f32[8,2048]{1,0:T(8,128)} %get-tuple-element.94.attn_gai, ...), custom_call_target="tpu_custom_call" | custom-call | bytes 67108864 | tf_op jit(solution)/shard_map/sum_weight_gradients/pallas_call | solution.py:1832
  444.5 0.0 copy-start.1
  444.5 0.0 copy-start
  444.5 16.4 %widen.1 = (f32[2,192,2048]{2,1,0:T(8,128)}, f32[2,192,2048]{2,1,0:T(8,128)}, f32[2,4,192,512]{3,2,1,0:T(8,128)}, f32[256,4096]{1,0:T(8,128)}, f32[256,512]{1,0:...) custom-call(s32[1]{0:T(128)} %bitcast.16.refs_0_, ...), custom_call_target="tpu_custom_call" | custom-call | tf_op jit(solution)/shard_map/widen/pallas_call | solution.py:1950
  460.9 0.0 copy-done.1
  460.9 0.8 copy.34
  461.7 0.0 copy-done
  461.7 1.0 copy.35
Async XLA Ops:
  444.5 16.4 %copy-start.1 = (bf16[128,2048]{1,0:T(8,128)(2,1)S(1)}, bf16[128,2048]{1,0:T(8,128)(2,1)}, u32[]{:S(2)}) copy-start(bf16[128,2048]{1,0:T(8,128)(2,1)} %get-tuple-element.142) | copy-start | bytes 1572868
  444.5 17.2 %copy-start = (f32[128,2048]{1,0:T(8,128)S(1)}, f32[128,2048]{1,0:T(8,128)}, u32[]{:S(2)}) copy-start(f32[128,2048]{1,0:T(8,128)} %get-tuple-element.143) | copy-start | bytes 3145732

commit v6 on v5

--- a/solution.py
+++ b/solution.py
@@ -1433,7 +1433,6 @@
         gather.begin()
     wait_all(wide_loads)
     wide_second = wide.second(wide_left, wide_right, second_a, second_b, ports)
-    SquareSum.start(wide_second)
     router_grad_ref[...] = dot_first(grad_logits, ffn_ref[...])[: router_grad_ref.shape[0]]
     ffn_gain_grad_ref[...] = jnp.broadcast_to(
         jnp.sum(gain_rows, axis=0, keepdims=True), ffn_gain_grad_ref.shape
@@ -1514,6 +1513,7 @@
                 out_grad[:, span] = dot_first(mixed_ref[...], Split.every(attn_ref, span)).astype(low)
 
             out_total.begin()
+            SquareSum.start(wide_second)
 
         span = pl.ds(pl.multiple_of(step * projection_tile, projection_tile), projection_tile)
         projection_grad[span] = dot_first(hidden_ref[:, span], columns[...]).astype(low)
@@ -1606,12 +1606,12 @@
     )
 def weights_kernel(
     attn_gain_ref, ffn_gain_ref, query_gain_ref, key_gain_ref, router_ref, out_own_ref, proj_hbm, resid_hbm,
-    gated_0, gated_1, down_hbm, wide_hbm, wide_a, wide_b,
-    query_grad_ref, key_grad_ref, value_grad_ref, out_grad_ref, small_out_ref, output_ref, wide_second_a, wide_second_b,
+    gated_0, gated_1, down_hbm, wide_hbm, wide_a, wide_b, done_hbm, done_a, done_b, done_second_a, done_second_b,
+    query_grad_ref, key_grad_ref, value_grad_ref, out_grad_ref, small_out_ref, output_ref, wide_second_a, wide_second_b, sum_0, sum_1,
     proj_ref, resid_ref, gated, down_w, mixture, load_sems, all_proj, first_a, first_b, second_a, second_b,
     send_a, send_b, quarter, small, got, part, small_sum, total_mixture,
     port_send, port_recv, swap_send, swap_recv, send_1, recv_1, send_2, recv_2, send_3, recv_3,
-    wide_left, wide_right, wide_sems, pair, flow, *scatter_sems,
+    wide_left, wide_right, wide_sems, last, last_sems, pair, flow, *scatter_sems,
 ):
     peers = lax.axis_size("expert")
     me = lax.axis_index("expert")
@@ -1666,12 +1666,30 @@
             src_ref=source, dst_ref=target, send_sem=send, recv_sem=recv, device_id=device, device_id_type=MESH
         )
 
+    def close(grads, first_a, first_b, second_a, second_b, total):
+        middle = width // 2
+        for side, first, second in ((0, first_a.at[y], second_a), (1, first_b.at[x], second_b)):
+            columns = pl.ds(side * middle, middle)
+            pieces = [
+                pltpu.make_async_copy(source, last.at[at], last_sems.at[at])
+                for at, source in enumerate((grads.at[group, :, columns], first, second))
+            ]
+            for copy in pieces:
+                copy.start()
+            wait_all(pieces)
+            last[0] = (last[0].astype(high) + last[1].astype(high) + last[2].astype(high)).astype(low)
+            store = pltpu.make_async_copy(last.at[0], total.at[:, columns], last_sems.at[3])
+            store.start()
+            store.wait()
+
     along_x = [2 * other + 1 - x for other in range(2)]
     along_y = [2 * (1 - y) + other for other in range(2)]
     proj_1a = [ports.copy(proj_part(0, along_x[k], proj_hbm), first_a.at[k], beside) for k in range(2)]
     proj_1b = [ports.copy(proj_part(1, along_y[k], proj_hbm), first_b.at[k], across) for k in range(2)]
     for copy in proj_1a + proj_1b:
         copy.start()
+    out_copy = SquareCopy(out_own_ref, out_grad_ref, ports)
+    out_copy.begin()
 
     small_1 = [
         remote(small_piece(small, peer), got.at[me], send_1.at[at], recv_1.at[me], {"expert": peer})
@@ -1711,8 +1729,7 @@
     wait_all(wide_loads)
     wide_sent = wide.second(wide_left, wide_right, wide_second_a, wide_second_b, ports)
     SquareSum.start(wide_sent)
-    out_copy = SquareCopy(out_own_ref, out_grad_ref, ports)
-    out_copy.begin()
+    close(done_hbm, done_a, done_b, done_second_a, done_second_b, sum_0)
     scatter.step(2) if chain.n > 2 else None
 
     for at, peer in enumerate(others):
@@ -1765,6 +1782,8 @@
     far = 3 - group
     scatter.step(1) if chain.n > 1 else None
     out_copy.hand_on()
+    SquareSum.arrive(wide_sent)
+    close(wide_hbm, wide_a, wide_b, wide_second_a, wide_second_b, sum_1)
 
     def proj_half(q, side):
         return all_proj.at[q, pl.ds(side * half, half)]
@@ -1796,7 +1815,6 @@
     scatter.total(total_mixture)
     output_ref[...] = (resid_ref[...] + total_mixture[...]).astype(low)
     out_copy.finish()
-    SquareSum.arrive(wide_sent)
     proj_fa.wait_recv()
     proj_fb.wait_recv()
     spread(far)
@@ -1808,7 +1826,7 @@
 
 def run_weights(
     grad_projection, out_own, attn_gain, ffn_gain, query_gain, key_gain, router, resid, first_gated, second_gated,
-    down_weight, second_wide, peers, kv_heads,
+    down_weight, second_wide, first_wide, peers, kv_heads,
 ):
     width, columns = grad_projection.shape
     head_size = query_gain.shape[1]
@@ -1839,9 +1857,10 @@
             jax.ShapeDtypeStruct((small_rows, width), high),
             jax.ShapeDtypeStruct((length, width), low),
             *wide_second,
+            *[jax.ShapeDtypeStruct(second_wide[0].shape[1:], low)] * 2,
         ],
-        in_specs=[VMEM] * 6 + [ANY] * 8,
-        out_specs=[VMEM] * 6 + [ANY] * 2,
+        in_specs=[VMEM] * 6 + [ANY] * 13,
+        out_specs=[VMEM] * 6 + [ANY] * 4,
         scratch_shapes=[
             low_buffer(peers, shard_rows, columns),
             pltpu.VMEM(resid.shape, high),
@@ -1868,6 +1887,7 @@
             dma((3,)), dma((4,)),
             dma((peers - 1,)), dma((peers,)),
             low_buffer(*wide_half), low_buffer(*wide_half), dma((4,)),
+            low_buffer(3, *wide_second[0].shape), dma((4,)),
             *Scatter.buffers(n, length, width),
         ],
         compiler_params=communicating(6),
@@ -1876,34 +1896,26 @@
     )(
         attn_gain, ffn_gain, query_gain, key_gain, router, out_own, grad_projection.reshape(peers, shard_rows, columns),
         resid, first_gated.reshape(n, 2 * length, hidden), second_gated.reshape(n, 2 * length, hidden),
-        down_weight, *second_wide,
-    )
-
-
-def widen_kernel(*refs):
-    sums, refs = refs[1:31], refs[31:]
-    sources, small_ref, refs = refs[:4], refs[4], refs[5:]
-    gate_ref, up_ref, down_ref, *targets = refs[:7]
-    attn_gain_ref, ffn_gain_ref, query_gain_ref, key_gain_ref, router_ref = refs[7:]
-    tile = down_ref.shape[3]
-    middle = gate_ref.shape[2] // 2
-    for expert in range(2):
+        down_weight, *second_wide, *first_wide,
+    )
+
+
+def widen_kernel(
+    gate_0, up_0, down_0, gate_1, up_1, down_1, query_in, key_in, value_in, out_in, small_ref,
+    gate_ref, up_ref, down_ref, query_ref, key_ref, value_ref, out_ref,
+    attn_gain_ref, ffn_gain_ref, query_gain_ref, key_gain_ref, router_ref,
+):
+    for expert, (gate, up, down) in enumerate(((gate_0, up_0, down_0), (gate_1, up_1, down_1))):
 
         @pl.when(pl.program_id(0) == expert)
         def place():
-            for kind, target in enumerate((gate_ref, up_ref, down_ref)):
-                at = 15 * expert + 5 * kind
-                grads, first_a, first_b, second_a, second_b = sums[at : at + 5]
-                for side, first, second in ((0, first_a, second_a), (1, first_b, second_b)):
-                    columns = pl.ds(side * middle, middle)
-                    total = grads[0, :, columns].astype(high) + first[0].astype(high) + second[...].astype(high)
-                    if kind < 2:
-                        target[0, :, columns] = total
-                    else:
-                        for part in range(middle // tile):
-                            target[0, side * (middle // tile) + part] = total[:, part * tile : (part + 1) * tile]
-
-    for source, target in zip(sources, targets):
+            gate_ref[0] = gate[...].astype(high)
+            up_ref[0] = up[...].astype(high)
+            tile = down_ref.shape[3]
+            for part in range(down_ref.shape[1]):
+                down_ref[0, part] = down[:, part * tile : (part + 1) * tile].astype(high)
+
+    for source, target in ((query_in, query_ref), (key_in, key_ref), (value_in, value_ref), (out_in, out_ref)):
         target[...] = source[...].astype(high)
 
     @pl.when((pl.program_id(0) == 0) & (pl.program_id(1) == 0))
@@ -1915,40 +1927,32 @@
         router_ref[...] = small_ref[8:]
 
 
-def run_widen(sums, weight_grads, small, head_size, hidden_units, model_width, groups):
+def run_widen(grads, weight_grads, small, head_size, hidden_units, model_width, groups):
     piece, tile = hidden_units // groups, model_width // groups
     operands, specs = [], []
-    block, middle = piece // groups, model_width // 2
-    group = lax.axis_index("dp").astype(jnp.int32).reshape(1)
+    block = piece // groups
 
     def of_expert(expert):
         return lambda x, j: jnp.where(x == expert, j, 0 if expert else groups - 1)
 
-    for expert, (grads, (first_a, first_b), (second_a, second_b)) in enumerate(sums):
+    for expert, rows in enumerate(grads):
         turn = of_expert(expert)
-        for at in range(3):
-
-            def row(x, j, turn=turn, at=at):
-                return at * groups + turn(x, j)
-
-            operands += [grads, first_a, first_b, second_a, second_b]
-            specs += [
-                pl.BlockSpec((1, block, model_width), lambda x, j, g, row=row: (g[0], row(x, j), 0)),
-                pl.BlockSpec((1, block, middle), lambda x, j, g, row=row: (g[0] // 2, row(x, j), 0)),
-                pl.BlockSpec((1, block, middle), lambda x, j, g, row=row: (g[0] % 2, row(x, j), 0)),
-                pl.BlockSpec((block, middle), lambda x, j, g, row=row: (row(x, j), 0)),
-                pl.BlockSpec((block, middle), lambda x, j, g, row=row: (row(x, j), 0)),
-            ]
+        operands += [rows] * 3
+        specs += [
+            pl.BlockSpec((block, model_width), lambda x, j, turn=turn, at=at: (at * groups + turn(x, j), 0))
+            for at in range(3)
+        ]
     steps = 2 * groups
     small_shapes = [
         (model_width,), (model_width,), (head_size,), (head_size,), (small.shape[0] - 8, model_width),
     ]
 
     def rows_of(array):
-        return pl.BlockSpec((array.shape[0] // steps, array.shape[1]), lambda x, j, g: (x * groups + j, 0))
+        return pl.BlockSpec((array.shape[0] // steps, array.shape[1]), lambda x, j: (x * groups + j, 0))
 
     return pl.pallas_call(
         widen_kernel,
+        grid=(2, groups),
         out_shape=[
             jax.ShapeDtypeStruct((2, piece, model_width), high),
             jax.ShapeDtypeStruct((2, piece, model_width), high),
@@ -1956,23 +1960,17 @@
             *[jax.ShapeDtypeStruct(array.shape, high) for array in weight_grads],
             *[jax.ShapeDtypeStruct(shape, high) for shape in small_shapes],
         ],
-        grid_spec=pltpu.PrefetchScalarGridSpec(
-            num_scalar_prefetch=1,
-            grid=(2, groups),
-            in_specs=specs
-            + [rows_of(array) for array in weight_grads]
-            + [pl.BlockSpec(small.shape, lambda x, j, g: (0, 0))],
-            out_specs=[
-                pl.BlockSpec((1, block, model_width), lambda x, j, g: (x, j, 0)),
-                pl.BlockSpec((1, block, model_width), lambda x, j, g: (x, j, 0)),
-                pl.BlockSpec((1, groups, block, tile), lambda x, j, g: (x, 0, j, 0)),
-                *[rows_of(array) for array in weight_grads],
-                *[pl.BlockSpec(shape, lambda x, j, g, rank=len(shape): (0,) * rank) for shape in small_shapes],
-            ],
-        ),
+        in_specs=specs + [rows_of(array) for array in weight_grads] + [pl.BlockSpec(small.shape, lambda x, j: (0, 0))],
+        out_specs=[
+            pl.BlockSpec((1, block, model_width), lambda x, j: (x, j, 0)),
+            pl.BlockSpec((1, block, model_width), lambda x, j: (x, j, 0)),
+            pl.BlockSpec((1, groups, block, tile), lambda x, j: (x, 0, j, 0)),
+            *[rows_of(array) for array in weight_grads],
+            *[pl.BlockSpec(shape, lambda x, j, rank=len(shape): (0,) * rank) for shape in small_shapes],
+        ],
         compiler_params=pltpu.CompilerParams(vmem_limit_bytes=60 << 20),
         name="widen",
-    )(group, *operands, *weight_grads, small)
+    )(*operands, *weight_grads, small)
 
 
 def gather_tokens(rows):
@@ -2066,11 +2064,12 @@
         value_low, inverse, mixed, query_gain_row, key_gain_row, cosines, sines, seg_col, seg_row, projection,
         hidden, tokens, gain_attn_row, (first_grads, *first_step), second_grads, experts, peers,
     )
-    *weight_grads, small, output, second_a, second_b = run_weights(
+    *weight_grads, small, output, _, _, first_sum, second_sum = run_weights(
         grad_projection, out_own, gain_attn_part, gain_ffn_part, query_gain_part, key_gain_part, grad_router,
-        resid, first_gated, second_gated, down_weight, (second_grads, *second_step), peers, kv_heads,
-    )
-    grads = ((first_grads, first_step, first_end), (second_grads, second_step, (second_a, second_b)))
+        resid, first_gated, second_gated, down_weight, (second_grads, *second_step),
+        (first_grads, *first_step, *first_end), peers, kv_heads,
+    )
+    grads = (first_sum, second_sum)
     gate_w, up_w, down_w, query_w, key_w, value_w, out_w, *sums = run_widen(
         grads, weight_grads, small, head_size, hidden_units, model_width, groups
     )

time: 469 us -> 463 us (0.987)
  Pallas kernels: 460 us -> 454 us
where the time goes in v6:
time: 463 us; the launch traced here: 457 us
  Pallas kernels  454 us (98%)
    pallas_call x1, Pallas kernels, run_first(): pl.pallas_call(first_kernel, out_shape=[jax.ShapeDtypeStruct((full, head_...  109 us
    pallas_call x1, Pallas kernels, run_input(): pl.pallas_call(input_kernel, out_shape=[jax.ShapeDtypeStruct((length, wid...  105 us
    pallas_call x1, Pallas kernels, run_weights(): pl.pallas_call(weights_kernel, out_shape=[jax.ShapeDtypeStruct((shard_row...  97.2 us
    pallas_call x1, Pallas kernels, run_gather(): pl.pallas_call(gather_kernel, out_shape=[jax.ShapeDtypeStruct((length * p...  73.4 us
    pallas_call x1, Pallas kernels, run_second(): pl.pallas_call(second_kernel, out_shape=[jax.ShapeDtypeStruct((length, se...  57 us
    pallas_call x1, Pallas kernels, run_widen(): pl.pallas_call(widen_kernel, grid=(2, groups), out_shape=[jax.ShapeDtypeS...  12.7 us

profile of v6, /device:TPU:0, one launch (start us, length us, event | category | flops | bytes accessed | tf_op | source)
XLA Modules:
  0.0 457.1 jit_solution(13371686931441766185)
XLA Ops:
  0.6 73.4 %gather_hidden.1 = (bf16[1024,2048]{1,0:T(8,128)(2,1)}, bf16[8,128,128]{2,1,0:T(8,128)(2,1)}, bf16[3,128,2048]{2,1,0:T(8,128)(2,1)}, s32[1024,128]{1,0:T(8,128)}...) custom-call(bf16[128,2048]{1,0:T(8,128)(2,1)} %tokens_ref.5, f32[1,2048]{1,0:T(1,128)} %bitcast.34, ...), custom_call_target="tpu_custom_call" | custom-call | bytes 67108864 | tf_op jit(solution)/shard_map/gather_hidden/pallas_call | solution.py:824
  74.0 109.3 %attention_and_first_expert.1 = (bf16[1024,128]{1,0:T(8,128)(2,1)}, bf16[1024,128]{1,0:T(8,128)(2,1)}, f32[2,64,128]{2,1,0:T(8,128)}, f32[128,2048]{1,0:T(8,128)...) custom-call(f32[1,128]{1,0:T(1,128)} %bitcast.37, ...), custom_call_target="tpu_custom_call" | custom-call | bytes 125829120 | tf_op jit(solution)/shard_map/attention_and_first_expert/pallas_call | solution.py:1260
  183.3 57.0 %second_expert.1 = (f32[128,2176]{1,0:T(8,128)}, bf16[8,2,64,768]{3,2,1,0:T(8,128)(2,1)}, bf16[4,576,2048]{2,1,0:T(8,128)(2,1)}, bf16[2,576,1024]{2,1,0:T(8,128)(2,1)}, bf16[2,576,1024]{2,1,0:T(8,128)(2,1)}) custom-call(f32[8,2,64,128]{3,2,1,0:T(8,128)} %get-tuple-element.75.gates_ref, bf16[8,2,64,2048]{3,2,1,0:T(8,128)(2,1)} %get-tuple-element.76.rows_hbm, ...), custom_call_target="tpu_custom_call" | custom-call | bytes 125829120 | tf_op jit(solution)/shard_map/second_expert/pallas_call | solution.py:1319
  240.4 104.5 %attention_backward_and_input.1 = (f32[128,2048]{1,0:T(8,128)}, bf16[128,2048]{1,0:T(8,128)(2,1)}, f32[8,2048]{1,0:T(8,128)}, f32[8,2048]{1,0:T(8,128)}, f32[8,1...) custom-call(f32[128,2176]{1,0:T(8,128)} %get-tuple-element.80.sums_r, ...), custom_call_target="tpu_custom_call" | custom-call | bytes 67108864 | tf_op jit(solution)/shard_map/attention_backward_and_input/pallas_call | solution.py:1557
  344.9 97.2 %sum_weight_gradients.1 = (bf16[256,4096]{1,0:T(8,128)(2,1)}, bf16[256,512]{1,0:T(8,128)(2,1)}, bf16[256,512]{1,0:T(8,128)(2,1)}, bf16[512,2048]{1,0:T(8,128)(2,...) custom-call(f32[8,2048]{1,0:T(8,128)} %get-tuple-element.94.attn_gai, ...), custom_call_target="tpu_custom_call" | custom-call | bytes 67108864 | tf_op jit(solution)/shard_map/sum_weight_gradients/pallas_call | solution.py:1850
  442.1 0.0 copy-start.1
  442.1 0.0 copy-start
  442.1 12.7 %widen.1 = (f32[2,192,2048]{2,1,0:T(8,128)}, f32[2,192,2048]{2,1,0:T(8,128)}, f32[2,4,192,512]{3,2,1,0:T(8,128)}, f32[256,4096]{1,0:T(8,128)}, f32[256,512]{1,0:...) custom-call(bf16[576,2048]{1,0:T(8,128)(2,1)} %get-tuple-element.109, ...), custom_call_target="tpu_custom_call" | custom-call | tf_op jit(solution)/shard_map/widen/pallas_call | solution.py:1953
  454.9 0.0 copy-done.1
  454.9 0.8 copy.34
  455.7 0.0 copy-done
  455.7 1.0 copy.35
Async XLA Ops:
  442.1 12.8 %copy-start.1 = (bf16[128,2048]{1,0:T(8,128)(2,1)S(1)}, bf16[128,2048]{1,0:T(8,128)(2,1)}, u32[]{:S(2)}) copy-start(bf16[128,2048]{1,0:T(8,128)(2,1)} %get-tuple-element.142) | copy-start | bytes 1572868
  442.1 13.6 %copy-start = (f32[128,2048]{1,0:T(8,128)S(1)}, f32[128,2048]{1,0:T(8,128)}, u32[]{:S(2)}) copy-start(f32[128,2048]{1,0:T(8,128)} %get-tuple-element.143) | copy-start | bytes 3145732

commit v7 on v6

--- a/solution.py
+++ b/solution.py
@@ -831,8 +831,8 @@
             jax.ShapeDtypeStruct((peers, groups, rows, columns), low),
             jax.ShapeDtypeStruct((length * peers, columns), high),
         ],
-        in_specs=[VMEM] * 5 + [ANY] * 3,
-        out_specs=[ANY, VMEM, VMEM, VMEM, ANY, ANY],
+        in_specs=[VMEM] * 4 + [ANY] * 4,
+        out_specs=[ANY, VMEM, ANY, VMEM, ANY, ANY],
         scratch_shapes=[
             pltpu.VMEM((length, 128), low),
             pltpu.VMEM((length, width), low),
@@ -1275,7 +1275,7 @@
             split(sent, low),
             jax.ShapeDtypeStruct((groups, 3 * hidden // groups, width), low),
         ],
-        in_specs=[VMEM] * 9 + [ANY] * 8,
+        in_specs=[VMEM] * 7 + [ANY] * 10,
         out_specs=[VMEM] * 3 + [ANY] * 11,
         scratch_shapes=[
             pltpu.VMEM((length, width), high),
@@ -1634,12 +1634,6 @@
         load.start()
     width = resid_ref.shape[1]
     head_size = query_gain_ref.shape[1]
-    small[...] = jnp.zeros_like(small)
-    small[0:1] = attn_gain_ref[0:1]
-    small[1:2] = ffn_gain_ref[0:1]
-    small[2:3, :head_size] = query_gain_ref[0:1]
-    small[3:4, :head_size] = key_gain_ref[0:1]
-    small[8:] = router_ref[...]
     piece = width // peers
 
     def small_piece(ref, peer):
@@ -1691,6 +1685,12 @@
     out_copy = SquareCopy(out_own_ref, out_grad_ref, ports)
     out_copy.begin()
 
+    small[...] = jnp.zeros_like(small)
+    small[0:1] = attn_gain_ref[0:1]
+    small[1:2] = ffn_gain_ref[0:1]
+    small[2:3, :head_size] = query_gain_ref[0:1]
+    small[3:4, :head_size] = key_gain_ref[0:1]
+    small[8:] = router_ref[...]
     small_1 = [
         remote(small_piece(small, peer), got.at[me], send_1.at[at], recv_1.at[me], {"expert": peer})
         for at, peer in enumerate(others)

time: 463 us -> 462 us (level)
  no operation moved by 1% of the time
where the time goes in v7:
time: 462 us; the launch traced here: 455 us
  Pallas kernels  452 us (98%)
    pallas_call x1, Pallas kernels, run_first(): pl.pallas_call(first_kernel, out_shape=[jax.ShapeDtypeStruct((full, head_...  108 us
    pallas_call x1, Pallas kernels, run_input(): pl.pallas_call(input_kernel, out_shape=[jax.ShapeDtypeStruct((length, wid...  105 us
    pallas_call x1, Pallas kernels, run_weights(): pl.pallas_call(weights_kernel, out_shape=[jax.ShapeDtypeStruct((shard_row...  96.6 us
    pallas_call x1, Pallas kernels, run_gather(): pl.pallas_call(gather_kernel, out_shape=[jax.ShapeDtypeStruct((length * p...  72.8 us
    pallas_call x1, Pallas kernels, run_second(): pl.pallas_call(second_kernel, out_shape=[jax.ShapeDtypeStruct((length, se...  57 us
    pallas_call x1, Pallas kernels, run_widen(): pl.pallas_call(widen_kernel, grid=(2, groups), out_shape=[jax.ShapeDtypeS...  12.7 us

profile of v7, /device:TPU:0, one launch (start us, length us, event | category | flops | bytes accessed | tf_op | source)
XLA Modules:
  0.0 455.2 jit_solution(14858827636195712922)
XLA Ops:
  0.6 72.8 %gather_hidden.1 = (bf16[1024,2048]{1,0:T(8,128)(2,1)}, bf16[8,128,128]{2,1,0:T(8,128)(2,1)}, bf16[3,128,2048]{2,1,0:T(8,128)(2,1)}, s32[1024,128]{1,0:T(8,128)}...) custom-call(bf16[128,2048]{1,0:T(8,128)(2,1)} %tokens_ref.5, f32[1,2048]{1,0:T(1,128)} %bitcast.34, ...), custom_call_target="tpu_custom_call" | custom-call | bytes 67108864 | tf_op jit(solution)/shard_map/gather_hidden/pallas_call | solution.py:824
  73.5 108.0 %attention_and_first_expert.1 = (bf16[1024,128]{1,0:T(8,128)(2,1)}, bf16[1024,128]{1,0:T(8,128)(2,1)}, f32[2,64,128]{2,1,0:T(8,128)}, f32[128,2048]{1,0:T(8,128)...) custom-call(f32[1,128]{1,0:T(1,128)} %bitcast.37, ...), custom_call_target="tpu_custom_call" | custom-call | bytes 125829120 | tf_op jit(solution)/shard_map/attention_and_first_expert/pallas_call | solution.py:1260
  181.5 57.0 %second_expert.1 = (f32[128,2176]{1,0:T(8,128)}, bf16[8,2,64,768]{3,2,1,0:T(8,128)(2,1)}, bf16[4,576,2048]{2,1,0:T(8,128)(2,1)}, bf16[2,576,1024]{2,1,0:T(8,128)(2,1)}, bf16[2,576,1024]{2,1,0:T(8,128)(2,1)}) custom-call(f32[8,2,64,128]{3,2,1,0:T(8,128)} %get-tuple-element.75.gates_ref, bf16[8,2,64,2048]{3,2,1,0:T(8,128)(2,1)} %get-tuple-element.76.rows_hbm, ...), custom_call_target="tpu_custom_call" | custom-call | bytes 125829120 | tf_op jit(solution)/shard_map/second_expert/pallas_call | solution.py:1319
  238.6 105.0 %attention_backward_and_input.1 = (f32[128,2048]{1,0:T(8,128)}, bf16[128,2048]{1,0:T(8,128)(2,1)}, f32[8,2048]{1,0:T(8,128)}, f32[8,2048]{1,0:T(8,128)}, f32[8,1...) custom-call(f32[128,2176]{1,0:T(8,128)} %get-tuple-element.80.sums_r, ...), custom_call_target="tpu_custom_call" | custom-call | bytes 67108864 | tf_op jit(solution)/shard_map/attention_backward_and_input/pallas_call | solution.py:1557
  343.6 96.6 %sum_weight_gradients.1 = (bf16[256,4096]{1,0:T(8,128)(2,1)}, bf16[256,512]{1,0:T(8,128)(2,1)}, bf16[256,512]{1,0:T(8,128)(2,1)}, bf16[512,2048]{1,0:T(8,128)(2,...) custom-call(f32[8,2048]{1,0:T(8,128)} %get-tuple-element.94.attn_gai, ...), custom_call_target="tpu_custom_call" | custom-call | bytes 67108864 | tf_op jit(solution)/shard_map/sum_weight_gradients/pallas_call | solution.py:1850
  440.2 0.0 copy-start.1
  440.2 0.0 copy-start
  440.2 12.7 %widen.1 = (f32[2,192,2048]{2,1,0:T(8,128)}, f32[2,192,2048]{2,1,0:T(8,128)}, f32[2,4,192,512]{3,2,1,0:T(8,128)}, f32[256,4096]{1,0:T(8,128)}, f32[256,512]{1,0:...) custom-call(bf16[576,2048]{1,0:T(8,128)(2,1)} %get-tuple-element.109, ...), custom_call_target="tpu_custom_call" | custom-call | tf_op jit(solution)/shard_map/widen/pallas_call | solution.py:1953
  453.0 0.0 copy-done.1
  453.0 0.8 copy.34
  453.8 0.0 copy-done
  453.8 1.0 copy.35
Async XLA Ops:
  440.2 12.8 %copy-start.1 = (bf16[128,2048]{1,0:T(8,128)(2,1)S(1)}, bf16[128,2048]{1,0:T(8,128)(2,1)}, u32[]{:S(2)}) copy-start(bf16[128,2048]{1,0:T(8,128)(2,1)} %get-tuple-element.142) | copy-start | bytes 1572868
  440.2 13.6 %copy-start = (f32[128,2048]{1,0:T(8,128)S(1)}, f32[128,2048]{1,0:T(8,128)}, u32[]{:S(2)}) copy-start(f32[128,2048]{1,0:T(8,128)} %get-tuple-element.143) | copy-start | bytes 3145732
